TPU v7x, 32 devices: a whole 2x2x4 slice. The times are simulated.
32 devices in a mesh: subset: 4 (over y, x), tile: 8 (over z, core).
Axes of the slice: x: 2, y: 2, z: 4, core: 2. Of those that a mesh axis runs over, the one named last changes fastest.
Arguments:
- start_volume: bfloat16 [4, 64, 32768], P(None, None, 'tile'), may hold values from 0 to 2
- measured: bfloat16 [4, 4, 64, 2048], P('subset'), may hold values from 3264 to 13056
- system_values: bfloat16 [4, 2048, 32768], P('subset', None, 'tile'), may hold values from 0.05 to 2088.96, as said below
- block_pattern: int32 [4, 16, 256], P('subset', None, 'tile'), may hold values from 0 to 1, as said below
- subset_order: int32 [64, 4], replicated, may hold values from 0 to 3, each once within a row
Outputs:
- volume_out: bfloat16 [4, 64, 32768], P(None, None, 'tile')
Inputs may be any that keep to these rules, and one draw needn't show every extreme that they name: `block_pattern`: each entry is 0 or 1; every block row and every block column of each subset's matrix within every 4096-voxel tile holds at least one 1. `system_values`: positive entries. `subset_order`: each row is a permutation of the 4 subsets.
All inputs are finite; a program needn't handle non-finite values.
Results may differ from a plain program's by a relative error of at most 0.0034.
Values may be sent and summed in bfloat16 or wider, within the bound.
No kernel may reach another device: no remote copies, remote signals or barrier semaphores. Data moves between devices by JAX's collectives and lax.ppermute only.
A program may use at most 128 MiB of HBM per device.

v0:
```python
import functools

import jax
import jax.numpy as jnp
from jax import lax
from jax.experimental import pallas as pl
from jax.experimental.pallas import tpu as pltpu
from jax.sharding import PartitionSpec as P

F32, BF16, F16 = jnp.float32, jnp.bfloat16, jnp.float16
RAY_SCALE = 2.0**-14
EXTRA = 16
COST = 16
AHEAD = 2
BATCHES = 2
VM = pl.BlockSpec(memory_space=pltpu.VMEM)
SM = pl.BlockSpec(memory_space=pltpu.SMEM)
HB = pl.BlockSpec(memory_space=pltpu.HBM)


def call(kernel, out_shape, args, specs, flops, name, scratch=(), vmem=8 << 20):
    out_specs = jax.tree.map(lambda _: VM, out_shape)
    return pl.pallas_call(
        kernel,
        out_shape=out_shape,
        in_specs=specs,
        out_specs=out_specs,
        scratch_shapes=scratch,
        name=name,
        cost_estimate=pl.CostEstimate(
            flops=COST * flops, bytes_accessed=0, transcendentals=0
        ),
        compiler_params=pltpu.CompilerParams(vmem_limit_bytes=vmem),
    )(*args)


def shaped(shape, dtype=F32):
    return jax.ShapeDtypeStruct(shape, dtype)


def dot_nn(a, b):
    return lax.dot_general(a, b, (((1,), (0,)), ((), ())), preferred_element_type=F32)


def load_kernel(
    place, matrix_hbm, pattern, order, start_hbm, matrix, flipped, narrow, volume, turn, apart,
    second, fronts, sems, start_sem,
):
    ray_blocks, col_blocks = pattern.shape
    ray_count, voxels = matrix.shape
    side = ray_count // ray_blocks
    loads = sems.shape[0]
    rows = ray_count // loads
    per_load = ray_blocks // loads
    slices = fronts.shape[1]
    owner, core, owners = place[0], place[1], place[2]

    def piece(i):
        where = pl.ds(pl.multiple_of(i * rows, rows), rows)
        return pltpu.make_async_copy(matrix_hbm.at[where], matrix.at[where], sems.at[i])

    first = pltpu.make_async_copy(start_hbm, fronts, start_sem)
    first.start()
    for i in range(AHEAD):
        piece(i).start()
    second[...] = jnp.full(second.shape, core.astype(F32))
    later = owner - order[...]
    later = jnp.where(later < 0, later + owners, later)
    turn[...] = later
    last = order[...] + (owners - 1)
    last = jnp.where(last >= owners, last - owners, last)
    apart[...] = last ^ owner
    batches, rows_in = narrow.shape[:2]
    batch = slices // batches
    narrow[:, batch:, :] = jnp.ones((batches, rows_in - batch, voxels), BF16)
    first.wait()
    chosen = [later[:, f : f + 1] == 0 for f in range(1, fronts.shape[0])]
    step = 4 * side

    @pl.loop(0, voxels // step)
    def _(i):
        cols = pl.ds(pl.multiple_of(i * step, step), step)
        got = fronts[0, :, cols].astype(F32)
        for f, here in enumerate(chosen):
            got = jnp.where(here, fronts[f + 1, :, cols].astype(F32), got)
        for b in range(batches):
            part = got[b * batch : (b + 1) * batch]
            volume[b, :, cols] = part
            narrow[b, :batch, cols] = part.astype(BF16)

    @pl.loop(0, loads)
    def _(i):
        piece(i).wait()

        @pl.when(i + AHEAD < loads)
        def _():
            piece(i + AHEAD).start()

        where = pl.ds(pl.multiple_of(i * rows, rows), rows)
        for c in range(0, col_blocks, 2):
            cols = slice(c * side, (c + 2) * side)
            blocks = matrix[where, cols]
            masked = []
            for r in range(per_load):
                keep = [pattern[i * per_load + r, c + k].astype(F32).astype(BF16) for k in (0, 1)]
                part = blocks[r * side : (r + 1) * side]
                masked.append(
                    jnp.concatenate([part[:, :side] * keep[0], part[:, side:] * keep[1]], 1)
                )
            blocks = jnp.concatenate(masked, 0)
            matrix[where, cols] = blocks
            flipped[cols, where] = blocks.T


def project(place, volume, flipped, rays):
    count = rays.shape[1]
    step = min(count, 1024)
    offset = place[0] * count

    @pl.loop(0, count // step)
    def _(i):
        where = pl.ds(pl.multiple_of(offset + i * step, step), step)
        rays[:, pl.ds(pl.multiple_of(i * step, step), step)] = dot_nn(volume[...], flipped[:, where])


def spread_first(place, residue, matrix, spread):
    count = residue.shape[1]
    where = pl.ds(pl.multiple_of(place[0] * count, count), count)
    step = 2048

    @pl.loop(0, matrix.shape[1] // step)
    def _(c):
        cols = pl.ds(pl.multiple_of(c * step, step), step)
        spread[:, cols] = dot_nn(residue[...], matrix[where, cols])


def spread_last(first, place, residue, so_far, volume, column, matrix, out, *column_out):
    count = residue.shape[1]
    slices = out.shape[0]
    step = 2048
    where = pl.ds(pl.multiple_of(place[0] * count, count), count)

    @pl.loop(0, matrix.shape[1] // step)
    def _(c):
        cols = pl.ds(pl.multiple_of(c * step, step), step)
        total = so_far[:, cols] + dot_nn(residue[...], matrix[where, cols])
        if first:
            inverse = 1.0 / total[slices : slices + 1, :]
            column_out[0][:, cols] = inverse
        else:
            inverse = column[:, cols]
        out[:, cols] = volume[:, cols] + total[:slices] * inverse


def passed(x, axis, distance):
    size = lax.axis_size(axis)
    return lax.ppermute(x, axis, [(i, (i + distance) % size) for i in range(size)])


def swapped(x, axis, bit):
    size = lax.axis_size(axis)
    return lax.ppermute(x, axis, [(i, i ^ bit) for i in range(size)])


def after(value, token):
    return value if token is None else lax.optimization_barrier((value, token))[0]


def from_all_owners(block):
    owners = lax.axis_size("subset")
    if owners != 4:
        return [block] + [swapped(block, "subset", d) for d in range(1, owners)]
    half = block.shape[1] // 2
    near = swapped(block, "subset", 1)
    far = swapped(block, "subset", 2)
    both = [swapped(far[:, :half], "subset", 1), swapped(near[:, half:], "subset", 2)]
    return [block, near, far, jnp.concatenate(both, axis=1)]


def body(start_volume, measured, system_values, block_pattern, subset_order):
    owner = lax.axis_index("subset")
    owners = lax.axis_size("subset")
    core = lax.axis_index("tile") % 2
    tiles = lax.axis_size("tile")
    fronts, slices, voxels = start_volume.shape
    ray_count = measured.shape[-1]
    ray_blocks = block_pattern.shape[1]
    half = ray_count // 2
    batch = slices // BATCHES
    rows = batch + EXTRA
    passes = owners
    loads = ray_blocks // 2
    work = 2 * slices * ray_count * voxels
    place = jnp.stack([owner, core, jnp.int32(owners)]).astype(jnp.int32)
    own = jnp.reshape(core, (1,)).astype(jnp.int32)
    other = jnp.reshape(1 - core, (1,)).astype(jnp.int32)
    place, own, other = lax.optimization_barrier((place, own, other))

    def pick(turns, j, parts):
        got = parts[0]
        for f in range(1, fronts):
            got = jnp.where(turns[:, f : f + 1] == j, parts[f], got)
        return got

    hbm = pltpu.with_memory_space_constraint
    matrix, flipped, all_rows, volume, turn, apart, second = call(
        load_kernel,
        (
            pltpu.VMEM((ray_count, voxels), BF16),
            pltpu.VMEM((voxels, ray_count), BF16),
            shaped((BATCHES, rows, voxels), BF16),
            shaped((BATCHES, batch, voxels)),
            shaped((slices, fronts), jnp.int32),
            shaped((slices, fronts), jnp.int32),
            shaped((1, half)),
        ),
        (
            place, hbm(system_values[0], pltpu.HBM), block_pattern[0], subset_order,
            hbm(start_volume, pltpu.HBM),
        ),
        [SM, HB, SM, VM, HB],
        work,
        "load",
        scratch=[
            pltpu.VMEM((fronts, slices, voxels), BF16),
            pltpu.SemaphoreType.DMA((loads,)),
            pltpu.SemaphoreType.DMA,
        ],
        vmem=10 << 20,
    )
    matrix = pltpu.with_memory_space_constraint(matrix, pltpu.VMEM)
    flipped = pltpu.with_memory_space_constraint(flipped, pltpu.VMEM)

    def products(kernel, shape, args, specs, name):
        return call(kernel, shape, args, specs, work // 2, name)

    targets = jnp.where(second == 0, measured[0][:, :, :half], measured[0][:, :, half:])
    these = [slice(n * batch, (n + 1) * batch) for n in range(BATCHES)]
    now = [volume[n] for n in range(BATCHES)]
    narrow = [all_rows[n] for n in range(BATCHES)]
    column = [jnp.zeros((1, voxels), F32)] * BATCHES
    inverse_row = [None] * BATCHES
    token = None
    for j in range(passes):
        totals = []
        for n in range(BATCHES):
            if j > 0:
                now[n] = after(now[n], token).astype(F32)
                narrow[n] = now[n].astype(BF16)
            height = narrow[n].shape[0]
            sent, held = [
                products(
                    project, shaped((height, half)), (where, narrow[n], flipped), [SM, VM, VM],
                    "project",
                )
                for where in (other, own)
            ]
            got = swapped((sent * RAY_SCALE).astype(F16), "tile", 1)
            totals.append(held * RAY_SCALE + got.astype(F32))
            token = totals[n].astype(F16)
        bit = 2
        while bit < tiles:
            got = [swapped(t.astype(F16), "tile", bit) for t in totals]
            for n in range(BATCHES):
                totals[n] = totals[n] + after(got[n], token).astype(F32)
                token = totals[n].astype(F16)
            bit *= 2
        for n in range(BATCHES):
            total = totals[n] if n == 0 else after(totals[n], token)
            if j == 0:
                inverse_row[n] = 1.0 / total[batch : batch + 1]
                total = total[:batch]
            target = pick(turn[these[n]], j, targets[:, these[n]].astype(F32)) * RAY_SCALE
            residue = ((target - total) * inverse_row[n]).astype(BF16)
            if j == 0:
                residue = jnp.concatenate([residue, jnp.ones((EXTRA, half), BF16)])
            height = residue.shape[0]
            their_residue = swapped(residue, "tile", 1)
            spread = products(
                spread_first, shaped((height, voxels)), (own, residue, matrix),
                [SM, VM, VM], "spread_first",
            )
            shapes = [shaped((batch, voxels))]
            if j == 0:
                shapes.append(shaped((1, voxels)))
            got = products(
                functools.partial(spread_last, j == 0), tuple(shapes),
                (other, their_residue, spread, now[n], column[n], matrix),
                [SM, VM, VM, VM, VM, VM], "spread_last",
            )
            now[n] = got[0]
            if j == 0:
                column[n] = got[1]
            token = now[n].astype(F16)
            if j + 1 < passes:
                now[n] = passed(token, "subset", 1)
    outs = []
    for n in range(BATCHES):
        found = from_all_owners(now[n].astype(BF16))
        parts = []
        for f in range(fronts):
            got = found[0]
            for d in range(1, owners):
                got = jnp.where(apart[these[n], f : f + 1] == d, found[d], got)
            parts.append(got)
        outs.append(jnp.stack(parts))
    return jnp.concatenate(outs, axis=1)


def solution(mesh):
    placed = (
        P(None, None, "tile"),
        P("subset", None, None, None),
        P("subset", None, "tile"),
        P("subset", None, "tile"),
        P(),
    )
    return jax.shard_map(
        body, mesh=mesh, in_specs=placed, out_specs=P(None, None, "tile"), check_vma=False
    )
```

profile of v0, /device:TPU:0, one launch (start us, length us, event | category | flops | bytes accessed | tf_op | source)
XLA Modules:
  0.0 158.2 jit_solution(10980338800843886549)
XLA Ops:
  1.5 10.6 %load.1 = (bf16[2048,4096]{1,0:T(8,128)(2,1)S(1)}, bf16[4096,2048]{1,0:T(8,128)(2,1)S(1)}, bf16[2,48,4096]{2,1,0:T(8,128)(2,1)S(1)}, f32[2,32,4096]{2,1,0:T(8,12...) custom-call(s32[3]{0:T(128)S(1)} %pad_add_fusion.place, bf16[2048,4096]{1,0:T(8,128)(2,1)} %bitcast.124, ...), custom_call_target="tpu_custom_call" | custom-call | flops 17179869184 | tf_op jit(solution)/shard_map/load/pallas_call | solution.py:23
  20.9 3.1 %collective-permute-start.1 = (f16[48,1024]{1,0:T(8,128)(2,1)S(1)}, f16[48,1024]{1,0:T(8,128)(2,1)S(1)}, u32[]{:S(2)}, u32[]{:S(2)}) collective-permute-start(f16[48,1024]{1,0:T(8,128)(2,1)S(1)} %fusion.10), channel_id=1, source_target_pairs={{0,2},{1,3},{2,0},{3,1},{4,6},{5,7},{6,4},{7,5},{8,10},{9,11},{10,... | collective-permute-start | bytes 294920 | tf_op jit(solution)/shard_map/ppermute | solution.py:162
  24.1 3.2 %collective-permute-done.1 = f16[48,1024]{1,0:T(8,128)(2,1)S(1)} collective-permute-done((f16[48,1024]{1,0:T(8,128)(2,1)S(1)}, f16[48,1024]{1,0:T(8,128)(2,1)S(1)}, u32[]{:S(2)}, u32[]{:S(2)}) %collective-permute-start.1) | collective-permute-done | bytes 98336 | tf_op jit(solution)/shard_map/ppermute | solution.py:162
  27.4 3.1 %collective-permute-start.3 = (f16[48,1024]{1,0:T(8,128)(2,1)S(1)}, f16[48,1024]{1,0:T(8,128)(2,1)S(1)}, u32[]{:S(2)}, u32[]{:S(2)}) collective-permute-start(f16[48,1024]{1,0:T(8,128)(2,1)S(1)} %fusion), channel_id=1, source_target_pairs={{0,4},{1,5},{2,6},{3,7},{4,0},{5,1},{6,2},{7,3},{8,12},{9,13},{10,... | collective-permute-start | bytes 294920 | tf_op jit(solution)/shard_map/ppermute | solution.py:162
  30.6 2.1 %collective-permute-start.7 = (f16[48,1024]{1,0:T(8,128)(2,1)S(1)}, f16[48,1024]{1,0:T(8,128)(2,1)S(1)}, u32[]{:S(2)}, u32[]{:S(2)}) collective-permute-start(f16[48,1024]{1,0:T(8,128)(2,1)S(1)} %fusion.1), channel_id=1, source_target_pairs={{0,4},{1,5},{2,6},{3,7},{4,0},{5,1},{6,2},{7,3},{8,12},{9,13},{10,... | collective-permute-start | bytes 294920 | tf_op jit(solution)/shard_map/ppermute | solution.py:162
  32.6 4.9 %collective-permute-done.3 = f16[48,1024]{1,0:T(8,128)(2,1)S(1)} collective-permute-done((f16[48,1024]{1,0:T(8,128)(2,1)S(1)}, f16[48,1024]{1,0:T(8,128)(2,1)S(1)}, u32[]{:S(2)}, u32[]{:S(2)}) %collective-permute-start.3) | collective-permute-done | bytes 98336 | tf_op jit(solution)/shard_map/ppermute | solution.py:162
  37.8 1.7 %spread_first.8.so_far = f32[48,4096]{1,0:T(8,128)S(1)} custom-call(s32[1]{0:T(128)} %bitcast.1.place, bf16[48,1024]{1,0:T(8,128)(2,1)S(1)} %concatenate.15.residue, bf16[2048,4096]{1,0:T(8,128)(2,1)S(1)} %get-tuple-element.51.matrix), custom_call_target="tpu_custom_call" | custom-call | flops 8589934592 | tf_op jit(solution)/shard_map/spread_first/pallas_call | solution.py:23
  39.5 1.7 %spread_last.8 = (f32[32,4096]{1,0:T(8,128)S(1)}, f32[1,4096]{1,0:T(1,128)S(1)}) custom-call(s32[1]{0:T(128)} %bitcast.2.place, bf16[48,1024]{1,0:T(8,128)(2,1)S(1)} %collective-permute-done.5.residue, f32[48,4096]{1,0:T(8,128)S(1)} %spread_first.8.so_far, f32[32,4096]{1,0:T(8,128)S(1)} %get-tuple-element.132.volume, ...), custom_call_target="tpu_custom_call" | custom-call | flops 8589934592 | tf_op jit(solution)/shard_map/spread_last/pallas_call | solution.py:23
  45.0 1.7 %spread_last.9 = (f32[32,4096]{1,0:T(8,128)S(1)}, f32[1,4096]{1,0:T(1,128)S(1)}) custom-call(s32[1]{0:T(128)} %bitcast.2.place, bf16[48,1024]{1,0:T(8,128)(2,1)S(1)} %collective-permute-done.8.residue, f32[48,4096]{1,0:T(8,128)S(1)} %spread_first.9.so_far, f32[32,4096]{1,0:T(8,128)S(1)} %get-tuple-element.131.volume, ...), custom_call_target="tpu_custom_call" | custom-call | flops 8589934592 | tf_op jit(solution)/shard_map/spread_last/pallas_call | solution.py:23
  46.8 1.7 %collective-permute-start.11 = (f16[32,4096]{1,0:T(8,128)(2,1)S(1)}, f16[32,4096]{1,0:T(8,128)(2,1)S(1)}, u32[]{:S(2)}, u32[]{:S(2)}) collective-permute-start(f16[32,4096]{1,0:T(8,128)(2,1)S(1)} %convert_element_type.277), channel_id=1, source_target_pairs={{0,8},{8,16},{16,24},{24,0},{1,9},{9,17},{17,25},{25,1},{2,10},{10... | collective-permute-start | bytes 786440 | tf_op jit(solution)/shard_map/ppermute | solution.py:157
  48.5 2.6 %collective-permute-done.6 = f16[32,4096]{1,0:T(8,128)(2,1)S(1)} collective-permute-done((f16[32,4096]{1,0:T(8,128)(2,1)S(1)}, f16[32,4096]{1,0:T(8,128)(2,1)S(1)}, u32[]{:S(2)}, u32[]{:S(2)}) %collective-permute-start.6) | collective-permute-done | bytes 262176 | tf_op jit(solution)/shard_map/ppermute | solution.py:157
  54.7 1.9 %collective-permute-done.11 = f16[32,4096]{1,0:T(8,128)(2,1)S(1)} collective-permute-done((f16[32,4096]{1,0:T(8,128)(2,1)S(1)}, f16[32,4096]{1,0:T(8,128)(2,1)S(1)}, u32[]{:S(2)}, u32[]{:S(2)}) %collective-permute-start.11) | collective-permute-done | bytes 262176 | tf_op jit(solution)/shard_map/ppermute | solution.py:157
  60.2 3.4 %collective-permute-start.13 = (f16[32,1024]{1,0:T(8,128)(2,1)S(1)}, f16[32,1024]{1,0:T(8,128)(2,1)S(1)}, u32[]{:S(2)}, u32[]{:S(2)}) collective-permute-start(f16[32,1024]{1,0:T(8,128)(2,1)S(1)} %fusion.4), channel_id=1, source_target_pairs={{0,4},{1,5},{2,6},{3,7},{4,0},{5,1},{6,2},{7,3},{8,12},{9,13},{10,... | collective-permute-start | bytes 196616 | tf_op jit(solution)/shard_map/ppermute | solution.py:162
  64.5 2.4 %collective-permute-start.17 = (f16[32,1024]{1,0:T(8,128)(2,1)S(1)}, f16[32,1024]{1,0:T(8,128)(2,1)S(1)}, u32[]{:S(2)}, u32[]{:S(2)}) collective-permute-start(f16[32,1024]{1,0:T(8,128)(2,1)S(1)} %fusion.5), channel_id=1, source_target_pairs={{0,4},{1,5},{2,6},{3,7},{4,0},{5,1},{6,2},{7,3},{8,12},{9,13},{10,... | collective-permute-start | bytes 196616 | tf_op jit(solution)/shard_map/ppermute | solution.py:162
  69.4 1.7 %spread_last.10 = f32[32,4096]{1,0:T(8,128)S(1)} custom-call(s32[1]{0:T(128)} %bitcast.2.place, bf16[32,1024]{1,0:T(8,128)(2,1)S(1)} %collective-permute-done.15.residue, f32[32,4096]{1,0:T(8,128)S(1)} %spread_first.10.so_far, f32[32,4096]{1,0:T(8,128)S(1)} %get-tuple-element.147.volume, f32[1,4096]{1,0:T(1,128)S(1)} %get-tuple-element.61.column, ...), custom_call_target="tpu_custom_call" | custom-call | flops 8589934592 | tf_op jit(solution)/shard_map/spread_last/pallas_call | solution.py:23
  73.9 1.7 %spread_last.11 = f32[32,4096]{1,0:T(8,128)S(1)} custom-call(s32[1]{0:T(128)} %bitcast.2.place, bf16[32,1024]{1,0:T(8,128)(2,1)S(1)} %collective-permute-done.18.residue, f32[32,4096]{1,0:T(8,128)S(1)} %spread_first.11.so_far, f32[32,4096]{1,0:T(8,128)S(1)} %get-tuple-element.145.volume, f32[1,4096]{1,0:T(1,128)S(1)} %get-tuple-element.63.column, ...), custom_call_target="tpu_custom_call" | custom-call | flops 8589934592 | tf_op jit(solution)/shard_map/spread_last/pallas_call | solution.py:23
  75.6 2.7 %collective-permute-start.21 = (f16[32,4096]{1,0:T(8,128)(2,1)S(1)}, f16[32,4096]{1,0:T(8,128)(2,1)S(1)}, u32[]{:S(2)}, u32[]{:S(2)}) collective-permute-start(f16[32,4096]{1,0:T(8,128)(2,1)S(1)} %convert_element_type.297), channel_id=1, source_target_pairs={{0,8},{8,16},{16,24},{24,0},{1,9},{9,17},{17,25},{25,1},{2,10},{10... | collective-permute-start | bytes 786440 | tf_op jit(solution)/shard_map/ppermute | solution.py:157
  78.3 2.9 %collective-permute-done.16 = f16[32,4096]{1,0:T(8,128)(2,1)S(1)} collective-permute-done((f16[32,4096]{1,0:T(8,128)(2,1)S(1)}, f16[32,4096]{1,0:T(8,128)(2,1)S(1)}, u32[]{:S(2)}, u32[]{:S(2)}) %collective-permute-start.16) | collective-permute-done | bytes 262176 | tf_op jit(solution)/shard_map/ppermute | solution.py:157
  84.5 1.9 %collective-permute-start.20 = (f16[32,1024]{1,0:T(8,128)(2,1)S(1)}, f16[32,1024]{1,0:T(8,128)(2,1)S(1)}, u32[]{:S(2)}, u32[]{:S(2)}) collective-permute-start(f16[32,1024]{1,0:T(8,128)(2,1)S(1)} %fusion.14), channel_id=1, source_target_pairs={{0,2},{1,3},{2,0},{3,1},{4,6},{5,7},{6,4},{7,5},{8,10},{9,11},{10,... | collective-permute-start | bytes 196616 | tf_op jit(solution)/shard_map/ppermute | solution.py:162
  89.9 1.7 %collective-permute-start.24 = (f16[32,1024]{1,0:T(8,128)(2,1)S(1)}, f16[32,1024]{1,0:T(8,128)(2,1)S(1)}, u32[]{:S(2)}, u32[]{:S(2)}) collective-permute-start(f16[32,1024]{1,0:T(8,128)(2,1)S(1)} %fusion.15), channel_id=1, source_target_pairs={{0,2},{1,3},{2,0},{3,1},{4,6},{5,7},{6,4},{7,5},{8,10},{9,11},{10,... | collective-permute-start | bytes 196616 | tf_op jit(solution)/shard_map/ppermute | solution.py:162
  95.8 2.3 %collective-permute-done.23 = f16[32,1024]{1,0:T(8,128)(2,1)S(1)} collective-permute-done((f16[32,1024]{1,0:T(8,128)(2,1)S(1)}, f16[32,1024]{1,0:T(8,128)(2,1)S(1)}, u32[]{:S(2)}, u32[]{:S(2)}) %collective-permute-start.23) | collective-permute-done | bytes 65568 | tf_op jit(solution)/shard_map/ppermute | solution.py:162
  100.0 1.7 %spread_last.12 = f32[32,4096]{1,0:T(8,128)S(1)} custom-call(s32[1]{0:T(128)} %bitcast.2.place, bf16[32,1024]{1,0:T(8,128)(2,1)S(1)} %collective-permute-done.25.residue, f32[32,4096]{1,0:T(8,128)S(1)} %spread_first.12.so_far, f32[32,4096]{1,0:T(8,128)S(1)} %get-tuple-element.143.volume, f32[1,4096]{1,0:T(1,128)S(1)} %get-tuple-element.61.column, ...), custom_call_target="tpu_custom_call" | custom-call | flops 8589934592 | tf_op jit(solution)/shard_map/spread_last/pallas_call | solution.py:23
  104.2 1.7 %spread_last.13 = f32[32,4096]{1,0:T(8,128)S(1)} custom-call(s32[1]{0:T(128)} %bitcast.2.place, bf16[32,1024]{1,0:T(8,128)(2,1)S(1)} %collective-permute-done.28.residue, f32[32,4096]{1,0:T(8,128)S(1)} %spread_first.13.so_far, f32[32,4096]{1,0:T(8,128)S(1)} %get-tuple-element.141.volume, f32[1,4096]{1,0:T(1,128)S(1)} %get-tuple-element.63.column, ...), custom_call_target="tpu_custom_call" | custom-call | flops 8589934592 | tf_op jit(solution)/shard_map/spread_last/pallas_call | solution.py:23
  106.0 3.0 %collective-permute-start.31 = (f16[32,4096]{1,0:T(8,128)(2,1)S(1)}, f16[32,4096]{1,0:T(8,128)(2,1)S(1)}, u32[]{:S(2)}, u32[]{:S(2)}) collective-permute-start(f16[32,4096]{1,0:T(8,128)(2,1)S(1)} %convert_element_type.317), channel_id=1, source_target_pairs={{0,8},{8,16},{16,24},{24,0},{1,9},{9,17},{17,25},{25,1},{2,10},{10... | collective-permute-start | bytes 786440 | tf_op jit(solution)/shard_map/ppermute | solution.py:157
  109.0 2.8 %collective-permute-done.26 = f16[32,4096]{1,0:T(8,128)(2,1)S(1)} collective-permute-done((f16[32,4096]{1,0:T(8,128)(2,1)S(1)}, f16[32,4096]{1,0:T(8,128)(2,1)S(1)}, u32[]{:S(2)}, u32[]{:S(2)}) %collective-permute-start.26) | collective-permute-done | bytes 262176 | tf_op jit(solution)/shard_map/ppermute | solution.py:157
  122.0 4.0 %collective-permute-done.34 = f16[32,1024]{1,0:T(8,128)(2,1)S(1)} collective-permute-done((f16[32,1024]{1,0:T(8,128)(2,1)S(1)}, f16[32,1024]{1,0:T(8,128)(2,1)S(1)}, u32[]{:S(2)}, u32[]{:S(2)}) %collective-permute-start.34) | collective-permute-done | bytes 65568 | tf_op jit(solution)/shard_map/ppermute | solution.py:162
  129.5 1.7 %collective-permute-done.40 = f16[32,1024]{1,0:T(8,128)(2,1)S(1)} collective-permute-done((f16[32,1024]{1,0:T(8,128)(2,1)S(1)}, f16[32,1024]{1,0:T(8,128)(2,1)S(1)}, u32[]{:S(2)}, u32[]{:S(2)}) %collective-permute-start.40) | collective-permute-done | bytes 65568 | tf_op jit(solution)/shard_map/ppermute | solution.py:162
  133.2 1.7 %spread_last.14 = f32[32,4096]{1,0:T(8,128)S(1)} custom-call(s32[1]{0:T(128)} %bitcast.2.place, bf16[32,1024]{1,0:T(8,128)(2,1)S(1)} %collective-permute-done.35.residue, f32[32,4096]{1,0:T(8,128)S(1)} %spread_first.14.so_far, f32[32,4096]{1,0:T(8,128)S(1)} %get-tuple-element.137.volume, f32[1,4096]{1,0:T(1,128)S(1)} %get-tuple-element.61.column, ...), custom_call_target="tpu_custom_call" | custom-call | flops 8589934592 | tf_op jit(solution)/shard_map/spread_last/pallas_call | solution.py:23
  136.6 1.7 %spread_last.15 = f32[32,4096]{1,0:T(8,128)S(1)} custom-call(s32[1]{0:T(128)} %bitcast.2.place, bf16[32,1024]{1,0:T(8,128)(2,1)S(1)} %collective-permute-done.41.residue, f32[32,4096]{1,0:T(8,128)S(1)} %spread_first.15.so_far, f32[32,4096]{1,0:T(8,128)S(1)} %get-tuple-element.139.volume, f32[1,4096]{1,0:T(1,128)S(1)} %get-tuple-element.63.column, ...), custom_call_target="tpu_custom_call" | custom-call | flops 8589934592 | tf_op jit(solution)/shard_map/spread_last/pallas_call | solution.py:23
  138.3 2.0 %collective-permute-start.44 = (bf16[32,4096]{1,0:T(8,128)(2,1)S(1)}, bf16[32,4096]{1,0:T(8,128)(2,1)S(1)}, u32[]{:S(2)}, u32[]{:S(2)}) collective-permute-start(bf16[32,4096]{1,0:T(8,128)(2,1)S(1)} %convert_element_type.337), channel_id=1, source_target_pairs={{0,8},{8,0},{16,24},{24,16},{1,9},{9,1},{17,25},{25,17},{2,10},{10... | collective-permute-start | bytes 786440 | tf_op jit(solution)/shard_map/ppermute | solution.py:162
  140.9 3.7 %collective-permute-done.36 = bf16[32,4096]{1,0:T(8,128)(2,1)S(1)} collective-permute-done((bf16[32,4096]{1,0:T(8,128)(2,1)S(1)}, bf16[32,4096]{1,0:T(8,128)(2,1)S(1)}, u32[]{:S(2)}, u32[]{:S(2)}) %collective-permute-start.36) | collective-permute-done | bytes 262176 | tf_op jit(solution)/shard_map/ppermute | solution.py:162
  153.2 3.1 %collective-permute-done.43 = bf16[32,2048]{1,0:T(8,128)(2,1)S(1)} collective-permute-done((bf16[32,2048]{1,0:T(8,128)(2,1)S(1)}, bf16[32,2048]{1,0:T(8,128)(2,1)S(1)}, u32[]{:S(2)}, u32[]{:S(2)}) %collective-permute-start.43) | collective-permute-done | bytes 131104 | tf_op jit(solution)/shard_map/ppermute | solution.py:162
  (202 shorter events, 71.2 us)
Async XLA Ops:
  13.8 7.1 %collective-permute-start = (f16[48,1024]{1,0:T(8,128)(2,1)S(1)}, f16[48,1024]{1,0:T(8,128)(2,1)S(1)}, u32[]{:S(2)}, u32[]{:S(2)}) collective-permute-start(f16[48,1024]{1,0:T(8,128)(2,1)S(1)} %multiply_convert_fusion.1), channel_id=1, source_target_pairs={{0,1},{1,0},{2,3},{3,2},{4,5},{5,4},{6,7},{7,6},{8,9},{9,8},{10,11... | collective-permute-start | bytes 294920 | tf_op jit(solution)/shard_map/ppermute | solution.py:162
  15.9 8.1 %collective-permute-start.2 = (f16[48,1024]{1,0:T(8,128)(2,1)S(1)}, f16[48,1024]{1,0:T(8,128)(2,1)S(1)}, u32[]{:S(2)}, u32[]{:S(2)}) collective-permute-start(f16[48,1024]{1,0:T(8,128)(2,1)S(1)} %multiply_convert_fusion), channel_id=1, source_target_pairs={{0,1},{1,0},{2,3},{3,2},{4,5},{5,4},{6,7},{7,6},{8,9},{9,8},{10,11... | collective-permute-start | bytes 294920 | tf_op jit(solution)/shard_map/ppermute | solution.py:162
  20.9 6.5 %collective-permute-start.1 = (f16[48,1024]{1,0:T(8,128)(2,1)S(1)}, f16[48,1024]{1,0:T(8,128)(2,1)S(1)}, u32[]{:S(2)}, u32[]{:S(2)}) collective-permute-start(f16[48,1024]{1,0:T(8,128)(2,1)S(1)} %fusion.10), channel_id=1, source_target_pairs={{0,2},{1,3},{2,0},{3,1},{4,6},{5,7},{6,4},{7,5},{8,10},{9,11},{10,... | collective-permute-start | bytes 294920 | tf_op jit(solution)/shard_map/ppermute | solution.py:162
  24.0 6.5 %collective-permute-start.4 = (f16[48,1024]{1,0:T(8,128)(2,1)S(1)}, f16[48,1024]{1,0:T(8,128)(2,1)S(1)}, u32[]{:S(2)}, u32[]{:S(2)}) collective-permute-start(f16[48,1024]{1,0:T(8,128)(2,1)S(1)} %fusion.11), channel_id=1, source_target_pairs={{0,2},{1,3},{2,0},{3,1},{4,6},{5,7},{6,4},{7,5},{8,10},{9,11},{10,... | collective-permute-start | bytes 294920 | tf_op jit(solution)/shard_map/ppermute | solution.py:162
  27.4 10.1 %collective-permute-start.3 = (f16[48,1024]{1,0:T(8,128)(2,1)S(1)}, f16[48,1024]{1,0:T(8,128)(2,1)S(1)}, u32[]{:S(2)}, u32[]{:S(2)}) collective-permute-start(f16[48,1024]{1,0:T(8,128)(2,1)S(1)} %fusion), channel_id=1, source_target_pairs={{0,4},{1,5},{2,6},{3,7},{4,0},{5,1},{6,2},{7,3},{8,12},{9,13},{10,... | collective-permute-start | bytes 294920 | tf_op jit(solution)/shard_map/ppermute | solution.py:162
  30.6 8.9 %collective-permute-start.7 = (f16[48,1024]{1,0:T(8,128)(2,1)S(1)}, f16[48,1024]{1,0:T(8,128)(2,1)S(1)}, u32[]{:S(2)}, u32[]{:S(2)}) collective-permute-start(f16[48,1024]{1,0:T(8,128)(2,1)S(1)} %fusion.1), channel_id=1, source_target_pairs={{0,4},{1,5},{2,6},{3,7},{4,0},{5,1},{6,2},{7,3},{8,12},{9,13},{10,... | collective-permute-start | bytes 294920 | tf_op jit(solution)/shard_map/ppermute | solution.py:162
  41.3 9.8 %collective-permute-start.6 = (f16[32,4096]{1,0:T(8,128)(2,1)S(1)}, f16[32,4096]{1,0:T(8,128)(2,1)S(1)}, u32[]{:S(2)}, u32[]{:S(2)}) collective-permute-start(f16[32,4096]{1,0:T(8,128)(2,1)S(1)} %convert_element_type.273), channel_id=1, source_target_pairs={{0,8},{8,16},{16,24},{24,0},{1,9},{9,17},{17,25},{25,1},{2,10},{10... | collective-permute-start | bytes 786440 | tf_op jit(solution)/shard_map/ppermute | solution.py:157
  46.8 9.8 %collective-permute-start.11 = (f16[32,4096]{1,0:T(8,128)(2,1)S(1)}, f16[32,4096]{1,0:T(8,128)(2,1)S(1)}, u32[]{:S(2)}, u32[]{:S(2)}) collective-permute-start(f16[32,4096]{1,0:T(8,128)(2,1)S(1)} %convert_element_type.277), channel_id=1, source_target_pairs={{0,8},{8,16},{16,24},{24,0},{1,9},{9,17},{17,25},{25,1},{2,10},{10... | collective-permute-start | bytes 786440 | tf_op jit(solution)/shard_map/ppermute | solution.py:157
  54.4 5.7 %collective-permute-start.10 = (f16[32,1024]{1,0:T(8,128)(2,1)S(1)}, f16[32,1024]{1,0:T(8,128)(2,1)S(1)}, u32[]{:S(2)}, u32[]{:S(2)}) collective-permute-start(f16[32,1024]{1,0:T(8,128)(2,1)S(1)} %fusion.12), channel_id=1, source_target_pairs={{0,2},{1,3},{2,0},{3,1},{4,6},{5,7},{6,4},{7,5},{8,10},{9,11},{10,... | collective-permute-start | bytes 196616 | tf_op jit(solution)/shard_map/ppermute | solution.py:162
  60.2 7.3 %collective-permute-start.13 = (f16[32,1024]{1,0:T(8,128)(2,1)S(1)}, f16[32,1024]{1,0:T(8,128)(2,1)S(1)}, u32[]{:S(2)}, u32[]{:S(2)}) collective-permute-start(f16[32,1024]{1,0:T(8,128)(2,1)S(1)} %fusion.4), channel_id=1, source_target_pairs={{0,4},{1,5},{2,6},{3,7},{4,0},{5,1},{6,2},{7,3},{8,12},{9,13},{10,... | collective-permute-start | bytes 196616 | tf_op jit(solution)/shard_map/ppermute | solution.py:162
  64.5 7.3 %collective-permute-start.17 = (f16[32,1024]{1,0:T(8,128)(2,1)S(1)}, f16[32,1024]{1,0:T(8,128)(2,1)S(1)}, u32[]{:S(2)}, u32[]{:S(2)}) collective-permute-start(f16[32,1024]{1,0:T(8,128)(2,1)S(1)} %fusion.5), channel_id=1, source_target_pairs={{0,4},{1,5},{2,6},{3,7},{4,0},{5,1},{6,2},{7,3},{8,12},{9,13},{10,... | collective-permute-start | bytes 196616 | tf_op jit(solution)/shard_map/ppermute | solution.py:162
  71.1 10.1 %collective-permute-start.16 = (f16[32,4096]{1,0:T(8,128)(2,1)S(1)}, f16[32,4096]{1,0:T(8,128)(2,1)S(1)}, u32[]{:S(2)}, u32[]{:S(2)}) collective-permute-start(f16[32,4096]{1,0:T(8,128)(2,1)S(1)} %convert_element_type.294), channel_id=1, source_target_pairs={{0,8},{8,16},{16,24},{24,0},{1,9},{9,17},{17,25},{25,1},{2,10},{10... | collective-permute-start | bytes 786440 | tf_op jit(solution)/shard_map/ppermute | solution.py:157
  75.6 10.8 %collective-permute-start.21 = (f16[32,4096]{1,0:T(8,128)(2,1)S(1)}, f16[32,4096]{1,0:T(8,128)(2,1)S(1)}, u32[]{:S(2)}, u32[]{:S(2)}) collective-permute-start(f16[32,4096]{1,0:T(8,128)(2,1)S(1)} %convert_element_type.297), channel_id=1, source_target_pairs={{0,8},{8,16},{16,24},{24,0},{1,9},{9,17},{17,25},{25,1},{2,10},{10... | collective-permute-start | bytes 786440 | tf_op jit(solution)/shard_map/ppermute | solution.py:157
  84.5 7.1 %collective-permute-start.20 = (f16[32,1024]{1,0:T(8,128)(2,1)S(1)}, f16[32,1024]{1,0:T(8,128)(2,1)S(1)}, u32[]{:S(2)}, u32[]{:S(2)}) collective-permute-start(f16[32,1024]{1,0:T(8,128)(2,1)S(1)} %fusion.14), channel_id=1, source_target_pairs={{0,2},{1,3},{2,0},{3,1},{4,6},{5,7},{6,4},{7,5},{8,10},{9,11},{10,... | collective-permute-start | bytes 196616 | tf_op jit(solution)/shard_map/ppermute | solution.py:162
  91.7 6.5 %collective-permute-start.23 = (f16[32,1024]{1,0:T(8,128)(2,1)S(1)}, f16[32,1024]{1,0:T(8,128)(2,1)S(1)}, u32[]{:S(2)}, u32[]{:S(2)}) collective-permute-start(f16[32,1024]{1,0:T(8,128)(2,1)S(1)} %fusion.6), channel_id=1, source_target_pairs={{0,4},{1,5},{2,6},{3,7},{4,0},{5,1},{6,2},{7,3},{8,12},{9,13},{10,... | collective-permute-start | bytes 196616 | tf_op jit(solution)/shard_map/ppermute | solution.py:162
  94.4 7.7 %collective-permute-start.27 = (f16[32,1024]{1,0:T(8,128)(2,1)S(1)}, f16[32,1024]{1,0:T(8,128)(2,1)S(1)}, u32[]{:S(2)}, u32[]{:S(2)}) collective-permute-start(f16[32,1024]{1,0:T(8,128)(2,1)S(1)} %fusion.7), channel_id=1, source_target_pairs={{0,4},{1,5},{2,6},{3,7},{4,0},{5,1},{6,2},{7,3},{8,12},{9,13},{10,... | collective-permute-start | bytes 196616 | tf_op jit(solution)/shard_map/ppermute | solution.py:162
  101.8 10.1 %collective-permute-start.26 = (f16[32,4096]{1,0:T(8,128)(2,1)S(1)}, f16[32,4096]{1,0:T(8,128)(2,1)S(1)}, u32[]{:S(2)}, u32[]{:S(2)}) collective-permute-start(f16[32,4096]{1,0:T(8,128)(2,1)S(1)} %convert_element_type.314), channel_id=1, source_target_pairs={{0,8},{8,16},{16,24},{24,0},{1,9},{9,17},{17,25},{25,1},{2,10},{10... | collective-permute-start | bytes 786440 | tf_op jit(solution)/shard_map/ppermute | solution.py:157
  106.0 11.0 %collective-permute-start.31 = (f16[32,4096]{1,0:T(8,128)(2,1)S(1)}, f16[32,4096]{1,0:T(8,128)(2,1)S(1)}, u32[]{:S(2)}, u32[]{:S(2)}) collective-permute-start(f16[32,4096]{1,0:T(8,128)(2,1)S(1)} %convert_element_type.317), channel_id=1, source_target_pairs={{0,8},{8,16},{16,24},{24,0},{1,9},{9,17},{17,25},{25,1},{2,10},{10... | collective-permute-start | bytes 786440 | tf_op jit(solution)/shard_map/ppermute | solution.py:157
  115.1 5.8 %collective-permute-start.30 = (f16[32,1024]{1,0:T(8,128)(2,1)S(1)}, f16[32,1024]{1,0:T(8,128)(2,1)S(1)}, u32[]{:S(2)}, u32[]{:S(2)}) collective-permute-start(f16[32,1024]{1,0:T(8,128)(2,1)S(1)} %fusion.16), channel_id=1, source_target_pairs={{0,2},{1,3},{2,0},{3,1},{4,6},{5,7},{6,4},{7,5},{8,10},{9,11},{10,... | collective-permute-start | bytes 196616 | tf_op jit(solution)/shard_map/ppermute | solution.py:162
  120.4 5.5 %collective-permute-start.34 = (f16[32,1024]{1,0:T(8,128)(2,1)S(1)}, f16[32,1024]{1,0:T(8,128)(2,1)S(1)}, u32[]{:S(2)}, u32[]{:S(2)}) collective-permute-start(f16[32,1024]{1,0:T(8,128)(2,1)S(1)} %fusion.17), channel_id=1, source_target_pairs={{0,2},{1,3},{2,0},{3,1},{4,6},{5,7},{6,4},{7,5},{8,10},{9,11},{10,... | collective-permute-start | bytes 196616 | tf_op jit(solution)/shard_map/ppermute | solution.py:162
  121.0 6.6 %collective-permute-start.33 = (f16[32,1024]{1,0:T(8,128)(2,1)S(1)}, f16[32,1024]{1,0:T(8,128)(2,1)S(1)}, u32[]{:S(2)}, u32[]{:S(2)}) collective-permute-start(f16[32,1024]{1,0:T(8,128)(2,1)S(1)} %fusion.8), channel_id=1, source_target_pairs={{0,4},{1,5},{2,6},{3,7},{4,0},{5,1},{6,2},{7,3},{8,12},{9,13},{10,... | collective-permute-start | bytes 196616 | tf_op jit(solution)/shard_map/ppermute | solution.py:162
  126.0 5.3 %collective-permute-start.40 = (f16[32,1024]{1,0:T(8,128)(2,1)S(1)}, f16[32,1024]{1,0:T(8,128)(2,1)S(1)}, u32[]{:S(2)}, u32[]{:S(2)}) collective-permute-start(f16[32,1024]{1,0:T(8,128)(2,1)S(1)} %fusion.9), channel_id=1, source_target_pairs={{0,4},{1,5},{2,6},{3,7},{4,0},{5,1},{6,2},{7,3},{8,12},{9,13},{10,... | collective-permute-start | bytes 196616 | tf_op jit(solution)/shard_map/ppermute | solution.py:162
  127.8 5.4 %collective-permute-start.35 = (bf16[32,1024]{1,0:T(8,128)(2,1)S(1)}, bf16[32,1024]{1,0:T(8,128)(2,1)S(1)}, u32[]{:S(2)}, u32[]{:S(2)}) collective-permute-start(bf16[32,1024]{1,0:T(8,128)(2,1)S(1)} %multiply_convert_fusion.3.residue), channel_id=1, source_target_pairs={{0,1},{1,0},{2,3},{3,2},{4,5},{5,4},{6,7},{7,6},{8,9},{9,8},{10,11... | collective-permute-start | bytes 196616 | tf_op jit(solution)/shard_map/ppermute | solution.py:162
  131.4 5.2 %collective-permute-start.41 = (bf16[32,1024]{1,0:T(8,128)(2,1)S(1)}, bf16[32,1024]{1,0:T(8,128)(2,1)S(1)}, u32[]{:S(2)}, u32[]{:S(2)}) collective-permute-start(bf16[32,1024]{1,0:T(8,128)(2,1)S(1)} %multiply_convert_fusion.2.residue), channel_id=1, source_target_pairs={{0,1},{1,0},{2,3},{3,2},{4,5},{5,4},{6,7},{7,6},{8,9},{9,8},{10,11... | collective-permute-start | bytes 196616 | tf_op jit(solution)/shard_map/ppermute | solution.py:162
  134.9 11.9 %collective-permute-start.38 = (bf16[32,4096]{1,0:T(8,128)(2,1)S(1)}, bf16[32,4096]{1,0:T(8,128)(2,1)S(1)}, u32[]{:S(2)}, u32[]{:S(2)}) collective-permute-start(bf16[32,4096]{1,0:T(8,128)(2,1)S(1)} %convert_element_type.334), channel_id=1, source_target_pairs={{0,8},{8,0},{16,24},{24,16},{1,9},{9,1},{17,25},{25,17},{2,10},{10... | collective-permute-start | bytes 786440 | tf_op jit(solution)/shard_map/ppermute | solution.py:162
  135.4 9.1 %collective-permute-start.36 = (bf16[32,4096]{1,0:T(8,128)(2,1)S(1)}, bf16[32,4096]{1,0:T(8,128)(2,1)S(1)}, u32[]{:S(2)}, u32[]{:S(2)}) collective-permute-start(bf16[32,4096]{1,0:T(8,128)(2,1)S(1)} %convert_element_type.334), channel_id=1, source_target_pairs={{0,16},{8,24},{16,0},{24,8},{1,17},{9,25},{17,1},{25,9},{2,18},{10... | collective-permute-start | bytes 786440 | tf_op jit(solution)/shard_map/ppermute | solution.py:162
  138.3 11.4 %collective-permute-start.44 = (bf16[32,4096]{1,0:T(8,128)(2,1)S(1)}, bf16[32,4096]{1,0:T(8,128)(2,1)S(1)}, u32[]{:S(2)}, u32[]{:S(2)}) collective-permute-start(bf16[32,4096]{1,0:T(8,128)(2,1)S(1)} %convert_element_type.337), channel_id=1, source_target_pairs={{0,8},{8,0},{16,24},{24,16},{1,9},{9,1},{17,25},{25,17},{2,10},{10... | collective-permute-start | bytes 786440 | tf_op jit(solution)/shard_map/ppermute | solution.py:162
  140.4 11.0 %collective-permute-start.42 = (bf16[32,4096]{1,0:T(8,128)(2,1)S(1)}, bf16[32,4096]{1,0:T(8,128)(2,1)S(1)}, u32[]{:S(2)}, u32[]{:S(2)}) collective-permute-start(bf16[32,4096]{1,0:T(8,128)(2,1)S(1)} %convert_element_type.337), channel_id=1, source_target_pairs={{0,16},{8,24},{16,0},{24,8},{1,17},{9,25},{17,1},{25,9},{2,18},{10... | collective-permute-start | bytes 786440 | tf_op jit(solution)/shard_map/ppermute | solution.py:162
  144.6 7.5 %collective-permute-start.37 = (bf16[32,2048]{1,0:T(8,128)(2,1)S(1)}, bf16[32,2048]{1,0:T(8,128)(2,1)S(1)}, u32[]{:S(2)}, u32[]{:S(2)}) collective-permute-start(bf16[32,2048]{1,0:T(8,128)(2,1)S(1)} %slice.244), channel_id=1, source_target_pairs={{0,8},{8,0},{16,24},{24,16},{1,9},{9,1},{17,25},{25,17},{2,10},{10... | collective-permute-start | bytes 393224 | tf_op jit(solution)/shard_map/ppermute | solution.py:162
  146.9 6.0 %collective-permute-start.39 = (bf16[32,2048]{1,0:T(8,128)(2,1)S(1)}, bf16[32,2048]{1,0:T(8,128)(2,1)S(1)}, u32[]{:S(2)}, u32[]{:S(2)}) collective-permute-start(bf16[32,2048]{1,0:T(8,128)(2,1)S(1)} %slice.245), channel_id=1, source_target_pairs={{0,16},{8,24},{16,0},{24,8},{1,17},{9,25},{17,1},{25,9},{2,18},{10... | collective-permute-start | bytes 393224 | tf_op jit(solution)/shard_map/ppermute | solution.py:162
  149.7 6.7 %collective-permute-start.45 = (bf16[32,2048]{1,0:T(8,128)(2,1)S(1)}, bf16[32,2048]{1,0:T(8,128)(2,1)S(1)}, u32[]{:S(2)}, u32[]{:S(2)}) collective-permute-start(bf16[32,2048]{1,0:T(8,128)(2,1)S(1)} %slice.247), channel_id=1, source_target_pairs={{0,16},{8,24},{16,0},{24,8},{1,17},{9,25},{17,1},{25,9},{2,18},{10... | collective-permute-start | bytes 393224 | tf_op jit(solution)/shard_map/ppermute | solution.py:162
  151.3 5.0 %collective-permute-start.43 = (bf16[32,2048]{1,0:T(8,128)(2,1)S(1)}, bf16[32,2048]{1,0:T(8,128)(2,1)S(1)}, u32[]{:S(2)}, u32[]{:S(2)}) collective-permute-start(bf16[32,2048]{1,0:T(8,128)(2,1)S(1)} %slice.246), channel_id=1, source_target_pairs={{0,8},{8,0},{16,24},{24,16},{1,9},{9,1},{17,25},{25,17},{2,10},{10... | collective-permute-start | bytes 393224 | tf_op jit(solution)/shard_map/ppermute | solution.py:162
  (30 other events, 110.2 us)
where the time goes:
time: 158 us
  Pallas kernels  62.3 us (39%)
  starting transfers between devices  45.1 us (29%)
  waiting for transfers between devices  41.3 us (26%)
  other arithmetic  6.63 us (4%)
  local copies, waits for them, and re-layouts  2.02 us (1%)
    pallas_call x33, Pallas kernels, call(): pl.pallas_call(kernel, out_shape=out_shape, in_specs=specs, out_specs=out...  62.3 us
    ppermute x40, starting transfers between devices, swapped(): return lax.ppermute(x, axis, [(i, i ^ bit) for i in range(size)])  35.1 us
    ppermute x40, waiting for transfers between devices, swapped(): return lax.ppermute(x, axis, [(i, i ^ bit) for i in range(size)])  29.8 us
    ppermute x6, waiting for transfers between devices, passed(): lax.ppermute(x, axis, [(i, (i + distance) % size) for i in range(size)])  11.5 us
    ppermute x6, starting transfers between devices, passed(): lax.ppermute(x, axis, [(i, (i + distance) % size) for i in range(size)])  9.93 us
  transfers between devices with their start and end apart: 46, of which 19 were waited for; matrix products, arithmetic and copies ran while one was open for 3% of the time, Pallas kernels for 31%

commit v1 on v0

--- a/solution.py
+++ b/solution.py
@@ -11,11 +11,12 @@
 RAY_SCALE = 2.0**-14
 EXTRA = 16
 COST = 16
-AHEAD = 2
+AHEAD = 3
 BATCHES = 2
 VM = pl.BlockSpec(memory_space=pltpu.VMEM)
 SM = pl.BlockSpec(memory_space=pltpu.SMEM)
 HB = pl.BlockSpec(memory_space=pltpu.HBM)
+AN = pl.BlockSpec(memory_space=pl.ANY)
 
 
 def call(kernel, out_shape, args, specs, flops, name, scratch=(), vmem=8 << 20):
@@ -43,8 +44,8 @@
 
 
 def load_kernel(
-    place, matrix_hbm, pattern, order, start_hbm, matrix, flipped, narrow, volume, turn, apart,
-    second, fronts, sems, start_sem,
+    place, matrix_hbm, pattern_hbm, order, start_hbm, matrix, flipped, narrow, volume, turn, apart,
+    second, fronts, pattern, sems, start_sem, pattern_sem,
 ):
     ray_blocks, col_blocks = pattern.shape
     ray_count, voxels = matrix.shape
@@ -59,6 +60,8 @@
         where = pl.ds(pl.multiple_of(i * rows, rows), rows)
         return pltpu.make_async_copy(matrix_hbm.at[where], matrix.at[where], sems.at[i])
 
+    blocks_in = pltpu.make_async_copy(pattern_hbm, pattern, pattern_sem)
+    blocks_in.start()
     first = pltpu.make_async_copy(start_hbm, fronts, start_sem)
     first.start()
     for i in range(AHEAD):
@@ -88,6 +91,8 @@
             volume[b, :, cols] = part
             narrow[b, :batch, cols] = part.astype(BF16)
 
+    blocks_in.wait()
+
     @pl.loop(0, loads)
     def _(i):
         piece(i).wait()
@@ -121,6 +126,14 @@
     def _(i):
         where = pl.ds(pl.multiple_of(offset + i * step, step), step)
         rays[:, pl.ds(pl.multiple_of(i * step, step), step)] = dot_nn(volume[...], flipped[:, where])
+
+
+def added(one, two, before, total):
+    total[...] = one[...] + two[...]
+
+
+def scaled(total, target, inverse, before, residue):
+    residue[...] = ((target[...] - total[...]) * inverse[...]).astype(BF16)
 
 
 def spread_first(place, residue, matrix, spread):
@@ -215,15 +228,18 @@
             shaped((1, half)),
         ),
         (
-            place, hbm(system_values[0], pltpu.HBM), block_pattern[0], subset_order,
+            place, hbm(system_values[0], pltpu.HBM), hbm(block_pattern[0], pltpu.HBM),
+            subset_order,
             hbm(start_volume, pltpu.HBM),
         ),
-        [SM, HB, SM, VM, HB],
+        [SM, HB, HB, VM, HB],
         work,
         "load",
         scratch=[
             pltpu.VMEM((fronts, slices, voxels), BF16),
+            pltpu.SMEM(block_pattern.shape[1:], jnp.int32),
             pltpu.SemaphoreType.DMA((loads,)),
+            pltpu.SemaphoreType.DMA,
             pltpu.SemaphoreType.DMA,
         ],
         vmem=10 << 20,
@@ -237,9 +253,9 @@
     targets = jnp.where(second == 0, measured[0][:, :, :half], measured[0][:, :, half:])
     these = [slice(n * batch, (n + 1) * batch) for n in range(BATCHES)]
     now = [volume[n] for n in range(BATCHES)]
-    narrow = [all_rows[n] for n in range(BATCHES)]
-    column = [jnp.zeros((1, voxels), F32)] * BATCHES
-    inverse_row = [None] * BATCHES
+    narrow = [all_rows[n] if n == 0 else all_rows[n, :batch] for n in range(BATCHES)]
+    column = jnp.zeros((1, voxels), F32)
+    inverse_row = None
     token = None
     for j in range(passes):
         totals = []
@@ -258,21 +274,44 @@
             got = swapped((sent * RAY_SCALE).astype(F16), "tile", 1)
             totals.append(held * RAY_SCALE + got.astype(F32))
             token = totals[n].astype(F16)
-        bit = 2
-        while bit < tiles:
-            got = [swapped(t.astype(F16), "tile", bit) for t in totals]
+        if j == 0:
             for n in range(BATCHES):
-                totals[n] = totals[n] + after(got[n], token).astype(F32)
+                bit = 2
+                while bit < tiles:
+                    got = swapped(totals[n].astype(F16), "tile", bit).astype(F32)
+                    if n > 0 and bit == 2:
+                        totals[n] = call(
+                            added, shaped(got.shape), (totals[n], got, totals[n - 1]),
+                            [VM, VM, AN], 1, "added",
+                        )
+                    else:
+                        totals[n] = totals[n] + got
+                    bit *= 2
+            token = totals[-1].astype(F16)
+        else:
+            got = [
+                [swapped(t.astype(F16), "tile", bits) for bits in range(2, tiles, 2)]
+                for t in totals
+            ]
+            for n in range(BATCHES):
+                for part in got[n]:
+                    totals[n] = totals[n] + part.astype(F32)
                 token = totals[n].astype(F16)
-            bit *= 2
         for n in range(BATCHES):
             total = totals[n] if n == 0 else after(totals[n], token)
-            if j == 0:
-                inverse_row[n] = 1.0 / total[batch : batch + 1]
+            sums = j == 0 and n == 0
+            if sums:
+                inverse_row = 1.0 / total[batch : batch + 1]
                 total = total[:batch]
             target = pick(turn[these[n]], j, targets[:, these[n]].astype(F32)) * RAY_SCALE
-            residue = ((target - total) * inverse_row[n]).astype(BF16)
-            if j == 0:
+            if n > 0 and j + 1 == passes:
+                residue = call(
+                    scaled, shaped((batch, half), BF16), (total, target, inverse_row, got[0]),
+                    [VM, VM, VM, AN], 1, "scaled",
+                )
+            else:
+                residue = ((target - total) * inverse_row).astype(BF16)
+            if sums:
                 residue = jnp.concatenate([residue, jnp.ones((EXTRA, half), BF16)])
             height = residue.shape[0]
             their_residue = swapped(residue, "tile", 1)
@@ -281,16 +320,16 @@
                 [SM, VM, VM], "spread_first",
             )
             shapes = [shaped((batch, voxels))]
-            if j == 0:
+            if sums:
                 shapes.append(shaped((1, voxels)))
             got = products(
-                functools.partial(spread_last, j == 0), tuple(shapes),
-                (other, their_residue, spread, now[n], column[n], matrix),
+                functools.partial(spread_last, sums), tuple(shapes),
+                (other, their_residue, spread, now[n], column, matrix),
                 [SM, VM, VM, VM, VM, VM], "spread_last",
             )
             now[n] = got[0]
-            if j == 0:
-                column[n] = got[1]
+            if sums:
+                column = got[1]
             token = now[n].astype(F16)
             if j + 1 < passes:
                 now[n] = passed(token, "subset", 1)

time: 158 us -> 154 us (0.975)
  waiting for transfers between devices: 41.3 us -> 26.5 us
  starting transfers between devices: 45.1 us -> 56.1 us
    ppermute x40 -> x46, starting transfers between devices: 35.1 us -> 46.7 us  [swapped(): return lax.ppermute(x, axis, [(i, i ^ bit) for i in range(size)])]
    ppermute x6, waiting for transfers between devices: 11.5 us -> 2.73 us  [passed(): lax.ppermute(x, axis, [(i, (i + distance) % size) for i in range(size)])]
    ppermute x40 -> x46, waiting for transfers between devices: 29.8 us -> 23.7 us  [swapped(): return lax.ppermute(x, axis, [(i, i ^ bit) for i in range(size)])]
    pallas_call x33 -> x35, Pallas kernels: 62.3 us -> 62.4 us  [call(): pl.pallas_call(kernel, out_shape=out_shape, in_specs=specs, out_specs=out...]
  transfers between devices with their start and end apart: 46 -> 52, of which waited for: 19 -> 17; matrix products, arithmetic and copies ran while one was open for 3% -> 3% of each run, Pallas kernels for 31% -> 32%
where the time goes in v1:
time: 154 us; the launch traced here: 153 us
  Pallas kernels  62.4 us (41%)
  starting transfers between devices  56.1 us (36%)
  waiting for transfers between devices  26.5 us (17%)
  other arithmetic  6.26 us (4%)
    pallas_call x35, Pallas kernels, call(): pl.pallas_call(kernel, out_shape=out_shape, in_specs=specs, out_specs=out...  62.4 us
    ppermute x46, starting transfers between devices, swapped(): return lax.ppermute(x, axis, [(i, i ^ bit) for i in range(size)])  46.7 us
    ppermute x46, waiting for transfers between devices, swapped(): return lax.ppermute(x, axis, [(i, i ^ bit) for i in range(size)])  23.7 us
    ppermute x6, starting transfers between devices, passed(): lax.ppermute(x, axis, [(i, (i + distance) % size) for i in range(size)])  9.4 us
  transfers between devices with their start and end apart: 52, of which 17 were waited for; matrix products, arithmetic and copies ran while one was open for 3% of the time, Pallas kernels for 32%

profile of v1, /device:TPU:0, one launch (start us, length us, event | category | flops | bytes accessed | tf_op | source)
XLA Modules:
  0.0 153.4 jit_solution(9146610755024087680)
XLA Ops:
  0.8 10.7 %load.1 = (bf16[2048,4096]{1,0:T(8,128)(2,1)S(1)}, bf16[4096,2048]{1,0:T(8,128)(2,1)S(1)}, bf16[2,48,4096]{2,1,0:T(8,128)(2,1)S(1)}, f32[2,32,4096]{2,1,0:T(8,12...) custom-call(s32[3]{0:T(128)S(1)} %pad_add_fusion.place, bf16[2048,4096]{1,0:T(8,128)(2,1)} %bitcast.121, ...), custom_call_target="tpu_custom_call" | custom-call | flops 17179869184 | tf_op jit(solution)/shard_map/load/pallas_call | solution.py:24
  19.1 3.1 %collective-permute-start.1 = (f16[48,1024]{1,0:T(8,128)(2,1)S(1)}, f16[48,1024]{1,0:T(8,128)(2,1)S(1)}, u32[]{:S(2)}, u32[]{:S(2)}) collective-permute-start(f16[48,1024]{1,0:T(8,128)(2,1)S(1)} %fusion.9), channel_id=1, source_target_pairs={{0,2},{1,3},{2,0},{3,1},{4,6},{5,7},{6,4},{7,5},{8,10},{9,11},{10,... | collective-permute-start | bytes 294920 | tf_op jit(solution)/shard_map/ppermute | solution.py:175
  22.3 3.3 %collective-permute-done.1 = f16[48,1024]{1,0:T(8,128)(2,1)S(1)} collective-permute-done((f16[48,1024]{1,0:T(8,128)(2,1)S(1)}, f16[48,1024]{1,0:T(8,128)(2,1)S(1)}, u32[]{:S(2)}, u32[]{:S(2)}) %collective-permute-start.1) | collective-permute-done | bytes 98336 | tf_op jit(solution)/shard_map/ppermute | solution.py:175
  25.7 3.0 %collective-permute-start.2 = (f16[48,1024]{1,0:T(8,128)(2,1)S(1)}, f16[48,1024]{1,0:T(8,128)(2,1)S(1)}, u32[]{:S(2)}, u32[]{:S(2)}) collective-permute-start(f16[48,1024]{1,0:T(8,128)(2,1)S(1)} %fusion), channel_id=1, source_target_pairs={{0,4},{1,5},{2,6},{3,7},{4,0},{5,1},{6,2},{7,3},{8,12},{9,13},{10,... | collective-permute-start | bytes 294920 | tf_op jit(solution)/shard_map/ppermute | solution.py:175
  31.4 3.1 %collective-permute-start.7 = (f16[32,1024]{1,0:T(8,128)(2,1)S(1)}, f16[32,1024]{1,0:T(8,128)(2,1)S(1)}, u32[]{:S(2)}, u32[]{:S(2)}) collective-permute-start(f16[32,1024]{1,0:T(8,128)(2,1)S(1)} %convert_element_type.267), channel_id=1, source_target_pairs={{0,4},{1,5},{2,6},{3,7},{4,0},{5,1},{6,2},{7,3},{8,12},{9,13},{10,... | collective-permute-start | bytes 196616 | tf_op jit(solution)/shard_map/ppermute | solution.py:175
  34.7 1.7 %spread_first.8.so_far = f32[48,4096]{1,0:T(8,128)S(1)} custom-call(s32[1]{0:T(128)} %bitcast.1.place, bf16[48,1024]{1,0:T(8,128)(2,1)S(1)} %concatenate.12.residue, bf16[2048,4096]{1,0:T(8,128)(2,1)S(1)} %get-tuple-element.34.matrix), custom_call_target="tpu_custom_call" | custom-call | flops 8589934592 | tf_op jit(solution)/shard_map/spread_first/pallas_call | solution.py:24
  36.8 1.8 %spread_last.8 = (f32[32,4096]{1,0:T(8,128)S(1)}, f32[1,4096]{1,0:T(1,128)S(1)}) custom-call(s32[1]{0:T(128)} %bitcast.2.place, bf16[48,1024]{1,0:T(8,128)(2,1)S(1)} %collective-permute-done.3.residue, f32[48,4096]{1,0:T(8,128)S(1)} %spread_first.8.so_far, f32[32,4096]{1,0:T(8,128)S(1)} %get-tuple-element.106.volume, ...), custom_call_target="tpu_custom_call" | custom-call | flops 8589934592 | tf_op jit(solution)/shard_map/spread_last/pallas_call | solution.py:24
  38.6 2.8 %collective-permute-start.4 = (f16[32,4096]{1,0:T(8,128)(2,1)S(1)}, f16[32,4096]{1,0:T(8,128)(2,1)S(1)}, u32[]{:S(2)}, u32[]{:S(2)}) collective-permute-start(f16[32,4096]{1,0:T(8,128)(2,1)S(1)} %convert_element_type.261), channel_id=1, source_target_pairs={{0,8},{8,16},{16,24},{24,0},{1,9},{9,17},{17,25},{25,1},{2,10},{10... | collective-permute-start | bytes 786440 | tf_op jit(solution)/shard_map/ppermute | solution.py:170
  43.3 1.7 %spread_last.9 = f32[32,4096]{1,0:T(8,128)S(1)} custom-call(s32[1]{0:T(128)} %bitcast.2.place, bf16[32,1024]{1,0:T(8,128)(2,1)S(1)} %collective-permute-done.8.residue, f32[32,4096]{1,0:T(8,128)S(1)} %spread_first.9.so_far, f32[32,4096]{1,0:T(8,128)S(1)} %get-tuple-element.105.volume, f32[1,4096]{1,0:T(1,128)S(1)} %get-tuple-element.38.column, ...), custom_call_target="tpu_custom_call" | custom-call | flops 8589934592 | tf_op jit(solution)/shard_map/spread_last/pallas_call | solution.py:24
  45.0 1.7 %collective-permute-start.15 = (f16[32,4096]{1,0:T(8,128)(2,1)S(1)}, f16[32,4096]{1,0:T(8,128)(2,1)S(1)}, u32[]{:S(2)}, u32[]{:S(2)}) collective-permute-start(f16[32,4096]{1,0:T(8,128)(2,1)S(1)} %convert_element_type.270), channel_id=1, source_target_pairs={{0,8},{8,16},{16,24},{24,0},{1,9},{9,17},{17,25},{25,1},{2,10},{10... | collective-permute-start | bytes 786440 | tf_op jit(solution)/shard_map/ppermute | solution.py:170
  51.4 4.4 %collective-permute-start.12 = (f16[32,1024]{1,0:T(8,128)(2,1)S(1)}, f16[32,1024]{1,0:T(8,128)(2,1)S(1)}, u32[]{:S(2)}, u32[]{:S(2)}) collective-permute-start(f16[32,1024]{1,0:T(8,128)(2,1)S(1)} %fusion.3), channel_id=1, source_target_pairs={{0,6},{1,7},{2,4},{3,5},{4,2},{5,3},{6,0},{7,1},{8,14},{9,15},{10,... | collective-permute-start | bytes 196616 | tf_op jit(solution)/shard_map/ppermute | solution.py:175
  59.7 2.5 %collective-permute-done.11 = f16[32,1024]{1,0:T(8,128)(2,1)S(1)} collective-permute-done((f16[32,1024]{1,0:T(8,128)(2,1)S(1)}, f16[32,1024]{1,0:T(8,128)(2,1)S(1)}, u32[]{:S(2)}, u32[]{:S(2)}) %collective-permute-start.11) | collective-permute-done | bytes 65568 | tf_op jit(solution)/shard_map/ppermute | solution.py:175
  64.2 1.7 %collective-permute-start.19 = (f16[32,1024]{1,0:T(8,128)(2,1)S(1)}, f16[32,1024]{1,0:T(8,128)(2,1)S(1)}, u32[]{:S(2)}, u32[]{:S(2)}) collective-permute-start(f16[32,1024]{1,0:T(8,128)(2,1)S(1)} %fusion.4), channel_id=1, source_target_pairs={{0,6},{1,7},{2,4},{3,5},{4,2},{5,3},{6,0},{7,1},{8,14},{9,15},{10,... | collective-permute-start | bytes 196616 | tf_op jit(solution)/shard_map/ppermute | solution.py:175
  66.0 2.6 %collective-permute-start.17 = (f16[32,1024]{1,0:T(8,128)(2,1)S(1)}, f16[32,1024]{1,0:T(8,128)(2,1)S(1)}, u32[]{:S(2)}, u32[]{:S(2)}) collective-permute-start(f16[32,1024]{1,0:T(8,128)(2,1)S(1)} %fusion.4), channel_id=1, source_target_pairs={{0,2},{1,3},{2,0},{3,1},{4,6},{5,7},{6,4},{7,5},{8,10},{9,11},{10,... | collective-permute-start | bytes 196616 | tf_op jit(solution)/shard_map/ppermute | solution.py:175
  68.6 1.7 %spread_last.10 = f32[32,4096]{1,0:T(8,128)S(1)} custom-call(s32[1]{0:T(128)} %bitcast.2.place, bf16[32,1024]{1,0:T(8,128)(2,1)S(1)} %collective-permute-done.13.residue, f32[32,4096]{1,0:T(8,128)S(1)} %spread_first.10.so_far, f32[32,4096]{1,0:T(8,128)S(1)} %get-tuple-element.121.volume, f32[1,4096]{1,0:T(1,128)S(1)} %get-tuple-element.38.column, ...), custom_call_target="tpu_custom_call" | custom-call | flops 8589934592 | tf_op jit(solution)/shard_map/spread_last/pallas_call | solution.py:24
  71.4 1.9 %collective-permute-done.18 = f16[32,1024]{1,0:T(8,128)(2,1)S(1)} collective-permute-done((f16[32,1024]{1,0:T(8,128)(2,1)S(1)}, f16[32,1024]{1,0:T(8,128)(2,1)S(1)}, u32[]{:S(2)}, u32[]{:S(2)}) %collective-permute-start.18) | collective-permute-done | bytes 65568 | tf_op jit(solution)/shard_map/ppermute | solution.py:175
  75.2 1.7 %spread_last.11 = f32[32,4096]{1,0:T(8,128)S(1)} custom-call(s32[1]{0:T(128)} %bitcast.2.place, bf16[32,1024]{1,0:T(8,128)(2,1)S(1)} %collective-permute-done.20.residue, f32[32,4096]{1,0:T(8,128)S(1)} %spread_first.11.so_far, f32[32,4096]{1,0:T(8,128)S(1)} %get-tuple-element.119.volume, f32[1,4096]{1,0:T(1,128)S(1)} %get-tuple-element.38.column, ...), custom_call_target="tpu_custom_call" | custom-call | flops 8589934592 | tf_op jit(solution)/shard_map/spread_last/pallas_call | solution.py:24
  82.5 1.7 %collective-permute-start.24 = (f16[32,1024]{1,0:T(8,128)(2,1)S(1)}, f16[32,1024]{1,0:T(8,128)(2,1)S(1)}, u32[]{:S(2)}, u32[]{:S(2)}) collective-permute-start(f16[32,1024]{1,0:T(8,128)(2,1)S(1)} %fusion.5), channel_id=1, source_target_pairs={{0,6},{1,7},{2,4},{3,5},{4,2},{5,3},{6,0},{7,1},{8,14},{9,15},{10,... | collective-permute-start | bytes 196616 | tf_op jit(solution)/shard_map/ppermute | solution.py:175
  84.3 2.6 %collective-permute-start.22 = (f16[32,1024]{1,0:T(8,128)(2,1)S(1)}, f16[32,1024]{1,0:T(8,128)(2,1)S(1)}, u32[]{:S(2)}, u32[]{:S(2)}) collective-permute-start(f16[32,1024]{1,0:T(8,128)(2,1)S(1)} %fusion.5), channel_id=1, source_target_pairs={{0,2},{1,3},{2,0},{3,1},{4,6},{5,7},{6,4},{7,5},{8,10},{9,11},{10,... | collective-permute-start | bytes 196616 | tf_op jit(solution)/shard_map/ppermute | solution.py:175
  93.6 1.7 %collective-permute-start.31 = (f16[32,1024]{1,0:T(8,128)(2,1)S(1)}, f16[32,1024]{1,0:T(8,128)(2,1)S(1)}, u32[]{:S(2)}, u32[]{:S(2)}) collective-permute-start(f16[32,1024]{1,0:T(8,128)(2,1)S(1)} %fusion.6), channel_id=1, source_target_pairs={{0,6},{1,7},{2,4},{3,5},{4,2},{5,3},{6,0},{7,1},{8,14},{9,15},{10,... | collective-permute-start | bytes 196616 | tf_op jit(solution)/shard_map/ppermute | solution.py:175
  95.3 2.7 %collective-permute-start.29 = (f16[32,1024]{1,0:T(8,128)(2,1)S(1)}, f16[32,1024]{1,0:T(8,128)(2,1)S(1)}, u32[]{:S(2)}, u32[]{:S(2)}) collective-permute-start(f16[32,1024]{1,0:T(8,128)(2,1)S(1)} %fusion.6), channel_id=1, source_target_pairs={{0,2},{1,3},{2,0},{3,1},{4,6},{5,7},{6,4},{7,5},{8,10},{9,11},{10,... | collective-permute-start | bytes 196616 | tf_op jit(solution)/shard_map/ppermute | solution.py:175
  98.1 1.7 %spread_last.12 = f32[32,4096]{1,0:T(8,128)S(1)} custom-call(s32[1]{0:T(128)} %bitcast.2.place, bf16[32,1024]{1,0:T(8,128)(2,1)S(1)} %collective-permute-done.25.residue, f32[32,4096]{1,0:T(8,128)S(1)} %spread_first.12.so_far, f32[32,4096]{1,0:T(8,128)S(1)} %get-tuple-element.117.volume, f32[1,4096]{1,0:T(1,128)S(1)} %get-tuple-element.38.column, ...), custom_call_target="tpu_custom_call" | custom-call | flops 8589934592 | tf_op jit(solution)/shard_map/spread_last/pallas_call | solution.py:24
  100.9 1.8 %collective-permute-done.30 = f16[32,1024]{1,0:T(8,128)(2,1)S(1)} collective-permute-done((f16[32,1024]{1,0:T(8,128)(2,1)S(1)}, f16[32,1024]{1,0:T(8,128)(2,1)S(1)}, u32[]{:S(2)}, u32[]{:S(2)}) %collective-permute-start.30) | collective-permute-done | bytes 65568 | tf_op jit(solution)/shard_map/ppermute | solution.py:175
  104.7 1.7 %spread_last.13 = f32[32,4096]{1,0:T(8,128)S(1)} custom-call(s32[1]{0:T(128)} %bitcast.2.place, bf16[32,1024]{1,0:T(8,128)(2,1)S(1)} %collective-permute-done.32.residue, f32[32,4096]{1,0:T(8,128)S(1)} %spread_first.13.so_far, f32[32,4096]{1,0:T(8,128)S(1)} %get-tuple-element.115.volume, f32[1,4096]{1,0:T(1,128)S(1)} %get-tuple-element.38.column, ...), custom_call_target="tpu_custom_call" | custom-call | flops 8589934592 | tf_op jit(solution)/shard_map/spread_last/pallas_call | solution.py:24
  111.9 1.7 %collective-permute-start.36 = (f16[32,1024]{1,0:T(8,128)(2,1)S(1)}, f16[32,1024]{1,0:T(8,128)(2,1)S(1)}, u32[]{:S(2)}, u32[]{:S(2)}) collective-permute-start(f16[32,1024]{1,0:T(8,128)(2,1)S(1)} %fusion.7), channel_id=1, source_target_pairs={{0,6},{1,7},{2,4},{3,5},{4,2},{5,3},{6,0},{7,1},{8,14},{9,15},{10,... | collective-permute-start | bytes 196616 | tf_op jit(solution)/shard_map/ppermute | solution.py:175
  113.7 2.6 %collective-permute-start.34 = (f16[32,1024]{1,0:T(8,128)(2,1)S(1)}, f16[32,1024]{1,0:T(8,128)(2,1)S(1)}, u32[]{:S(2)}, u32[]{:S(2)}) collective-permute-start(f16[32,1024]{1,0:T(8,128)(2,1)S(1)} %fusion.7), channel_id=1, source_target_pairs={{0,2},{1,3},{2,0},{3,1},{4,6},{5,7},{6,4},{7,5},{8,10},{9,11},{10,... | collective-permute-start | bytes 196616 | tf_op jit(solution)/shard_map/ppermute | solution.py:175
  123.0 1.7 %collective-permute-start.46 = (f16[32,1024]{1,0:T(8,128)(2,1)S(1)}, f16[32,1024]{1,0:T(8,128)(2,1)S(1)}, u32[]{:S(2)}, u32[]{:S(2)}) collective-permute-start(f16[32,1024]{1,0:T(8,128)(2,1)S(1)} %fusion.8), channel_id=1, source_target_pairs={{0,6},{1,7},{2,4},{3,5},{4,2},{5,3},{6,0},{7,1},{8,14},{9,15},{10,... | collective-permute-start | bytes 196616 | tf_op jit(solution)/shard_map/ppermute | solution.py:175
  124.7 2.7 %collective-permute-start.44 = (f16[32,1024]{1,0:T(8,128)(2,1)S(1)}, f16[32,1024]{1,0:T(8,128)(2,1)S(1)}, u32[]{:S(2)}, u32[]{:S(2)}) collective-permute-start(f16[32,1024]{1,0:T(8,128)(2,1)S(1)} %fusion.8), channel_id=1, source_target_pairs={{0,2},{1,3},{2,0},{3,1},{4,6},{5,7},{6,4},{7,5},{8,10},{9,11},{10,... | collective-permute-start | bytes 196616 | tf_op jit(solution)/shard_map/ppermute | solution.py:175
  127.5 1.7 %spread_last.14.before = f32[32,4096]{1,0:T(8,128)S(1)} custom-call(s32[1]{0:T(128)} %bitcast.2.place, bf16[32,1024]{1,0:T(8,128)(2,1)S(1)} %collective-permute-done.37.residue, f32[32,4096]{1,0:T(8,128)S(1)} %spread_first.14.so_far, f32[32,4096]{1,0:T(8,128)S(1)} %get-tuple-element.113.volume, f32[1,4096]{1,0:T(1,128)S(1)} %get-tuple-element.38.column, ...), custom_call_target="tpu_custom_call" | custom-call | flops 8589934592 | tf_op jit(solution)/shard_map/spread_last/pallas_call | solution.py:24
  134.0 1.7 %spread_last.15 = f32[32,4096]{1,0:T(8,128)S(1)} custom-call(s32[1]{0:T(128)} %bitcast.2.place, bf16[32,1024]{1,0:T(8,128)(2,1)S(1)} %collective-permute-done.47.residue, f32[32,4096]{1,0:T(8,128)S(1)} %spread_first.15.so_far, f32[32,4096]{1,0:T(8,128)S(1)} %get-tuple-element.111.volume, f32[1,4096]{1,0:T(1,128)S(1)} %get-tuple-element.38.column, ...), custom_call_target="tpu_custom_call" | custom-call | flops 8589934592 | tf_op jit(solution)/shard_map/spread_last/pallas_call | solution.py:24
  141.1 3.8 %collective-permute-done.50 = bf16[32,4096]{1,0:T(8,128)(2,1)S(1)} collective-permute-done((bf16[32,4096]{1,0:T(8,128)(2,1)S(1)}, bf16[32,4096]{1,0:T(8,128)(2,1)S(1)}, u32[]{:S(2)}, u32[]{:S(2)}) %collective-permute-start.50) | collective-permute-done | bytes 262176 | tf_op jit(solution)/shard_map/ppermute | solution.py:175
  149.3 2.2 %collective-permute-done.49 = bf16[32,2048]{1,0:T(8,128)(2,1)S(1)} collective-permute-done((bf16[32,2048]{1,0:T(8,128)(2,1)S(1)}, bf16[32,2048]{1,0:T(8,128)(2,1)S(1)}, u32[]{:S(2)}, u32[]{:S(2)}) %collective-permute-start.49) | collective-permute-done | bytes 131104 | tf_op jit(solution)/shard_map/ppermute | solution.py:175
  (207 shorter events, 71.1 us)
Async XLA Ops:
  13.2 9.1 %collective-permute-start.5 = (f16[32,1024]{1,0:T(8,128)(2,1)S(1)}, f16[32,1024]{1,0:T(8,128)(2,1)S(1)}, u32[]{:S(2)}, u32[]{:S(2)}) collective-permute-start(f16[32,1024]{1,0:T(8,128)(2,1)S(1)} %multiply_convert_fusion.13), channel_id=1, source_target_pairs={{0,1},{1,0},{2,3},{3,2},{4,5},{5,4},{6,7},{7,6},{8,9},{9,8},{10,11... | collective-permute-start | bytes 196616 | tf_op jit(solution)/shard_map/ppermute | solution.py:175
  22.3 7.6 %collective-permute-start.6 = (f16[32,1024]{1,0:T(8,128)(2,1)S(1)}, f16[32,1024]{1,0:T(8,128)(2,1)S(1)}, u32[]{:S(2)}, u32[]{:S(2)}) collective-permute-start(f16[32,1024]{1,0:T(8,128)(2,1)S(1)} %get-tuple-element.95), channel_id=1, source_target_pairs={{0,2},{1,3},{2,0},{3,1},{4,6},{5,7},{6,4},{7,5},{8,10},{9,11},{10,... | collective-permute-start | bytes 196616 | tf_op jit(solution)/shard_map/ppermute | solution.py:175
  38.6 9.3 %collective-permute-start.4 = (f16[32,4096]{1,0:T(8,128)(2,1)S(1)}, f16[32,4096]{1,0:T(8,128)(2,1)S(1)}, u32[]{:S(2)}, u32[]{:S(2)}) collective-permute-start(f16[32,4096]{1,0:T(8,128)(2,1)S(1)} %convert_element_type.261), channel_id=1, source_target_pairs={{0,8},{8,16},{16,24},{24,0},{1,9},{9,17},{17,25},{25,1},{2,10},{10... | collective-permute-start | bytes 786440 | tf_op jit(solution)/shard_map/ppermute | solution.py:170
  45.0 11.4 %collective-permute-start.15 = (f16[32,4096]{1,0:T(8,128)(2,1)S(1)}, f16[32,4096]{1,0:T(8,128)(2,1)S(1)}, u32[]{:S(2)}, u32[]{:S(2)}) collective-permute-start(f16[32,4096]{1,0:T(8,128)(2,1)S(1)} %convert_element_type.270), channel_id=1, source_target_pairs={{0,8},{8,16},{16,24},{24,0},{1,9},{9,17},{17,25},{25,1},{2,10},{10... | collective-permute-start | bytes 786440 | tf_op jit(solution)/shard_map/ppermute | solution.py:170
  51.4 8.3 %collective-permute-start.12 = (f16[32,1024]{1,0:T(8,128)(2,1)S(1)}, f16[32,1024]{1,0:T(8,128)(2,1)S(1)}, u32[]{:S(2)}, u32[]{:S(2)}) collective-permute-start(f16[32,1024]{1,0:T(8,128)(2,1)S(1)} %fusion.3), channel_id=1, source_target_pairs={{0,6},{1,7},{2,4},{3,5},{4,2},{5,3},{6,0},{7,1},{8,14},{9,15},{10,... | collective-permute-start | bytes 196616 | tf_op jit(solution)/shard_map/ppermute | solution.py:175
  55.7 6.5 %collective-permute-start.11 = (f16[32,1024]{1,0:T(8,128)(2,1)S(1)}, f16[32,1024]{1,0:T(8,128)(2,1)S(1)}, u32[]{:S(2)}, u32[]{:S(2)}) collective-permute-start(f16[32,1024]{1,0:T(8,128)(2,1)S(1)} %fusion.3), channel_id=1, source_target_pairs={{0,4},{1,5},{2,6},{3,7},{4,0},{5,1},{6,2},{7,3},{8,12},{9,13},{10,... | collective-permute-start | bytes 196616 | tf_op jit(solution)/shard_map/ppermute | solution.py:175
  64.2 7.2 %collective-permute-start.19 = (f16[32,1024]{1,0:T(8,128)(2,1)S(1)}, f16[32,1024]{1,0:T(8,128)(2,1)S(1)}, u32[]{:S(2)}, u32[]{:S(2)}) collective-permute-start(f16[32,1024]{1,0:T(8,128)(2,1)S(1)} %fusion.4), channel_id=1, source_target_pairs={{0,6},{1,7},{2,4},{3,5},{4,2},{5,3},{6,0},{7,1},{8,14},{9,15},{10,... | collective-permute-start | bytes 196616 | tf_op jit(solution)/shard_map/ppermute | solution.py:175
  65.9 7.4 %collective-permute-start.18 = (f16[32,1024]{1,0:T(8,128)(2,1)S(1)}, f16[32,1024]{1,0:T(8,128)(2,1)S(1)}, u32[]{:S(2)}, u32[]{:S(2)}) collective-permute-start(f16[32,1024]{1,0:T(8,128)(2,1)S(1)} %fusion.4), channel_id=1, source_target_pairs={{0,4},{1,5},{2,6},{3,7},{4,0},{5,1},{6,2},{7,3},{8,12},{9,13},{10,... | collective-permute-start | bytes 196616 | tf_op jit(solution)/shard_map/ppermute | solution.py:175
  66.0 7.3 %collective-permute-start.17 = (f16[32,1024]{1,0:T(8,128)(2,1)S(1)}, f16[32,1024]{1,0:T(8,128)(2,1)S(1)}, u32[]{:S(2)}, u32[]{:S(2)}) collective-permute-start(f16[32,1024]{1,0:T(8,128)(2,1)S(1)} %fusion.4), channel_id=1, source_target_pairs={{0,2},{1,3},{2,0},{3,1},{4,6},{5,7},{6,4},{7,5},{8,10},{9,11},{10,... | collective-permute-start | bytes 196616 | tf_op jit(solution)/shard_map/ppermute | solution.py:175
  70.4 8.8 %collective-permute-start.14 = (f16[32,4096]{1,0:T(8,128)(2,1)S(1)}, f16[32,4096]{1,0:T(8,128)(2,1)S(1)}, u32[]{:S(2)}, u32[]{:S(2)}) collective-permute-start(f16[32,4096]{1,0:T(8,128)(2,1)S(1)} %convert_element_type.280), channel_id=1, source_target_pairs={{0,8},{8,16},{16,24},{24,0},{1,9},{9,17},{17,25},{25,1},{2,10},{10... | collective-permute-start | bytes 786440 | tf_op jit(solution)/shard_map/ppermute | solution.py:170
  77.0 10.0 %collective-permute-start.27 = (f16[32,4096]{1,0:T(8,128)(2,1)S(1)}, f16[32,4096]{1,0:T(8,128)(2,1)S(1)}, u32[]{:S(2)}, u32[]{:S(2)}) collective-permute-start(f16[32,4096]{1,0:T(8,128)(2,1)S(1)} %convert_element_type.290), channel_id=1, source_target_pairs={{0,8},{8,16},{16,24},{24,0},{1,9},{9,17},{17,25},{25,1},{2,10},{10... | collective-permute-start | bytes 786440 | tf_op jit(solution)/shard_map/ppermute | solution.py:170
  82.5 7.8 %collective-permute-start.24 = (f16[32,1024]{1,0:T(8,128)(2,1)S(1)}, f16[32,1024]{1,0:T(8,128)(2,1)S(1)}, u32[]{:S(2)}, u32[]{:S(2)}) collective-permute-start(f16[32,1024]{1,0:T(8,128)(2,1)S(1)} %fusion.5), channel_id=1, source_target_pairs={{0,6},{1,7},{2,4},{3,5},{4,2},{5,3},{6,0},{7,1},{8,14},{9,15},{10,... | collective-permute-start | bytes 196616 | tf_op jit(solution)/shard_map/ppermute | solution.py:175
  84.2 7.5 %collective-permute-start.23 = (f16[32,1024]{1,0:T(8,128)(2,1)S(1)}, f16[32,1024]{1,0:T(8,128)(2,1)S(1)}, u32[]{:S(2)}, u32[]{:S(2)}) collective-permute-start(f16[32,1024]{1,0:T(8,128)(2,1)S(1)} %fusion.5), channel_id=1, source_target_pairs={{0,4},{1,5},{2,6},{3,7},{4,0},{5,1},{6,2},{7,3},{8,12},{9,13},{10,... | collective-permute-start | bytes 196616 | tf_op jit(solution)/shard_map/ppermute | solution.py:175
  84.3 7.4 %collective-permute-start.22 = (f16[32,1024]{1,0:T(8,128)(2,1)S(1)}, f16[32,1024]{1,0:T(8,128)(2,1)S(1)}, u32[]{:S(2)}, u32[]{:S(2)}) collective-permute-start(f16[32,1024]{1,0:T(8,128)(2,1)S(1)} %fusion.5), channel_id=1, source_target_pairs={{0,2},{1,3},{2,0},{3,1},{4,6},{5,7},{6,4},{7,5},{8,10},{9,11},{10,... | collective-permute-start | bytes 196616 | tf_op jit(solution)/shard_map/ppermute | solution.py:175
  93.6 7.4 %collective-permute-start.31 = (f16[32,1024]{1,0:T(8,128)(2,1)S(1)}, f16[32,1024]{1,0:T(8,128)(2,1)S(1)}, u32[]{:S(2)}, u32[]{:S(2)}) collective-permute-start(f16[32,1024]{1,0:T(8,128)(2,1)S(1)} %fusion.6), channel_id=1, source_target_pairs={{0,6},{1,7},{2,4},{3,5},{4,2},{5,3},{6,0},{7,1},{8,14},{9,15},{10,... | collective-permute-start | bytes 196616 | tf_op jit(solution)/shard_map/ppermute | solution.py:175
  95.3 7.4 %collective-permute-start.30 = (f16[32,1024]{1,0:T(8,128)(2,1)S(1)}, f16[32,1024]{1,0:T(8,128)(2,1)S(1)}, u32[]{:S(2)}, u32[]{:S(2)}) collective-permute-start(f16[32,1024]{1,0:T(8,128)(2,1)S(1)} %fusion.6), channel_id=1, source_target_pairs={{0,4},{1,5},{2,6},{3,7},{4,0},{5,1},{6,2},{7,3},{8,12},{9,13},{10,... | collective-permute-start | bytes 196616 | tf_op jit(solution)/shard_map/ppermute | solution.py:175
  95.3 7.4 %collective-permute-start.29 = (f16[32,1024]{1,0:T(8,128)(2,1)S(1)}, f16[32,1024]{1,0:T(8,128)(2,1)S(1)}, u32[]{:S(2)}, u32[]{:S(2)}) collective-permute-start(f16[32,1024]{1,0:T(8,128)(2,1)S(1)} %fusion.6), channel_id=1, source_target_pairs={{0,2},{1,3},{2,0},{3,1},{4,6},{5,7},{6,4},{7,5},{8,10},{9,11},{10,... | collective-permute-start | bytes 196616 | tf_op jit(solution)/shard_map/ppermute | solution.py:175
  99.8 8.8 %collective-permute-start.26 = (f16[32,4096]{1,0:T(8,128)(2,1)S(1)}, f16[32,4096]{1,0:T(8,128)(2,1)S(1)}, u32[]{:S(2)}, u32[]{:S(2)}) collective-permute-start(f16[32,4096]{1,0:T(8,128)(2,1)S(1)} %convert_element_type.300), channel_id=1, source_target_pairs={{0,8},{8,16},{16,24},{24,0},{1,9},{9,17},{17,25},{25,1},{2,10},{10... | collective-permute-start | bytes 786440 | tf_op jit(solution)/shard_map/ppermute | solution.py:170
  106.5 9.9 %collective-permute-start.42 = (f16[32,4096]{1,0:T(8,128)(2,1)S(1)}, f16[32,4096]{1,0:T(8,128)(2,1)S(1)}, u32[]{:S(2)}, u32[]{:S(2)}) collective-permute-start(f16[32,4096]{1,0:T(8,128)(2,1)S(1)} %convert_element_type.310), channel_id=1, source_target_pairs={{0,8},{8,16},{16,24},{24,0},{1,9},{9,17},{17,25},{25,1},{2,10},{10... | collective-permute-start | bytes 786440 | tf_op jit(solution)/shard_map/ppermute | solution.py:170
  111.9 7.8 %collective-permute-start.36 = (f16[32,1024]{1,0:T(8,128)(2,1)S(1)}, f16[32,1024]{1,0:T(8,128)(2,1)S(1)}, u32[]{:S(2)}, u32[]{:S(2)}) collective-permute-start(f16[32,1024]{1,0:T(8,128)(2,1)S(1)} %fusion.7), channel_id=1, source_target_pairs={{0,6},{1,7},{2,4},{3,5},{4,2},{5,3},{6,0},{7,1},{8,14},{9,15},{10,... | collective-permute-start | bytes 196616 | tf_op jit(solution)/shard_map/ppermute | solution.py:175
  113.6 7.5 %collective-permute-start.35 = (f16[32,1024]{1,0:T(8,128)(2,1)S(1)}, f16[32,1024]{1,0:T(8,128)(2,1)S(1)}, u32[]{:S(2)}, u32[]{:S(2)}) collective-permute-start(f16[32,1024]{1,0:T(8,128)(2,1)S(1)} %fusion.7), channel_id=1, source_target_pairs={{0,4},{1,5},{2,6},{3,7},{4,0},{5,1},{6,2},{7,3},{8,12},{9,13},{10,... | collective-permute-start | bytes 196616 | tf_op jit(solution)/shard_map/ppermute | solution.py:175
  113.7 7.3 %collective-permute-start.34 = (f16[32,1024]{1,0:T(8,128)(2,1)S(1)}, f16[32,1024]{1,0:T(8,128)(2,1)S(1)}, u32[]{:S(2)}, u32[]{:S(2)}) collective-permute-start(f16[32,1024]{1,0:T(8,128)(2,1)S(1)} %fusion.7), channel_id=1, source_target_pairs={{0,2},{1,3},{2,0},{3,1},{4,6},{5,7},{6,4},{7,5},{8,10},{9,11},{10,... | collective-permute-start | bytes 196616 | tf_op jit(solution)/shard_map/ppermute | solution.py:175
  123.0 7.9 %collective-permute-start.46 = (f16[32,1024]{1,0:T(8,128)(2,1)S(1)}, f16[32,1024]{1,0:T(8,128)(2,1)S(1)}, u32[]{:S(2)}, u32[]{:S(2)}) collective-permute-start(f16[32,1024]{1,0:T(8,128)(2,1)S(1)} %fusion.8), channel_id=1, source_target_pairs={{0,6},{1,7},{2,4},{3,5},{4,2},{5,3},{6,0},{7,1},{8,14},{9,15},{10,... | collective-permute-start | bytes 196616 | tf_op jit(solution)/shard_map/ppermute | solution.py:175
  124.7 7.4 %collective-permute-start.45 = (f16[32,1024]{1,0:T(8,128)(2,1)S(1)}, f16[32,1024]{1,0:T(8,128)(2,1)S(1)}, u32[]{:S(2)}, u32[]{:S(2)}) collective-permute-start(f16[32,1024]{1,0:T(8,128)(2,1)S(1)} %fusion.8), channel_id=1, source_target_pairs={{0,4},{1,5},{2,6},{3,7},{4,0},{5,1},{6,2},{7,3},{8,12},{9,13},{10,... | collective-permute-start | bytes 196616 | tf_op jit(solution)/shard_map/ppermute | solution.py:175
  124.7 7.4 %collective-permute-start.44 = (f16[32,1024]{1,0:T(8,128)(2,1)S(1)}, f16[32,1024]{1,0:T(8,128)(2,1)S(1)}, u32[]{:S(2)}, u32[]{:S(2)}) collective-permute-start(f16[32,1024]{1,0:T(8,128)(2,1)S(1)} %fusion.8), channel_id=1, source_target_pairs={{0,2},{1,3},{2,0},{3,1},{4,6},{5,7},{6,4},{7,5},{8,10},{9,11},{10,... | collective-permute-start | bytes 196616 | tf_op jit(solution)/shard_map/ppermute | solution.py:175
  129.2 10.8 %collective-permute-start.40 = (bf16[32,4096]{1,0:T(8,128)(2,1)S(1)}, bf16[32,4096]{1,0:T(8,128)(2,1)S(1)}, u32[]{:S(2)}, u32[]{:S(2)}) collective-permute-start(bf16[32,4096]{1,0:T(8,128)(2,1)S(1)} %convert_element_type.320), channel_id=1, source_target_pairs={{0,8},{8,0},{16,24},{24,16},{1,9},{9,1},{17,25},{25,17},{2,10},{10... | collective-permute-start | bytes 786440 | tf_op jit(solution)/shard_map/ppermute | solution.py:175
  130.4 7.6 %collective-permute-start.38 = (bf16[32,4096]{1,0:T(8,128)(2,1)S(1)}, bf16[32,4096]{1,0:T(8,128)(2,1)S(1)}, u32[]{:S(2)}, u32[]{:S(2)}) collective-permute-start(bf16[32,4096]{1,0:T(8,128)(2,1)S(1)} %convert_element_type.320), channel_id=1, source_target_pairs={{0,16},{8,24},{16,0},{24,8},{1,17},{9,25},{17,1},{25,9},{2,18},{10... | collective-permute-start | bytes 786440 | tf_op jit(solution)/shard_map/ppermute | solution.py:175
  135.7 9.2 %collective-permute-start.50 = (bf16[32,4096]{1,0:T(8,128)(2,1)S(1)}, bf16[32,4096]{1,0:T(8,128)(2,1)S(1)}, u32[]{:S(2)}, u32[]{:S(2)}) collective-permute-start(bf16[32,4096]{1,0:T(8,128)(2,1)S(1)} %convert_element_type.329), channel_id=1, source_target_pairs={{0,8},{8,0},{16,24},{24,16},{1,9},{9,1},{17,25},{25,17},{2,10},{10... | collective-permute-start | bytes 786440 | tf_op jit(solution)/shard_map/ppermute | solution.py:175
  137.0 9.5 %collective-permute-start.48 = (bf16[32,4096]{1,0:T(8,128)(2,1)S(1)}, bf16[32,4096]{1,0:T(8,128)(2,1)S(1)}, u32[]{:S(2)}, u32[]{:S(2)}) collective-permute-start(bf16[32,4096]{1,0:T(8,128)(2,1)S(1)} %convert_element_type.329), channel_id=1, source_target_pairs={{0,16},{8,24},{16,0},{24,8},{1,17},{9,25},{17,1},{25,9},{2,18},{10... | collective-permute-start | bytes 786440 | tf_op jit(solution)/shard_map/ppermute | solution.py:175
  138.0 9.3 %collective-permute-start.39 = (bf16[32,2048]{1,0:T(8,128)(2,1)S(1)}, bf16[32,2048]{1,0:T(8,128)(2,1)S(1)}, u32[]{:S(2)}, u32[]{:S(2)}) collective-permute-start(bf16[32,2048]{1,0:T(8,128)(2,1)S(1)} %slice.236), channel_id=1, source_target_pairs={{0,8},{8,0},{16,24},{24,16},{1,9},{9,1},{17,25},{25,17},{2,10},{10... | collective-permute-start | bytes 393224 | tf_op jit(solution)/shard_map/ppermute | solution.py:175
  140.0 8.9 %collective-permute-start.41 = (bf16[32,2048]{1,0:T(8,128)(2,1)S(1)}, bf16[32,2048]{1,0:T(8,128)(2,1)S(1)}, u32[]{:S(2)}, u32[]{:S(2)}) collective-permute-start(bf16[32,2048]{1,0:T(8,128)(2,1)S(1)} %slice.237), channel_id=1, source_target_pairs={{0,16},{8,24},{16,0},{24,8},{1,17},{9,25},{17,1},{25,9},{2,18},{10... | collective-permute-start | bytes 393224 | tf_op jit(solution)/shard_map/ppermute | solution.py:175
  144.9 6.7 %collective-permute-start.51 = (bf16[32,2048]{1,0:T(8,128)(2,1)S(1)}, bf16[32,2048]{1,0:T(8,128)(2,1)S(1)}, u32[]{:S(2)}, u32[]{:S(2)}) collective-permute-start(bf16[32,2048]{1,0:T(8,128)(2,1)S(1)} %slice.239), channel_id=1, source_target_pairs={{0,16},{8,24},{16,0},{24,8},{1,17},{9,25},{17,1},{25,9},{2,18},{10... | collective-permute-start | bytes 393224 | tf_op jit(solution)/shard_map/ppermute | solution.py:175
  (35 other events, 144.1 us)

commit v2 on v1

--- a/solution.py
+++ b/solution.py
@@ -11,7 +11,7 @@
 RAY_SCALE = 2.0**-14
 EXTRA = 16
 COST = 16
-AHEAD = 3
+AHEAD = 2
 BATCHES = 2
 VM = pl.BlockSpec(memory_space=pltpu.VMEM)
 SM = pl.BlockSpec(memory_space=pltpu.SMEM)
@@ -45,7 +45,7 @@
 
 def load_kernel(
     place, matrix_hbm, pattern_hbm, order, start_hbm, matrix, flipped, narrow, volume, turn, apart,
-    second, fronts, pattern, sems, start_sem, pattern_sem,
+    second, fronts, pattern, ends_in, sems, start_sem, pattern_sem, order_sem,
 ):
     ray_blocks, col_blocks = pattern.shape
     ray_count, voxels = matrix.shape
@@ -60,6 +60,8 @@
         where = pl.ds(pl.multiple_of(i * rows, rows), rows)
         return pltpu.make_async_copy(matrix_hbm.at[where], matrix.at[where], sems.at[i])
 
+    order_in = pltpu.make_async_copy(order, ends_in, order_sem)
+    order_in.start()
     blocks_in = pltpu.make_async_copy(pattern_hbm, pattern, pattern_sem)
     blocks_in.start()
     first = pltpu.make_async_copy(start_hbm, fronts, start_sem)
@@ -67,10 +69,12 @@
     for i in range(AHEAD):
         piece(i).start()
     second[...] = jnp.full(second.shape, core.astype(F32))
-    later = owner - order[...]
+    order_in.wait()
+    ends = jnp.transpose(ends_in[...])
+    later = owner - ends
     later = jnp.where(later < 0, later + owners, later)
     turn[...] = later
-    last = order[...] + (owners - 1)
+    last = ends + (owners - 1)
     last = jnp.where(last >= owners, last - owners, last)
     apart[...] = last ^ owner
     batches, rows_in = narrow.shape[:2]
@@ -229,16 +233,18 @@
         ),
         (
             place, hbm(system_values[0], pltpu.HBM), hbm(block_pattern[0], pltpu.HBM),
-            subset_order,
+            hbm(jnp.transpose(subset_order), pltpu.HBM),
             hbm(start_volume, pltpu.HBM),
         ),
-        [SM, HB, HB, VM, HB],
+        [SM, HB, HB, HB, HB],
         work,
         "load",
         scratch=[
             pltpu.VMEM((fronts, slices, voxels), BF16),
             pltpu.SMEM(block_pattern.shape[1:], jnp.int32),
+            pltpu.VMEM((fronts, slices), jnp.int32),
             pltpu.SemaphoreType.DMA((loads,)),
+            pltpu.SemaphoreType.DMA,
             pltpu.SemaphoreType.DMA,
             pltpu.SemaphoreType.DMA,
         ],
@@ -333,7 +339,7 @@
             token = now[n].astype(F16)
             if j + 1 < passes:
                 now[n] = passed(token, "subset", 1)
-    outs = []
+    out = jnp.zeros(start_volume.shape, BF16)
     for n in range(BATCHES):
         found = from_all_owners(now[n].astype(BF16))
         parts = []
@@ -342,8 +348,8 @@
             for d in range(1, owners):
                 got = jnp.where(apart[these[n], f : f + 1] == d, found[d], got)
             parts.append(got)
-        outs.append(jnp.stack(parts))
-    return jnp.concatenate(outs, axis=1)
+        out = lax.dynamic_update_slice(out, jnp.stack(parts), (0, n * batch, 0))
+    return out
 
 
 def solution(mesh):

time: 154 us -> 153 us (level)
  no operation moved by 1% of the time
where the time goes in v2:
time: 153 us
  Pallas kernels  62.2 us (41%)
  starting transfers between devices  56.1 us (37%)
  waiting for transfers between devices  26.5 us (17%)
  other arithmetic  6.26 us (4%)
    pallas_call x35, Pallas kernels, call(): pl.pallas_call(kernel, out_shape=out_shape, in_specs=specs, out_specs=out...  62.2 us
    ppermute x46, starting transfers between devices, swapped(): return lax.ppermute(x, axis, [(i, i ^ bit) for i in range(size)])  46.7 us
    ppermute x46, waiting for transfers between devices, swapped(): return lax.ppermute(x, axis, [(i, i ^ bit) for i in range(size)])  23.8 us
    ppermute x6, starting transfers between devices, passed(): lax.ppermute(x, axis, [(i, (i + distance) % size) for i in range(size)])  9.39 us
  transfers between devices with their start and end apart: 52, of which 17 were waited for; matrix products, arithmetic and copies ran while one was open for 3% of the time, Pallas kernels for 32%

profile of v2, /device:TPU:0, one launch (start us, length us, event | category | flops | bytes accessed | tf_op | source)
XLA Modules:
  0.0 152.5 jit_solution(665847170337117175)
XLA Ops:
  0.1 10.6 %load.1 = (bf16[2048,4096]{1,0:T(8,128)(2,1)S(1)}, bf16[4096,2048]{1,0:T(8,128)(2,1)S(1)}, bf16[2,48,4096]{2,1,0:T(8,128)(2,1)S(1)}, f32[2,32,4096]{2,1,0:T(8,12...) custom-call(s32[3]{0:T(128)S(1)} %pad_add_fusion.place, bf16[2048,4096]{1,0:T(8,128)(2,1)} %bitcast.122, ...), custom_call_target="tpu_custom_call" | custom-call | flops 17179869184 | tf_op jit(solution)/shard_map/load/pallas_call | solution.py:24
  18.3 3.1 %collective-permute-start.1 = (f16[48,1024]{1,0:T(8,128)(2,1)S(1)}, f16[48,1024]{1,0:T(8,128)(2,1)S(1)}, u32[]{:S(2)}, u32[]{:S(2)}) collective-permute-start(f16[48,1024]{1,0:T(8,128)(2,1)S(1)} %fusion.9), channel_id=1, source_target_pairs={{0,2},{1,3},{2,0},{3,1},{4,6},{5,7},{6,4},{7,5},{8,10},{9,11},{10,... | collective-permute-start | bytes 294920 | tf_op jit(solution)/shard_map/ppermute | solution.py:179
  21.5 3.3 %collective-permute-done.1 = f16[48,1024]{1,0:T(8,128)(2,1)S(1)} collective-permute-done((f16[48,1024]{1,0:T(8,128)(2,1)S(1)}, f16[48,1024]{1,0:T(8,128)(2,1)S(1)}, u32[]{:S(2)}, u32[]{:S(2)}) %collective-permute-start.1) | collective-permute-done | bytes 98336 | tf_op jit(solution)/shard_map/ppermute | solution.py:179
  24.8 3.0 %collective-permute-start.2 = (f16[48,1024]{1,0:T(8,128)(2,1)S(1)}, f16[48,1024]{1,0:T(8,128)(2,1)S(1)}, u32[]{:S(2)}, u32[]{:S(2)}) collective-permute-start(f16[48,1024]{1,0:T(8,128)(2,1)S(1)} %fusion), channel_id=1, source_target_pairs={{0,4},{1,5},{2,6},{3,7},{4,0},{5,1},{6,2},{7,3},{8,12},{9,13},{10,... | collective-permute-start | bytes 294920 | tf_op jit(solution)/shard_map/ppermute | solution.py:179
  30.5 3.1 %collective-permute-start.7 = (f16[32,1024]{1,0:T(8,128)(2,1)S(1)}, f16[32,1024]{1,0:T(8,128)(2,1)S(1)}, u32[]{:S(2)}, u32[]{:S(2)}) collective-permute-start(f16[32,1024]{1,0:T(8,128)(2,1)S(1)} %convert_element_type.267), channel_id=1, source_target_pairs={{0,4},{1,5},{2,6},{3,7},{4,0},{5,1},{6,2},{7,3},{8,12},{9,13},{10,... | collective-permute-start | bytes 196616 | tf_op jit(solution)/shard_map/ppermute | solution.py:179
  33.8 1.7 %spread_first.8.so_far = f32[48,4096]{1,0:T(8,128)S(1)} custom-call(s32[1]{0:T(128)} %bitcast.1.place, bf16[48,1024]{1,0:T(8,128)(2,1)S(1)} %concatenate.10.residue, bf16[2048,4096]{1,0:T(8,128)(2,1)S(1)} %get-tuple-element.34.matrix), custom_call_target="tpu_custom_call" | custom-call | flops 8589934592 | tf_op jit(solution)/shard_map/spread_first/pallas_call | solution.py:24
  35.9 1.7 %spread_last.8 = (f32[32,4096]{1,0:T(8,128)S(1)}, f32[1,4096]{1,0:T(1,128)S(1)}) custom-call(s32[1]{0:T(128)} %bitcast.2.place, bf16[48,1024]{1,0:T(8,128)(2,1)S(1)} %collective-permute-done.3.residue, f32[48,4096]{1,0:T(8,128)S(1)} %spread_first.8.so_far, f32[32,4096]{1,0:T(8,128)S(1)} %get-tuple-element.106.volume, ...), custom_call_target="tpu_custom_call" | custom-call | flops 8589934592 | tf_op jit(solution)/shard_map/spread_last/pallas_call | solution.py:24
  37.7 2.8 %collective-permute-start.4 = (f16[32,4096]{1,0:T(8,128)(2,1)S(1)}, f16[32,4096]{1,0:T(8,128)(2,1)S(1)}, u32[]{:S(2)}, u32[]{:S(2)}) collective-permute-start(f16[32,4096]{1,0:T(8,128)(2,1)S(1)} %convert_element_type.261), channel_id=1, source_target_pairs={{0,8},{8,16},{16,24},{24,0},{1,9},{9,17},{17,25},{25,1},{2,10},{10... | collective-permute-start | bytes 786440 | tf_op jit(solution)/shard_map/ppermute | solution.py:174
  42.4 1.7 %spread_last.9 = f32[32,4096]{1,0:T(8,128)S(1)} custom-call(s32[1]{0:T(128)} %bitcast.2.place, bf16[32,1024]{1,0:T(8,128)(2,1)S(1)} %collective-permute-done.8.residue, f32[32,4096]{1,0:T(8,128)S(1)} %spread_first.9.so_far, f32[32,4096]{1,0:T(8,128)S(1)} %get-tuple-element.105.volume, f32[1,4096]{1,0:T(1,128)S(1)} %get-tuple-element.38.column, ...), custom_call_target="tpu_custom_call" | custom-call | flops 8589934592 | tf_op jit(solution)/shard_map/spread_last/pallas_call | solution.py:24
  44.1 1.7 %collective-permute-start.15 = (f16[32,4096]{1,0:T(8,128)(2,1)S(1)}, f16[32,4096]{1,0:T(8,128)(2,1)S(1)}, u32[]{:S(2)}, u32[]{:S(2)}) collective-permute-start(f16[32,4096]{1,0:T(8,128)(2,1)S(1)} %convert_element_type.270), channel_id=1, source_target_pairs={{0,8},{8,16},{16,24},{24,0},{1,9},{9,17},{17,25},{25,1},{2,10},{10... | collective-permute-start | bytes 786440 | tf_op jit(solution)/shard_map/ppermute | solution.py:174
  50.5 4.4 %collective-permute-start.12 = (f16[32,1024]{1,0:T(8,128)(2,1)S(1)}, f16[32,1024]{1,0:T(8,128)(2,1)S(1)}, u32[]{:S(2)}, u32[]{:S(2)}) collective-permute-start(f16[32,1024]{1,0:T(8,128)(2,1)S(1)} %fusion.3), channel_id=1, source_target_pairs={{0,6},{1,7},{2,4},{3,5},{4,2},{5,3},{6,0},{7,1},{8,14},{9,15},{10,... | collective-permute-start | bytes 196616 | tf_op jit(solution)/shard_map/ppermute | solution.py:179
  58.8 2.5 %collective-permute-done.11 = f16[32,1024]{1,0:T(8,128)(2,1)S(1)} collective-permute-done((f16[32,1024]{1,0:T(8,128)(2,1)S(1)}, f16[32,1024]{1,0:T(8,128)(2,1)S(1)}, u32[]{:S(2)}, u32[]{:S(2)}) %collective-permute-start.11) | collective-permute-done | bytes 65568 | tf_op jit(solution)/shard_map/ppermute | solution.py:179
  63.3 1.7 %collective-permute-start.19 = (f16[32,1024]{1,0:T(8,128)(2,1)S(1)}, f16[32,1024]{1,0:T(8,128)(2,1)S(1)}, u32[]{:S(2)}, u32[]{:S(2)}) collective-permute-start(f16[32,1024]{1,0:T(8,128)(2,1)S(1)} %fusion.4), channel_id=1, source_target_pairs={{0,6},{1,7},{2,4},{3,5},{4,2},{5,3},{6,0},{7,1},{8,14},{9,15},{10,... | collective-permute-start | bytes 196616 | tf_op jit(solution)/shard_map/ppermute | solution.py:179
  65.2 2.6 %collective-permute-start.17 = (f16[32,1024]{1,0:T(8,128)(2,1)S(1)}, f16[32,1024]{1,0:T(8,128)(2,1)S(1)}, u32[]{:S(2)}, u32[]{:S(2)}) collective-permute-start(f16[32,1024]{1,0:T(8,128)(2,1)S(1)} %fusion.4), channel_id=1, source_target_pairs={{0,2},{1,3},{2,0},{3,1},{4,6},{5,7},{6,4},{7,5},{8,10},{9,11},{10,... | collective-permute-start | bytes 196616 | tf_op jit(solution)/shard_map/ppermute | solution.py:179
  67.8 1.7 %spread_last.10 = f32[32,4096]{1,0:T(8,128)S(1)} custom-call(s32[1]{0:T(128)} %bitcast.2.place, bf16[32,1024]{1,0:T(8,128)(2,1)S(1)} %collective-permute-done.13.residue, f32[32,4096]{1,0:T(8,128)S(1)} %spread_first.10.so_far, f32[32,4096]{1,0:T(8,128)S(1)} %get-tuple-element.121.volume, f32[1,4096]{1,0:T(1,128)S(1)} %get-tuple-element.38.column, ...), custom_call_target="tpu_custom_call" | custom-call | flops 8589934592 | tf_op jit(solution)/shard_map/spread_last/pallas_call | solution.py:24
  70.5 1.9 %collective-permute-done.18 = f16[32,1024]{1,0:T(8,128)(2,1)S(1)} collective-permute-done((f16[32,1024]{1,0:T(8,128)(2,1)S(1)}, f16[32,1024]{1,0:T(8,128)(2,1)S(1)}, u32[]{:S(2)}, u32[]{:S(2)}) %collective-permute-start.18) | collective-permute-done | bytes 65568 | tf_op jit(solution)/shard_map/ppermute | solution.py:179
  74.4 1.7 %spread_last.11 = f32[32,4096]{1,0:T(8,128)S(1)} custom-call(s32[1]{0:T(128)} %bitcast.2.place, bf16[32,1024]{1,0:T(8,128)(2,1)S(1)} %collective-permute-done.20.residue, f32[32,4096]{1,0:T(8,128)S(1)} %spread_first.11.so_far, f32[32,4096]{1,0:T(8,128)S(1)} %get-tuple-element.119.volume, f32[1,4096]{1,0:T(1,128)S(1)} %get-tuple-element.38.column, ...), custom_call_target="tpu_custom_call" | custom-call | flops 8589934592 | tf_op jit(solution)/shard_map/spread_last/pallas_call | solution.py:24
  81.6 1.7 %collective-permute-start.24 = (f16[32,1024]{1,0:T(8,128)(2,1)S(1)}, f16[32,1024]{1,0:T(8,128)(2,1)S(1)}, u32[]{:S(2)}, u32[]{:S(2)}) collective-permute-start(f16[32,1024]{1,0:T(8,128)(2,1)S(1)} %fusion.5), channel_id=1, source_target_pairs={{0,6},{1,7},{2,4},{3,5},{4,2},{5,3},{6,0},{7,1},{8,14},{9,15},{10,... | collective-permute-start | bytes 196616 | tf_op jit(solution)/shard_map/ppermute | solution.py:179
  83.4 2.6 %collective-permute-start.22 = (f16[32,1024]{1,0:T(8,128)(2,1)S(1)}, f16[32,1024]{1,0:T(8,128)(2,1)S(1)}, u32[]{:S(2)}, u32[]{:S(2)}) collective-permute-start(f16[32,1024]{1,0:T(8,128)(2,1)S(1)} %fusion.5), channel_id=1, source_target_pairs={{0,2},{1,3},{2,0},{3,1},{4,6},{5,7},{6,4},{7,5},{8,10},{9,11},{10,... | collective-permute-start | bytes 196616 | tf_op jit(solution)/shard_map/ppermute | solution.py:179
  92.7 1.7 %collective-permute-start.31 = (f16[32,1024]{1,0:T(8,128)(2,1)S(1)}, f16[32,1024]{1,0:T(8,128)(2,1)S(1)}, u32[]{:S(2)}, u32[]{:S(2)}) collective-permute-start(f16[32,1024]{1,0:T(8,128)(2,1)S(1)} %fusion.6), channel_id=1, source_target_pairs={{0,6},{1,7},{2,4},{3,5},{4,2},{5,3},{6,0},{7,1},{8,14},{9,15},{10,... | collective-permute-start | bytes 196616 | tf_op jit(solution)/shard_map/ppermute | solution.py:179
  94.4 2.8 %collective-permute-start.29 = (f16[32,1024]{1,0:T(8,128)(2,1)S(1)}, f16[32,1024]{1,0:T(8,128)(2,1)S(1)}, u32[]{:S(2)}, u32[]{:S(2)}) collective-permute-start(f16[32,1024]{1,0:T(8,128)(2,1)S(1)} %fusion.6), channel_id=1, source_target_pairs={{0,2},{1,3},{2,0},{3,1},{4,6},{5,7},{6,4},{7,5},{8,10},{9,11},{10,... | collective-permute-start | bytes 196616 | tf_op jit(solution)/shard_map/ppermute | solution.py:179
  97.2 1.7 %spread_last.12 = f32[32,4096]{1,0:T(8,128)S(1)} custom-call(s32[1]{0:T(128)} %bitcast.2.place, bf16[32,1024]{1,0:T(8,128)(2,1)S(1)} %collective-permute-done.25.residue, f32[32,4096]{1,0:T(8,128)S(1)} %spread_first.12.so_far, f32[32,4096]{1,0:T(8,128)S(1)} %get-tuple-element.117.volume, f32[1,4096]{1,0:T(1,128)S(1)} %get-tuple-element.38.column, ...), custom_call_target="tpu_custom_call" | custom-call | flops 8589934592 | tf_op jit(solution)/shard_map/spread_last/pallas_call | solution.py:24
  100.0 1.8 %collective-permute-done.30 = f16[32,1024]{1,0:T(8,128)(2,1)S(1)} collective-permute-done((f16[32,1024]{1,0:T(8,128)(2,1)S(1)}, f16[32,1024]{1,0:T(8,128)(2,1)S(1)}, u32[]{:S(2)}, u32[]{:S(2)}) %collective-permute-start.30) | collective-permute-done | bytes 65568 | tf_op jit(solution)/shard_map/ppermute | solution.py:179
  103.8 1.7 %spread_last.13 = f32[32,4096]{1,0:T(8,128)S(1)} custom-call(s32[1]{0:T(128)} %bitcast.2.place, bf16[32,1024]{1,0:T(8,128)(2,1)S(1)} %collective-permute-done.32.residue, f32[32,4096]{1,0:T(8,128)S(1)} %spread_first.13.so_far, f32[32,4096]{1,0:T(8,128)S(1)} %get-tuple-element.115.volume, f32[1,4096]{1,0:T(1,128)S(1)} %get-tuple-element.38.column, ...), custom_call_target="tpu_custom_call" | custom-call | flops 8589934592 | tf_op jit(solution)/shard_map/spread_last/pallas_call | solution.py:24
  111.0 1.7 %collective-permute-start.36 = (f16[32,1024]{1,0:T(8,128)(2,1)S(1)}, f16[32,1024]{1,0:T(8,128)(2,1)S(1)}, u32[]{:S(2)}, u32[]{:S(2)}) collective-permute-start(f16[32,1024]{1,0:T(8,128)(2,1)S(1)} %fusion.7), channel_id=1, source_target_pairs={{0,6},{1,7},{2,4},{3,5},{4,2},{5,3},{6,0},{7,1},{8,14},{9,15},{10,... | collective-permute-start | bytes 196616 | tf_op jit(solution)/shard_map/ppermute | solution.py:179
  112.9 2.6 %collective-permute-start.34 = (f16[32,1024]{1,0:T(8,128)(2,1)S(1)}, f16[32,1024]{1,0:T(8,128)(2,1)S(1)}, u32[]{:S(2)}, u32[]{:S(2)}) collective-permute-start(f16[32,1024]{1,0:T(8,128)(2,1)S(1)} %fusion.7), channel_id=1, source_target_pairs={{0,2},{1,3},{2,0},{3,1},{4,6},{5,7},{6,4},{7,5},{8,10},{9,11},{10,... | collective-permute-start | bytes 196616 | tf_op jit(solution)/shard_map/ppermute | solution.py:179
  122.1 1.7 %collective-permute-start.46 = (f16[32,1024]{1,0:T(8,128)(2,1)S(1)}, f16[32,1024]{1,0:T(8,128)(2,1)S(1)}, u32[]{:S(2)}, u32[]{:S(2)}) collective-permute-start(f16[32,1024]{1,0:T(8,128)(2,1)S(1)} %fusion.8), channel_id=1, source_target_pairs={{0,6},{1,7},{2,4},{3,5},{4,2},{5,3},{6,0},{7,1},{8,14},{9,15},{10,... | collective-permute-start | bytes 196616 | tf_op jit(solution)/shard_map/ppermute | solution.py:179
  123.8 2.8 %collective-permute-start.44 = (f16[32,1024]{1,0:T(8,128)(2,1)S(1)}, f16[32,1024]{1,0:T(8,128)(2,1)S(1)}, u32[]{:S(2)}, u32[]{:S(2)}) collective-permute-start(f16[32,1024]{1,0:T(8,128)(2,1)S(1)} %fusion.8), channel_id=1, source_target_pairs={{0,2},{1,3},{2,0},{3,1},{4,6},{5,7},{6,4},{7,5},{8,10},{9,11},{10,... | collective-permute-start | bytes 196616 | tf_op jit(solution)/shard_map/ppermute | solution.py:179
  126.6 1.7 %spread_last.14.before = f32[32,4096]{1,0:T(8,128)S(1)} custom-call(s32[1]{0:T(128)} %bitcast.2.place, bf16[32,1024]{1,0:T(8,128)(2,1)S(1)} %collective-permute-done.37.residue, f32[32,4096]{1,0:T(8,128)S(1)} %spread_first.14.so_far, f32[32,4096]{1,0:T(8,128)S(1)} %get-tuple-element.113.volume, f32[1,4096]{1,0:T(1,128)S(1)} %get-tuple-element.38.column, ...), custom_call_target="tpu_custom_call" | custom-call | flops 8589934592 | tf_op jit(solution)/shard_map/spread_last/pallas_call | solution.py:24
  133.1 1.7 %spread_last.15 = f32[32,4096]{1,0:T(8,128)S(1)} custom-call(s32[1]{0:T(128)} %bitcast.2.place, bf16[32,1024]{1,0:T(8,128)(2,1)S(1)} %collective-permute-done.47.residue, f32[32,4096]{1,0:T(8,128)S(1)} %spread_first.15.so_far, f32[32,4096]{1,0:T(8,128)S(1)} %get-tuple-element.111.volume, f32[1,4096]{1,0:T(1,128)S(1)} %get-tuple-element.38.column, ...), custom_call_target="tpu_custom_call" | custom-call | flops 8589934592 | tf_op jit(solution)/shard_map/spread_last/pallas_call | solution.py:24
  140.2 3.8 %collective-permute-done.50 = bf16[32,4096]{1,0:T(8,128)(2,1)S(1)} collective-permute-done((bf16[32,4096]{1,0:T(8,128)(2,1)S(1)}, bf16[32,4096]{1,0:T(8,128)(2,1)S(1)}, u32[]{:S(2)}, u32[]{:S(2)}) %collective-permute-start.50) | collective-permute-done | bytes 262176 | tf_op jit(solution)/shard_map/ppermute | solution.py:179
  148.4 2.3 %collective-permute-done.49 = bf16[32,2048]{1,0:T(8,128)(2,1)S(1)} collective-permute-done((bf16[32,2048]{1,0:T(8,128)(2,1)S(1)}, bf16[32,2048]{1,0:T(8,128)(2,1)S(1)}, u32[]{:S(2)}, u32[]{:S(2)}) %collective-permute-start.49) | collective-permute-done | bytes 131104 | tf_op jit(solution)/shard_map/ppermute | solution.py:179
  (206 shorter events, 70.3 us)
Async XLA Ops:
  12.3 9.1 %collective-permute-start.5 = (f16[32,1024]{1,0:T(8,128)(2,1)S(1)}, f16[32,1024]{1,0:T(8,128)(2,1)S(1)}, u32[]{:S(2)}, u32[]{:S(2)}) collective-permute-start(f16[32,1024]{1,0:T(8,128)(2,1)S(1)} %multiply_convert_fusion.13), channel_id=1, source_target_pairs={{0,1},{1,0},{2,3},{3,2},{4,5},{5,4},{6,7},{7,6},{8,9},{9,8},{10,11... | collective-permute-start | bytes 196616 | tf_op jit(solution)/shard_map/ppermute | solution.py:179
  21.4 7.6 %collective-permute-start.6 = (f16[32,1024]{1,0:T(8,128)(2,1)S(1)}, f16[32,1024]{1,0:T(8,128)(2,1)S(1)}, u32[]{:S(2)}, u32[]{:S(2)}) collective-permute-start(f16[32,1024]{1,0:T(8,128)(2,1)S(1)} %get-tuple-element.95), channel_id=1, source_target_pairs={{0,2},{1,3},{2,0},{3,1},{4,6},{5,7},{6,4},{7,5},{8,10},{9,11},{10,... | collective-permute-start | bytes 196616 | tf_op jit(solution)/shard_map/ppermute | solution.py:179
  37.7 9.3 %collective-permute-start.4 = (f16[32,4096]{1,0:T(8,128)(2,1)S(1)}, f16[32,4096]{1,0:T(8,128)(2,1)S(1)}, u32[]{:S(2)}, u32[]{:S(2)}) collective-permute-start(f16[32,4096]{1,0:T(8,128)(2,1)S(1)} %convert_element_type.261), channel_id=1, source_target_pairs={{0,8},{8,16},{16,24},{24,0},{1,9},{9,17},{17,25},{25,1},{2,10},{10... | collective-permute-start | bytes 786440 | tf_op jit(solution)/shard_map/ppermute | solution.py:174
  44.1 11.4 %collective-permute-start.15 = (f16[32,4096]{1,0:T(8,128)(2,1)S(1)}, f16[32,4096]{1,0:T(8,128)(2,1)S(1)}, u32[]{:S(2)}, u32[]{:S(2)}) collective-permute-start(f16[32,4096]{1,0:T(8,128)(2,1)S(1)} %convert_element_type.270), channel_id=1, source_target_pairs={{0,8},{8,16},{16,24},{24,0},{1,9},{9,17},{17,25},{25,1},{2,10},{10... | collective-permute-start | bytes 786440 | tf_op jit(solution)/shard_map/ppermute | solution.py:174
  50.5 8.3 %collective-permute-start.12 = (f16[32,1024]{1,0:T(8,128)(2,1)S(1)}, f16[32,1024]{1,0:T(8,128)(2,1)S(1)}, u32[]{:S(2)}, u32[]{:S(2)}) collective-permute-start(f16[32,1024]{1,0:T(8,128)(2,1)S(1)} %fusion.3), channel_id=1, source_target_pairs={{0,6},{1,7},{2,4},{3,5},{4,2},{5,3},{6,0},{7,1},{8,14},{9,15},{10,... | collective-permute-start | bytes 196616 | tf_op jit(solution)/shard_map/ppermute | solution.py:179
  54.9 6.5 %collective-permute-start.11 = (f16[32,1024]{1,0:T(8,128)(2,1)S(1)}, f16[32,1024]{1,0:T(8,128)(2,1)S(1)}, u32[]{:S(2)}, u32[]{:S(2)}) collective-permute-start(f16[32,1024]{1,0:T(8,128)(2,1)S(1)} %fusion.3), channel_id=1, source_target_pairs={{0,4},{1,5},{2,6},{3,7},{4,0},{5,1},{6,2},{7,3},{8,12},{9,13},{10,... | collective-permute-start | bytes 196616 | tf_op jit(solution)/shard_map/ppermute | solution.py:179
  63.3 7.2 %collective-permute-start.19 = (f16[32,1024]{1,0:T(8,128)(2,1)S(1)}, f16[32,1024]{1,0:T(8,128)(2,1)S(1)}, u32[]{:S(2)}, u32[]{:S(2)}) collective-permute-start(f16[32,1024]{1,0:T(8,128)(2,1)S(1)} %fusion.4), channel_id=1, source_target_pairs={{0,6},{1,7},{2,4},{3,5},{4,2},{5,3},{6,0},{7,1},{8,14},{9,15},{10,... | collective-permute-start | bytes 196616 | tf_op jit(solution)/shard_map/ppermute | solution.py:179
  65.0 7.4 %collective-permute-start.18 = (f16[32,1024]{1,0:T(8,128)(2,1)S(1)}, f16[32,1024]{1,0:T(8,128)(2,1)S(1)}, u32[]{:S(2)}, u32[]{:S(2)}) collective-permute-start(f16[32,1024]{1,0:T(8,128)(2,1)S(1)} %fusion.4), channel_id=1, source_target_pairs={{0,4},{1,5},{2,6},{3,7},{4,0},{5,1},{6,2},{7,3},{8,12},{9,13},{10,... | collective-permute-start | bytes 196616 | tf_op jit(solution)/shard_map/ppermute | solution.py:179
  65.2 7.3 %collective-permute-start.17 = (f16[32,1024]{1,0:T(8,128)(2,1)S(1)}, f16[32,1024]{1,0:T(8,128)(2,1)S(1)}, u32[]{:S(2)}, u32[]{:S(2)}) collective-permute-start(f16[32,1024]{1,0:T(8,128)(2,1)S(1)} %fusion.4), channel_id=1, source_target_pairs={{0,2},{1,3},{2,0},{3,1},{4,6},{5,7},{6,4},{7,5},{8,10},{9,11},{10,... | collective-permute-start | bytes 196616 | tf_op jit(solution)/shard_map/ppermute | solution.py:179
  69.5 8.8 %collective-permute-start.14 = (f16[32,4096]{1,0:T(8,128)(2,1)S(1)}, f16[32,4096]{1,0:T(8,128)(2,1)S(1)}, u32[]{:S(2)}, u32[]{:S(2)}) collective-permute-start(f16[32,4096]{1,0:T(8,128)(2,1)S(1)} %convert_element_type.280), channel_id=1, source_target_pairs={{0,8},{8,16},{16,24},{24,0},{1,9},{9,17},{17,25},{25,1},{2,10},{10... | collective-permute-start | bytes 786440 | tf_op jit(solution)/shard_map/ppermute | solution.py:174
  76.1 10.0 %collective-permute-start.27 = (f16[32,4096]{1,0:T(8,128)(2,1)S(1)}, f16[32,4096]{1,0:T(8,128)(2,1)S(1)}, u32[]{:S(2)}, u32[]{:S(2)}) collective-permute-start(f16[32,4096]{1,0:T(8,128)(2,1)S(1)} %convert_element_type.290), channel_id=1, source_target_pairs={{0,8},{8,16},{16,24},{24,0},{1,9},{9,17},{17,25},{25,1},{2,10},{10... | collective-permute-start | bytes 786440 | tf_op jit(solution)/shard_map/ppermute | solution.py:174
  81.6 7.8 %collective-permute-start.24 = (f16[32,1024]{1,0:T(8,128)(2,1)S(1)}, f16[32,1024]{1,0:T(8,128)(2,1)S(1)}, u32[]{:S(2)}, u32[]{:S(2)}) collective-permute-start(f16[32,1024]{1,0:T(8,128)(2,1)S(1)} %fusion.5), channel_id=1, source_target_pairs={{0,6},{1,7},{2,4},{3,5},{4,2},{5,3},{6,0},{7,1},{8,14},{9,15},{10,... | collective-permute-start | bytes 196616 | tf_op jit(solution)/shard_map/ppermute | solution.py:179
  83.3 7.5 %collective-permute-start.23 = (f16[32,1024]{1,0:T(8,128)(2,1)S(1)}, f16[32,1024]{1,0:T(8,128)(2,1)S(1)}, u32[]{:S(2)}, u32[]{:S(2)}) collective-permute-start(f16[32,1024]{1,0:T(8,128)(2,1)S(1)} %fusion.5), channel_id=1, source_target_pairs={{0,4},{1,5},{2,6},{3,7},{4,0},{5,1},{6,2},{7,3},{8,12},{9,13},{10,... | collective-permute-start | bytes 196616 | tf_op jit(solution)/shard_map/ppermute | solution.py:179
  83.4 7.4 %collective-permute-start.22 = (f16[32,1024]{1,0:T(8,128)(2,1)S(1)}, f16[32,1024]{1,0:T(8,128)(2,1)S(1)}, u32[]{:S(2)}, u32[]{:S(2)}) collective-permute-start(f16[32,1024]{1,0:T(8,128)(2,1)S(1)} %fusion.5), channel_id=1, source_target_pairs={{0,2},{1,3},{2,0},{3,1},{4,6},{5,7},{6,4},{7,5},{8,10},{9,11},{10,... | collective-permute-start | bytes 196616 | tf_op jit(solution)/shard_map/ppermute | solution.py:179
  92.7 7.4 %collective-permute-start.31 = (f16[32,1024]{1,0:T(8,128)(2,1)S(1)}, f16[32,1024]{1,0:T(8,128)(2,1)S(1)}, u32[]{:S(2)}, u32[]{:S(2)}) collective-permute-start(f16[32,1024]{1,0:T(8,128)(2,1)S(1)} %fusion.6), channel_id=1, source_target_pairs={{0,6},{1,7},{2,4},{3,5},{4,2},{5,3},{6,0},{7,1},{8,14},{9,15},{10,... | collective-permute-start | bytes 196616 | tf_op jit(solution)/shard_map/ppermute | solution.py:179
  94.4 7.4 %collective-permute-start.30 = (f16[32,1024]{1,0:T(8,128)(2,1)S(1)}, f16[32,1024]{1,0:T(8,128)(2,1)S(1)}, u32[]{:S(2)}, u32[]{:S(2)}) collective-permute-start(f16[32,1024]{1,0:T(8,128)(2,1)S(1)} %fusion.6), channel_id=1, source_target_pairs={{0,4},{1,5},{2,6},{3,7},{4,0},{5,1},{6,2},{7,3},{8,12},{9,13},{10,... | collective-permute-start | bytes 196616 | tf_op jit(solution)/shard_map/ppermute | solution.py:179
  94.4 7.4 %collective-permute-start.29 = (f16[32,1024]{1,0:T(8,128)(2,1)S(1)}, f16[32,1024]{1,0:T(8,128)(2,1)S(1)}, u32[]{:S(2)}, u32[]{:S(2)}) collective-permute-start(f16[32,1024]{1,0:T(8,128)(2,1)S(1)} %fusion.6), channel_id=1, source_target_pairs={{0,2},{1,3},{2,0},{3,1},{4,6},{5,7},{6,4},{7,5},{8,10},{9,11},{10,... | collective-permute-start | bytes 196616 | tf_op jit(solution)/shard_map/ppermute | solution.py:179
  98.9 8.8 %collective-permute-start.26 = (f16[32,4096]{1,0:T(8,128)(2,1)S(1)}, f16[32,4096]{1,0:T(8,128)(2,1)S(1)}, u32[]{:S(2)}, u32[]{:S(2)}) collective-permute-start(f16[32,4096]{1,0:T(8,128)(2,1)S(1)} %convert_element_type.300), channel_id=1, source_target_pairs={{0,8},{8,16},{16,24},{24,0},{1,9},{9,17},{17,25},{25,1},{2,10},{10... | collective-permute-start | bytes 786440 | tf_op jit(solution)/shard_map/ppermute | solution.py:174
  105.6 9.9 %collective-permute-start.42 = (f16[32,4096]{1,0:T(8,128)(2,1)S(1)}, f16[32,4096]{1,0:T(8,128)(2,1)S(1)}, u32[]{:S(2)}, u32[]{:S(2)}) collective-permute-start(f16[32,4096]{1,0:T(8,128)(2,1)S(1)} %convert_element_type.310), channel_id=1, source_target_pairs={{0,8},{8,16},{16,24},{24,0},{1,9},{9,17},{17,25},{25,1},{2,10},{10... | collective-permute-start | bytes 786440 | tf_op jit(solution)/shard_map/ppermute | solution.py:174
  111.0 7.8 %collective-permute-start.36 = (f16[32,1024]{1,0:T(8,128)(2,1)S(1)}, f16[32,1024]{1,0:T(8,128)(2,1)S(1)}, u32[]{:S(2)}, u32[]{:S(2)}) collective-permute-start(f16[32,1024]{1,0:T(8,128)(2,1)S(1)} %fusion.7), channel_id=1, source_target_pairs={{0,6},{1,7},{2,4},{3,5},{4,2},{5,3},{6,0},{7,1},{8,14},{9,15},{10,... | collective-permute-start | bytes 196616 | tf_op jit(solution)/shard_map/ppermute | solution.py:179
  112.7 7.5 %collective-permute-start.35 = (f16[32,1024]{1,0:T(8,128)(2,1)S(1)}, f16[32,1024]{1,0:T(8,128)(2,1)S(1)}, u32[]{:S(2)}, u32[]{:S(2)}) collective-permute-start(f16[32,1024]{1,0:T(8,128)(2,1)S(1)} %fusion.7), channel_id=1, source_target_pairs={{0,4},{1,5},{2,6},{3,7},{4,0},{5,1},{6,2},{7,3},{8,12},{9,13},{10,... | collective-permute-start | bytes 196616 | tf_op jit(solution)/shard_map/ppermute | solution.py:179
  112.9 7.3 %collective-permute-start.34 = (f16[32,1024]{1,0:T(8,128)(2,1)S(1)}, f16[32,1024]{1,0:T(8,128)(2,1)S(1)}, u32[]{:S(2)}, u32[]{:S(2)}) collective-permute-start(f16[32,1024]{1,0:T(8,128)(2,1)S(1)} %fusion.7), channel_id=1, source_target_pairs={{0,2},{1,3},{2,0},{3,1},{4,6},{5,7},{6,4},{7,5},{8,10},{9,11},{10,... | collective-permute-start | bytes 196616 | tf_op jit(solution)/shard_map/ppermute | solution.py:179
  122.1 7.9 %collective-permute-start.46 = (f16[32,1024]{1,0:T(8,128)(2,1)S(1)}, f16[32,1024]{1,0:T(8,128)(2,1)S(1)}, u32[]{:S(2)}, u32[]{:S(2)}) collective-permute-start(f16[32,1024]{1,0:T(8,128)(2,1)S(1)} %fusion.8), channel_id=1, source_target_pairs={{0,6},{1,7},{2,4},{3,5},{4,2},{5,3},{6,0},{7,1},{8,14},{9,15},{10,... | collective-permute-start | bytes 196616 | tf_op jit(solution)/shard_map/ppermute | solution.py:179
  123.8 7.4 %collective-permute-start.45 = (f16[32,1024]{1,0:T(8,128)(2,1)S(1)}, f16[32,1024]{1,0:T(8,128)(2,1)S(1)}, u32[]{:S(2)}, u32[]{:S(2)}) collective-permute-start(f16[32,1024]{1,0:T(8,128)(2,1)S(1)} %fusion.8), channel_id=1, source_target_pairs={{0,4},{1,5},{2,6},{3,7},{4,0},{5,1},{6,2},{7,3},{8,12},{9,13},{10,... | collective-permute-start | bytes 196616 | tf_op jit(solution)/shard_map/ppermute | solution.py:179
  123.8 7.4 %collective-permute-start.44 = (f16[32,1024]{1,0:T(8,128)(2,1)S(1)}, f16[32,1024]{1,0:T(8,128)(2,1)S(1)}, u32[]{:S(2)}, u32[]{:S(2)}) collective-permute-start(f16[32,1024]{1,0:T(8,128)(2,1)S(1)} %fusion.8), channel_id=1, source_target_pairs={{0,2},{1,3},{2,0},{3,1},{4,6},{5,7},{6,4},{7,5},{8,10},{9,11},{10,... | collective-permute-start | bytes 196616 | tf_op jit(solution)/shard_map/ppermute | solution.py:179
  128.3 10.8 %collective-permute-start.40 = (bf16[32,4096]{1,0:T(8,128)(2,1)S(1)}, bf16[32,4096]{1,0:T(8,128)(2,1)S(1)}, u32[]{:S(2)}, u32[]{:S(2)}) collective-permute-start(bf16[32,4096]{1,0:T(8,128)(2,1)S(1)} %convert_element_type.320), channel_id=1, source_target_pairs={{0,8},{8,0},{16,24},{24,16},{1,9},{9,1},{17,25},{25,17},{2,10},{10... | collective-permute-start | bytes 786440 | tf_op jit(solution)/shard_map/ppermute | solution.py:179
  129.5 7.6 %collective-permute-start.38 = (bf16[32,4096]{1,0:T(8,128)(2,1)S(1)}, bf16[32,4096]{1,0:T(8,128)(2,1)S(1)}, u32[]{:S(2)}, u32[]{:S(2)}) collective-permute-start(bf16[32,4096]{1,0:T(8,128)(2,1)S(1)} %convert_element_type.320), channel_id=1, source_target_pairs={{0,16},{8,24},{16,0},{24,8},{1,17},{9,25},{17,1},{25,9},{2,18},{10... | collective-permute-start | bytes 786440 | tf_op jit(solution)/shard_map/ppermute | solution.py:179
  134.9 9.2 %collective-permute-start.50 = (bf16[32,4096]{1,0:T(8,128)(2,1)S(1)}, bf16[32,4096]{1,0:T(8,128)(2,1)S(1)}, u32[]{:S(2)}, u32[]{:S(2)}) collective-permute-start(bf16[32,4096]{1,0:T(8,128)(2,1)S(1)} %convert_element_type.329), channel_id=1, source_target_pairs={{0,8},{8,0},{16,24},{24,16},{1,9},{9,1},{17,25},{25,17},{2,10},{10... | collective-permute-start | bytes 786440 | tf_op jit(solution)/shard_map/ppermute | solution.py:179
  136.1 9.5 %collective-permute-start.48 = (bf16[32,4096]{1,0:T(8,128)(2,1)S(1)}, bf16[32,4096]{1,0:T(8,128)(2,1)S(1)}, u32[]{:S(2)}, u32[]{:S(2)}) collective-permute-start(bf16[32,4096]{1,0:T(8,128)(2,1)S(1)} %convert_element_type.329), channel_id=1, source_target_pairs={{0,16},{8,24},{16,0},{24,8},{1,17},{9,25},{17,1},{25,9},{2,18},{10... | collective-permute-start | bytes 786440 | tf_op jit(solution)/shard_map/ppermute | solution.py:179
  137.1 9.3 %collective-permute-start.39 = (bf16[32,2048]{1,0:T(8,128)(2,1)S(1)}, bf16[32,2048]{1,0:T(8,128)(2,1)S(1)}, u32[]{:S(2)}, u32[]{:S(2)}) collective-permute-start(bf16[32,2048]{1,0:T(8,128)(2,1)S(1)} %slice.236), channel_id=1, source_target_pairs={{0,8},{8,0},{16,24},{24,16},{1,9},{9,1},{17,25},{25,17},{2,10},{10... | collective-permute-start | bytes 393224 | tf_op jit(solution)/shard_map/ppermute | solution.py:179
  139.2 8.9 %collective-permute-start.41 = (bf16[32,2048]{1,0:T(8,128)(2,1)S(1)}, bf16[32,2048]{1,0:T(8,128)(2,1)S(1)}, u32[]{:S(2)}, u32[]{:S(2)}) collective-permute-start(bf16[32,2048]{1,0:T(8,128)(2,1)S(1)} %slice.237), channel_id=1, source_target_pairs={{0,16},{8,24},{16,0},{24,8},{1,17},{9,25},{17,1},{25,9},{2,18},{10... | collective-permute-start | bytes 393224 | tf_op jit(solution)/shard_map/ppermute | solution.py:179
  144.0 6.6 %collective-permute-start.51 = (bf16[32,2048]{1,0:T(8,128)(2,1)S(1)}, bf16[32,2048]{1,0:T(8,128)(2,1)S(1)}, u32[]{:S(2)}, u32[]{:S(2)}) collective-permute-start(bf16[32,2048]{1,0:T(8,128)(2,1)S(1)} %slice.239), channel_id=1, source_target_pairs={{0,16},{8,24},{16,0},{24,8},{1,17},{9,25},{17,1},{25,9},{2,18},{10... | collective-permute-start | bytes 393224 | tf_op jit(solution)/shard_map/ppermute | solution.py:179
  (35 other events, 144.0 us)

commit v3 on v2

--- a/solution.py
+++ b/solution.py
@@ -82,10 +82,17 @@
     narrow[:, batch:, :] = jnp.ones((batches, rows_in - batch, voxels), BF16)
     first.wait()
     chosen = [later[:, f : f + 1] == 0 for f in range(1, fronts.shape[0])]
-    step = 4 * side
-
-    @pl.loop(0, voxels // step)
+    step = voxels // loads
+    blocks_in.wait()
+
+    @pl.loop(0, loads)
     def _(i):
+        piece(i).wait()
+
+        @pl.when(i + AHEAD < loads)
+        def _():
+            piece(i + AHEAD).start()
+
         cols = pl.ds(pl.multiple_of(i * step, step), step)
         got = fronts[0, :, cols].astype(F32)
         for f, here in enumerate(chosen):
@@ -94,17 +101,6 @@
             part = got[b * batch : (b + 1) * batch]
             volume[b, :, cols] = part
             narrow[b, :batch, cols] = part.astype(BF16)
-
-    blocks_in.wait()
-
-    @pl.loop(0, loads)
-    def _(i):
-        piece(i).wait()
-
-        @pl.when(i + AHEAD < loads)
-        def _():
-            piece(i + AHEAD).start()
-
         where = pl.ds(pl.multiple_of(i * rows, rows), rows)
         for c in range(0, col_blocks, 2):
             cols = slice(c * side, (c + 2) * side)

time: 153 us -> 152 us (level)
  no operation moved by 1% of the time
where the time goes in v3:
time: 152 us
  Pallas kernels  61.5 us (40%)
  starting transfers between devices  56.1 us (37%)
  waiting for transfers between devices  26.5 us (17%)
  other arithmetic  6.26 us (4%)
    pallas_call x35, Pallas kernels, call(): pl.pallas_call(kernel, out_shape=out_shape, in_specs=specs, out_specs=out...  61.5 us
    ppermute x46, starting transfers between devices, swapped(): return lax.ppermute(x, axis, [(i, i ^ bit) for i in range(size)])  46.7 us
    ppermute x46, waiting for transfers between devices, swapped(): return lax.ppermute(x, axis, [(i, i ^ bit) for i in range(size)])  23.7 us
    ppermute x6, starting transfers between devices, passed(): lax.ppermute(x, axis, [(i, (i + distance) % size) for i in range(size)])  9.4 us
  transfers between devices with their start and end apart: 52, of which 17 were waited for; matrix products, arithmetic and copies ran while one was open for 3% of the time, Pallas kernels for 32%

profile of v3, /device:TPU:0, one launch (start us, length us, event | category | flops | bytes accessed | tf_op | source)
XLA Modules:
  0.0 151.8 jit_solution(4227080138887535547)
XLA Ops:
  0.1 9.9 %load.1 = (bf16[2048,4096]{1,0:T(8,128)(2,1)S(1)}, bf16[4096,2048]{1,0:T(8,128)(2,1)S(1)}, bf16[2,48,4096]{2,1,0:T(8,128)(2,1)S(1)}, f32[2,32,4096]{2,1,0:T(8,12...) custom-call(s32[3]{0:T(128)S(1)} %pad_add_fusion.place, bf16[2048,4096]{1,0:T(8,128)(2,1)} %bitcast.122, ...), custom_call_target="tpu_custom_call" | custom-call | flops 17179869184 | tf_op jit(solution)/shard_map/load/pallas_call | solution.py:24
  17.6 3.1 %collective-permute-start.1 = (f16[48,1024]{1,0:T(8,128)(2,1)S(1)}, f16[48,1024]{1,0:T(8,128)(2,1)S(1)}, u32[]{:S(2)}, u32[]{:S(2)}) collective-permute-start(f16[48,1024]{1,0:T(8,128)(2,1)S(1)} %fusion.9), channel_id=1, source_target_pairs={{0,2},{1,3},{2,0},{3,1},{4,6},{5,7},{6,4},{7,5},{8,10},{9,11},{10,... | collective-permute-start | bytes 294920 | tf_op jit(solution)/shard_map/ppermute | solution.py:175
  20.8 3.3 %collective-permute-done.1 = f16[48,1024]{1,0:T(8,128)(2,1)S(1)} collective-permute-done((f16[48,1024]{1,0:T(8,128)(2,1)S(1)}, f16[48,1024]{1,0:T(8,128)(2,1)S(1)}, u32[]{:S(2)}, u32[]{:S(2)}) %collective-permute-start.1) | collective-permute-done | bytes 98336 | tf_op jit(solution)/shard_map/ppermute | solution.py:175
  24.1 3.0 %collective-permute-start.2 = (f16[48,1024]{1,0:T(8,128)(2,1)S(1)}, f16[48,1024]{1,0:T(8,128)(2,1)S(1)}, u32[]{:S(2)}, u32[]{:S(2)}) collective-permute-start(f16[48,1024]{1,0:T(8,128)(2,1)S(1)} %fusion), channel_id=1, source_target_pairs={{0,4},{1,5},{2,6},{3,7},{4,0},{5,1},{6,2},{7,3},{8,12},{9,13},{10,... | collective-permute-start | bytes 294920 | tf_op jit(solution)/shard_map/ppermute | solution.py:175
  29.8 3.1 %collective-permute-start.7 = (f16[32,1024]{1,0:T(8,128)(2,1)S(1)}, f16[32,1024]{1,0:T(8,128)(2,1)S(1)}, u32[]{:S(2)}, u32[]{:S(2)}) collective-permute-start(f16[32,1024]{1,0:T(8,128)(2,1)S(1)} %convert_element_type.267), channel_id=1, source_target_pairs={{0,4},{1,5},{2,6},{3,7},{4,0},{5,1},{6,2},{7,3},{8,12},{9,13},{10,... | collective-permute-start | bytes 196616 | tf_op jit(solution)/shard_map/ppermute | solution.py:175
  33.1 1.7 %spread_first.8.so_far = f32[48,4096]{1,0:T(8,128)S(1)} custom-call(s32[1]{0:T(128)} %bitcast.1.place, bf16[48,1024]{1,0:T(8,128)(2,1)S(1)} %concatenate.10.residue, bf16[2048,4096]{1,0:T(8,128)(2,1)S(1)} %get-tuple-element.34.matrix), custom_call_target="tpu_custom_call" | custom-call | flops 8589934592 | tf_op jit(solution)/shard_map/spread_first/pallas_call | solution.py:24
  35.2 1.7 %spread_last.8 = (f32[32,4096]{1,0:T(8,128)S(1)}, f32[1,4096]{1,0:T(1,128)S(1)}) custom-call(s32[1]{0:T(128)} %bitcast.2.place, bf16[48,1024]{1,0:T(8,128)(2,1)S(1)} %collective-permute-done.3.residue, f32[48,4096]{1,0:T(8,128)S(1)} %spread_first.8.so_far, f32[32,4096]{1,0:T(8,128)S(1)} %get-tuple-element.106.volume, ...), custom_call_target="tpu_custom_call" | custom-call | flops 8589934592 | tf_op jit(solution)/shard_map/spread_last/pallas_call | solution.py:24
  37.0 2.8 %collective-permute-start.4 = (f16[32,4096]{1,0:T(8,128)(2,1)S(1)}, f16[32,4096]{1,0:T(8,128)(2,1)S(1)}, u32[]{:S(2)}, u32[]{:S(2)}) collective-permute-start(f16[32,4096]{1,0:T(8,128)(2,1)S(1)} %convert_element_type.261), channel_id=1, source_target_pairs={{0,8},{8,16},{16,24},{24,0},{1,9},{9,17},{17,25},{25,1},{2,10},{10... | collective-permute-start | bytes 786440 | tf_op jit(solution)/shard_map/ppermute | solution.py:170
  41.7 1.7 %spread_last.9 = f32[32,4096]{1,0:T(8,128)S(1)} custom-call(s32[1]{0:T(128)} %bitcast.2.place, bf16[32,1024]{1,0:T(8,128)(2,1)S(1)} %collective-permute-done.8.residue, f32[32,4096]{1,0:T(8,128)S(1)} %spread_first.9.so_far, f32[32,4096]{1,0:T(8,128)S(1)} %get-tuple-element.105.volume, f32[1,4096]{1,0:T(1,128)S(1)} %get-tuple-element.38.column, ...), custom_call_target="tpu_custom_call" | custom-call | flops 8589934592 | tf_op jit(solution)/shard_map/spread_last/pallas_call | solution.py:24
  43.4 1.7 %collective-permute-start.15 = (f16[32,4096]{1,0:T(8,128)(2,1)S(1)}, f16[32,4096]{1,0:T(8,128)(2,1)S(1)}, u32[]{:S(2)}, u32[]{:S(2)}) collective-permute-start(f16[32,4096]{1,0:T(8,128)(2,1)S(1)} %convert_element_type.270), channel_id=1, source_target_pairs={{0,8},{8,16},{16,24},{24,0},{1,9},{9,17},{17,25},{25,1},{2,10},{10... | collective-permute-start | bytes 786440 | tf_op jit(solution)/shard_map/ppermute | solution.py:170
  49.8 4.4 %collective-permute-start.12 = (f16[32,1024]{1,0:T(8,128)(2,1)S(1)}, f16[32,1024]{1,0:T(8,128)(2,1)S(1)}, u32[]{:S(2)}, u32[]{:S(2)}) collective-permute-start(f16[32,1024]{1,0:T(8,128)(2,1)S(1)} %fusion.3), channel_id=1, source_target_pairs={{0,6},{1,7},{2,4},{3,5},{4,2},{5,3},{6,0},{7,1},{8,14},{9,15},{10,... | collective-permute-start | bytes 196616 | tf_op jit(solution)/shard_map/ppermute | solution.py:175
  58.1 2.5 %collective-permute-done.11 = f16[32,1024]{1,0:T(8,128)(2,1)S(1)} collective-permute-done((f16[32,1024]{1,0:T(8,128)(2,1)S(1)}, f16[32,1024]{1,0:T(8,128)(2,1)S(1)}, u32[]{:S(2)}, u32[]{:S(2)}) %collective-permute-start.11) | collective-permute-done | bytes 65568 | tf_op jit(solution)/shard_map/ppermute | solution.py:175
  62.6 1.7 %collective-permute-start.19 = (f16[32,1024]{1,0:T(8,128)(2,1)S(1)}, f16[32,1024]{1,0:T(8,128)(2,1)S(1)}, u32[]{:S(2)}, u32[]{:S(2)}) collective-permute-start(f16[32,1024]{1,0:T(8,128)(2,1)S(1)} %fusion.4), channel_id=1, source_target_pairs={{0,6},{1,7},{2,4},{3,5},{4,2},{5,3},{6,0},{7,1},{8,14},{9,15},{10,... | collective-permute-start | bytes 196616 | tf_op jit(solution)/shard_map/ppermute | solution.py:175
  64.5 2.6 %collective-permute-start.17 = (f16[32,1024]{1,0:T(8,128)(2,1)S(1)}, f16[32,1024]{1,0:T(8,128)(2,1)S(1)}, u32[]{:S(2)}, u32[]{:S(2)}) collective-permute-start(f16[32,1024]{1,0:T(8,128)(2,1)S(1)} %fusion.4), channel_id=1, source_target_pairs={{0,2},{1,3},{2,0},{3,1},{4,6},{5,7},{6,4},{7,5},{8,10},{9,11},{10,... | collective-permute-start | bytes 196616 | tf_op jit(solution)/shard_map/ppermute | solution.py:175
  67.1 1.7 %spread_last.10 = f32[32,4096]{1,0:T(8,128)S(1)} custom-call(s32[1]{0:T(128)} %bitcast.2.place, bf16[32,1024]{1,0:T(8,128)(2,1)S(1)} %collective-permute-done.13.residue, f32[32,4096]{1,0:T(8,128)S(1)} %spread_first.10.so_far, f32[32,4096]{1,0:T(8,128)S(1)} %get-tuple-element.121.volume, f32[1,4096]{1,0:T(1,128)S(1)} %get-tuple-element.38.column, ...), custom_call_target="tpu_custom_call" | custom-call | flops 8589934592 | tf_op jit(solution)/shard_map/spread_last/pallas_call | solution.py:24
  69.8 1.9 %collective-permute-done.18 = f16[32,1024]{1,0:T(8,128)(2,1)S(1)} collective-permute-done((f16[32,1024]{1,0:T(8,128)(2,1)S(1)}, f16[32,1024]{1,0:T(8,128)(2,1)S(1)}, u32[]{:S(2)}, u32[]{:S(2)}) %collective-permute-start.18) | collective-permute-done | bytes 65568 | tf_op jit(solution)/shard_map/ppermute | solution.py:175
  73.6 1.7 %spread_last.11 = f32[32,4096]{1,0:T(8,128)S(1)} custom-call(s32[1]{0:T(128)} %bitcast.2.place, bf16[32,1024]{1,0:T(8,128)(2,1)S(1)} %collective-permute-done.20.residue, f32[32,4096]{1,0:T(8,128)S(1)} %spread_first.11.so_far, f32[32,4096]{1,0:T(8,128)S(1)} %get-tuple-element.119.volume, f32[1,4096]{1,0:T(1,128)S(1)} %get-tuple-element.38.column, ...), custom_call_target="tpu_custom_call" | custom-call | flops 8589934592 | tf_op jit(solution)/shard_map/spread_last/pallas_call | solution.py:24
  80.9 1.7 %collective-permute-start.24 = (f16[32,1024]{1,0:T(8,128)(2,1)S(1)}, f16[32,1024]{1,0:T(8,128)(2,1)S(1)}, u32[]{:S(2)}, u32[]{:S(2)}) collective-permute-start(f16[32,1024]{1,0:T(8,128)(2,1)S(1)} %fusion.5), channel_id=1, source_target_pairs={{0,6},{1,7},{2,4},{3,5},{4,2},{5,3},{6,0},{7,1},{8,14},{9,15},{10,... | collective-permute-start | bytes 196616 | tf_op jit(solution)/shard_map/ppermute | solution.py:175
  82.7 2.6 %collective-permute-start.22 = (f16[32,1024]{1,0:T(8,128)(2,1)S(1)}, f16[32,1024]{1,0:T(8,128)(2,1)S(1)}, u32[]{:S(2)}, u32[]{:S(2)}) collective-permute-start(f16[32,1024]{1,0:T(8,128)(2,1)S(1)} %fusion.5), channel_id=1, source_target_pairs={{0,2},{1,3},{2,0},{3,1},{4,6},{5,7},{6,4},{7,5},{8,10},{9,11},{10,... | collective-permute-start | bytes 196616 | tf_op jit(solution)/shard_map/ppermute | solution.py:175
  92.0 1.7 %collective-permute-start.31 = (f16[32,1024]{1,0:T(8,128)(2,1)S(1)}, f16[32,1024]{1,0:T(8,128)(2,1)S(1)}, u32[]{:S(2)}, u32[]{:S(2)}) collective-permute-start(f16[32,1024]{1,0:T(8,128)(2,1)S(1)} %fusion.6), channel_id=1, source_target_pairs={{0,6},{1,7},{2,4},{3,5},{4,2},{5,3},{6,0},{7,1},{8,14},{9,15},{10,... | collective-permute-start | bytes 196616 | tf_op jit(solution)/shard_map/ppermute | solution.py:175
  93.7 2.7 %collective-permute-start.29 = (f16[32,1024]{1,0:T(8,128)(2,1)S(1)}, f16[32,1024]{1,0:T(8,128)(2,1)S(1)}, u32[]{:S(2)}, u32[]{:S(2)}) collective-permute-start(f16[32,1024]{1,0:T(8,128)(2,1)S(1)} %fusion.6), channel_id=1, source_target_pairs={{0,2},{1,3},{2,0},{3,1},{4,6},{5,7},{6,4},{7,5},{8,10},{9,11},{10,... | collective-permute-start | bytes 196616 | tf_op jit(solution)/shard_map/ppermute | solution.py:175
  96.5 1.7 %spread_last.12 = f32[32,4096]{1,0:T(8,128)S(1)} custom-call(s32[1]{0:T(128)} %bitcast.2.place, bf16[32,1024]{1,0:T(8,128)(2,1)S(1)} %collective-permute-done.25.residue, f32[32,4096]{1,0:T(8,128)S(1)} %spread_first.12.so_far, f32[32,4096]{1,0:T(8,128)S(1)} %get-tuple-element.117.volume, f32[1,4096]{1,0:T(1,128)S(1)} %get-tuple-element.38.column, ...), custom_call_target="tpu_custom_call" | custom-call | flops 8589934592 | tf_op jit(solution)/shard_map/spread_last/pallas_call | solution.py:24
  99.3 1.8 %collective-permute-done.30 = f16[32,1024]{1,0:T(8,128)(2,1)S(1)} collective-permute-done((f16[32,1024]{1,0:T(8,128)(2,1)S(1)}, f16[32,1024]{1,0:T(8,128)(2,1)S(1)}, u32[]{:S(2)}, u32[]{:S(2)}) %collective-permute-start.30) | collective-permute-done | bytes 65568 | tf_op jit(solution)/shard_map/ppermute | solution.py:175
  103.1 1.7 %spread_last.13 = f32[32,4096]{1,0:T(8,128)S(1)} custom-call(s32[1]{0:T(128)} %bitcast.2.place, bf16[32,1024]{1,0:T(8,128)(2,1)S(1)} %collective-permute-done.32.residue, f32[32,4096]{1,0:T(8,128)S(1)} %spread_first.13.so_far, f32[32,4096]{1,0:T(8,128)S(1)} %get-tuple-element.115.volume, f32[1,4096]{1,0:T(1,128)S(1)} %get-tuple-element.38.column, ...), custom_call_target="tpu_custom_call" | custom-call | flops 8589934592 | tf_op jit(solution)/shard_map/spread_last/pallas_call | solution.py:24
  110.3 1.7 %collective-permute-start.36 = (f16[32,1024]{1,0:T(8,128)(2,1)S(1)}, f16[32,1024]{1,0:T(8,128)(2,1)S(1)}, u32[]{:S(2)}, u32[]{:S(2)}) collective-permute-start(f16[32,1024]{1,0:T(8,128)(2,1)S(1)} %fusion.7), channel_id=1, source_target_pairs={{0,6},{1,7},{2,4},{3,5},{4,2},{5,3},{6,0},{7,1},{8,14},{9,15},{10,... | collective-permute-start | bytes 196616 | tf_op jit(solution)/shard_map/ppermute | solution.py:175
  112.1 2.6 %collective-permute-start.34 = (f16[32,1024]{1,0:T(8,128)(2,1)S(1)}, f16[32,1024]{1,0:T(8,128)(2,1)S(1)}, u32[]{:S(2)}, u32[]{:S(2)}) collective-permute-start(f16[32,1024]{1,0:T(8,128)(2,1)S(1)} %fusion.7), channel_id=1, source_target_pairs={{0,2},{1,3},{2,0},{3,1},{4,6},{5,7},{6,4},{7,5},{8,10},{9,11},{10,... | collective-permute-start | bytes 196616 | tf_op jit(solution)/shard_map/ppermute | solution.py:175
  121.4 1.7 %collective-permute-start.46 = (f16[32,1024]{1,0:T(8,128)(2,1)S(1)}, f16[32,1024]{1,0:T(8,128)(2,1)S(1)}, u32[]{:S(2)}, u32[]{:S(2)}) collective-permute-start(f16[32,1024]{1,0:T(8,128)(2,1)S(1)} %fusion.8), channel_id=1, source_target_pairs={{0,6},{1,7},{2,4},{3,5},{4,2},{5,3},{6,0},{7,1},{8,14},{9,15},{10,... | collective-permute-start | bytes 196616 | tf_op jit(solution)/shard_map/ppermute | solution.py:175
  123.1 2.7 %collective-permute-start.44 = (f16[32,1024]{1,0:T(8,128)(2,1)S(1)}, f16[32,1024]{1,0:T(8,128)(2,1)S(1)}, u32[]{:S(2)}, u32[]{:S(2)}) collective-permute-start(f16[32,1024]{1,0:T(8,128)(2,1)S(1)} %fusion.8), channel_id=1, source_target_pairs={{0,2},{1,3},{2,0},{3,1},{4,6},{5,7},{6,4},{7,5},{8,10},{9,11},{10,... | collective-permute-start | bytes 196616 | tf_op jit(solution)/shard_map/ppermute | solution.py:175
  125.9 1.7 %spread_last.14.before = f32[32,4096]{1,0:T(8,128)S(1)} custom-call(s32[1]{0:T(128)} %bitcast.2.place, bf16[32,1024]{1,0:T(8,128)(2,1)S(1)} %collective-permute-done.37.residue, f32[32,4096]{1,0:T(8,128)S(1)} %spread_first.14.so_far, f32[32,4096]{1,0:T(8,128)S(1)} %get-tuple-element.113.volume, f32[1,4096]{1,0:T(1,128)S(1)} %get-tuple-element.38.column, ...), custom_call_target="tpu_custom_call" | custom-call | flops 8589934592 | tf_op jit(solution)/shard_map/spread_last/pallas_call | solution.py:24
  132.4 1.7 %spread_last.15 = f32[32,4096]{1,0:T(8,128)S(1)} custom-call(s32[1]{0:T(128)} %bitcast.2.place, bf16[32,1024]{1,0:T(8,128)(2,1)S(1)} %collective-permute-done.47.residue, f32[32,4096]{1,0:T(8,128)S(1)} %spread_first.15.so_far, f32[32,4096]{1,0:T(8,128)S(1)} %get-tuple-element.111.volume, f32[1,4096]{1,0:T(1,128)S(1)} %get-tuple-element.38.column, ...), custom_call_target="tpu_custom_call" | custom-call | flops 8589934592 | tf_op jit(solution)/shard_map/spread_last/pallas_call | solution.py:24
  139.5 3.8 %collective-permute-done.50 = bf16[32,4096]{1,0:T(8,128)(2,1)S(1)} collective-permute-done((bf16[32,4096]{1,0:T(8,128)(2,1)S(1)}, bf16[32,4096]{1,0:T(8,128)(2,1)S(1)}, u32[]{:S(2)}, u32[]{:S(2)}) %collective-permute-start.50) | collective-permute-done | bytes 262176 | tf_op jit(solution)/shard_map/ppermute | solution.py:175
  147.7 2.3 %collective-permute-done.49 = bf16[32,2048]{1,0:T(8,128)(2,1)S(1)} collective-permute-done((bf16[32,2048]{1,0:T(8,128)(2,1)S(1)}, bf16[32,2048]{1,0:T(8,128)(2,1)S(1)}, u32[]{:S(2)}, u32[]{:S(2)}) %collective-permute-start.49) | collective-permute-done | bytes 131104 | tf_op jit(solution)/shard_map/ppermute | solution.py:175
  (206 shorter events, 70.3 us)
Async XLA Ops:
  11.6 9.1 %collective-permute-start.5 = (f16[32,1024]{1,0:T(8,128)(2,1)S(1)}, f16[32,1024]{1,0:T(8,128)(2,1)S(1)}, u32[]{:S(2)}, u32[]{:S(2)}) collective-permute-start(f16[32,1024]{1,0:T(8,128)(2,1)S(1)} %multiply_convert_fusion.13), channel_id=1, source_target_pairs={{0,1},{1,0},{2,3},{3,2},{4,5},{5,4},{6,7},{7,6},{8,9},{9,8},{10,11... | collective-permute-start | bytes 196616 | tf_op jit(solution)/shard_map/ppermute | solution.py:175
  20.7 7.6 %collective-permute-start.6 = (f16[32,1024]{1,0:T(8,128)(2,1)S(1)}, f16[32,1024]{1,0:T(8,128)(2,1)S(1)}, u32[]{:S(2)}, u32[]{:S(2)}) collective-permute-start(f16[32,1024]{1,0:T(8,128)(2,1)S(1)} %get-tuple-element.95), channel_id=1, source_target_pairs={{0,2},{1,3},{2,0},{3,1},{4,6},{5,7},{6,4},{7,5},{8,10},{9,11},{10,... | collective-permute-start | bytes 196616 | tf_op jit(solution)/shard_map/ppermute | solution.py:175
  37.0 9.3 %collective-permute-start.4 = (f16[32,4096]{1,0:T(8,128)(2,1)S(1)}, f16[32,4096]{1,0:T(8,128)(2,1)S(1)}, u32[]{:S(2)}, u32[]{:S(2)}) collective-permute-start(f16[32,4096]{1,0:T(8,128)(2,1)S(1)} %convert_element_type.261), channel_id=1, source_target_pairs={{0,8},{8,16},{16,24},{24,0},{1,9},{9,17},{17,25},{25,1},{2,10},{10... | collective-permute-start | bytes 786440 | tf_op jit(solution)/shard_map/ppermute | solution.py:170
  43.4 11.4 %collective-permute-start.15 = (f16[32,4096]{1,0:T(8,128)(2,1)S(1)}, f16[32,4096]{1,0:T(8,128)(2,1)S(1)}, u32[]{:S(2)}, u32[]{:S(2)}) collective-permute-start(f16[32,4096]{1,0:T(8,128)(2,1)S(1)} %convert_element_type.270), channel_id=1, source_target_pairs={{0,8},{8,16},{16,24},{24,0},{1,9},{9,17},{17,25},{25,1},{2,10},{10... | collective-permute-start | bytes 786440 | tf_op jit(solution)/shard_map/ppermute | solution.py:170
  49.8 8.3 %collective-permute-start.12 = (f16[32,1024]{1,0:T(8,128)(2,1)S(1)}, f16[32,1024]{1,0:T(8,128)(2,1)S(1)}, u32[]{:S(2)}, u32[]{:S(2)}) collective-permute-start(f16[32,1024]{1,0:T(8,128)(2,1)S(1)} %fusion.3), channel_id=1, source_target_pairs={{0,6},{1,7},{2,4},{3,5},{4,2},{5,3},{6,0},{7,1},{8,14},{9,15},{10,... | collective-permute-start | bytes 196616 | tf_op jit(solution)/shard_map/ppermute | solution.py:175
  54.2 6.5 %collective-permute-start.11 = (f16[32,1024]{1,0:T(8,128)(2,1)S(1)}, f16[32,1024]{1,0:T(8,128)(2,1)S(1)}, u32[]{:S(2)}, u32[]{:S(2)}) collective-permute-start(f16[32,1024]{1,0:T(8,128)(2,1)S(1)} %fusion.3), channel_id=1, source_target_pairs={{0,4},{1,5},{2,6},{3,7},{4,0},{5,1},{6,2},{7,3},{8,12},{9,13},{10,... | collective-permute-start | bytes 196616 | tf_op jit(solution)/shard_map/ppermute | solution.py:175
  62.6 7.2 %collective-permute-start.19 = (f16[32,1024]{1,0:T(8,128)(2,1)S(1)}, f16[32,1024]{1,0:T(8,128)(2,1)S(1)}, u32[]{:S(2)}, u32[]{:S(2)}) collective-permute-start(f16[32,1024]{1,0:T(8,128)(2,1)S(1)} %fusion.4), channel_id=1, source_target_pairs={{0,6},{1,7},{2,4},{3,5},{4,2},{5,3},{6,0},{7,1},{8,14},{9,15},{10,... | collective-permute-start | bytes 196616 | tf_op jit(solution)/shard_map/ppermute | solution.py:175
  64.3 7.4 %collective-permute-start.18 = (f16[32,1024]{1,0:T(8,128)(2,1)S(1)}, f16[32,1024]{1,0:T(8,128)(2,1)S(1)}, u32[]{:S(2)}, u32[]{:S(2)}) collective-permute-start(f16[32,1024]{1,0:T(8,128)(2,1)S(1)} %fusion.4), channel_id=1, source_target_pairs={{0,4},{1,5},{2,6},{3,7},{4,0},{5,1},{6,2},{7,3},{8,12},{9,13},{10,... | collective-permute-start | bytes 196616 | tf_op jit(solution)/shard_map/ppermute | solution.py:175
  64.5 7.3 %collective-permute-start.17 = (f16[32,1024]{1,0:T(8,128)(2,1)S(1)}, f16[32,1024]{1,0:T(8,128)(2,1)S(1)}, u32[]{:S(2)}, u32[]{:S(2)}) collective-permute-start(f16[32,1024]{1,0:T(8,128)(2,1)S(1)} %fusion.4), channel_id=1, source_target_pairs={{0,2},{1,3},{2,0},{3,1},{4,6},{5,7},{6,4},{7,5},{8,10},{9,11},{10,... | collective-permute-start | bytes 196616 | tf_op jit(solution)/shard_map/ppermute | solution.py:175
  68.8 8.8 %collective-permute-start.14 = (f16[32,4096]{1,0:T(8,128)(2,1)S(1)}, f16[32,4096]{1,0:T(8,128)(2,1)S(1)}, u32[]{:S(2)}, u32[]{:S(2)}) collective-permute-start(f16[32,4096]{1,0:T(8,128)(2,1)S(1)} %convert_element_type.280), channel_id=1, source_target_pairs={{0,8},{8,16},{16,24},{24,0},{1,9},{9,17},{17,25},{25,1},{2,10},{10... | collective-permute-start | bytes 786440 | tf_op jit(solution)/shard_map/ppermute | solution.py:170
  75.4 9.9 %collective-permute-start.27 = (f16[32,4096]{1,0:T(8,128)(2,1)S(1)}, f16[32,4096]{1,0:T(8,128)(2,1)S(1)}, u32[]{:S(2)}, u32[]{:S(2)}) collective-permute-start(f16[32,4096]{1,0:T(8,128)(2,1)S(1)} %convert_element_type.290), channel_id=1, source_target_pairs={{0,8},{8,16},{16,24},{24,0},{1,9},{9,17},{17,25},{25,1},{2,10},{10... | collective-permute-start | bytes 786440 | tf_op jit(solution)/shard_map/ppermute | solution.py:170
  80.9 7.8 %collective-permute-start.24 = (f16[32,1024]{1,0:T(8,128)(2,1)S(1)}, f16[32,1024]{1,0:T(8,128)(2,1)S(1)}, u32[]{:S(2)}, u32[]{:S(2)}) collective-permute-start(f16[32,1024]{1,0:T(8,128)(2,1)S(1)} %fusion.5), channel_id=1, source_target_pairs={{0,6},{1,7},{2,4},{3,5},{4,2},{5,3},{6,0},{7,1},{8,14},{9,15},{10,... | collective-permute-start | bytes 196616 | tf_op jit(solution)/shard_map/ppermute | solution.py:175
  82.6 7.5 %collective-permute-start.23 = (f16[32,1024]{1,0:T(8,128)(2,1)S(1)}, f16[32,1024]{1,0:T(8,128)(2,1)S(1)}, u32[]{:S(2)}, u32[]{:S(2)}) collective-permute-start(f16[32,1024]{1,0:T(8,128)(2,1)S(1)} %fusion.5), channel_id=1, source_target_pairs={{0,4},{1,5},{2,6},{3,7},{4,0},{5,1},{6,2},{7,3},{8,12},{9,13},{10,... | collective-permute-start | bytes 196616 | tf_op jit(solution)/shard_map/ppermute | solution.py:175
  82.7 7.3 %collective-permute-start.22 = (f16[32,1024]{1,0:T(8,128)(2,1)S(1)}, f16[32,1024]{1,0:T(8,128)(2,1)S(1)}, u32[]{:S(2)}, u32[]{:S(2)}) collective-permute-start(f16[32,1024]{1,0:T(8,128)(2,1)S(1)} %fusion.5), channel_id=1, source_target_pairs={{0,2},{1,3},{2,0},{3,1},{4,6},{5,7},{6,4},{7,5},{8,10},{9,11},{10,... | collective-permute-start | bytes 196616 | tf_op jit(solution)/shard_map/ppermute | solution.py:175
  92.0 7.4 %collective-permute-start.31 = (f16[32,1024]{1,0:T(8,128)(2,1)S(1)}, f16[32,1024]{1,0:T(8,128)(2,1)S(1)}, u32[]{:S(2)}, u32[]{:S(2)}) collective-permute-start(f16[32,1024]{1,0:T(8,128)(2,1)S(1)} %fusion.6), channel_id=1, source_target_pairs={{0,6},{1,7},{2,4},{3,5},{4,2},{5,3},{6,0},{7,1},{8,14},{9,15},{10,... | collective-permute-start | bytes 196616 | tf_op jit(solution)/shard_map/ppermute | solution.py:175
  93.7 7.4 %collective-permute-start.30 = (f16[32,1024]{1,0:T(8,128)(2,1)S(1)}, f16[32,1024]{1,0:T(8,128)(2,1)S(1)}, u32[]{:S(2)}, u32[]{:S(2)}) collective-permute-start(f16[32,1024]{1,0:T(8,128)(2,1)S(1)} %fusion.6), channel_id=1, source_target_pairs={{0,4},{1,5},{2,6},{3,7},{4,0},{5,1},{6,2},{7,3},{8,12},{9,13},{10,... | collective-permute-start | bytes 196616 | tf_op jit(solution)/shard_map/ppermute | solution.py:175
  93.7 7.4 %collective-permute-start.29 = (f16[32,1024]{1,0:T(8,128)(2,1)S(1)}, f16[32,1024]{1,0:T(8,128)(2,1)S(1)}, u32[]{:S(2)}, u32[]{:S(2)}) collective-permute-start(f16[32,1024]{1,0:T(8,128)(2,1)S(1)} %fusion.6), channel_id=1, source_target_pairs={{0,2},{1,3},{2,0},{3,1},{4,6},{5,7},{6,4},{7,5},{8,10},{9,11},{10,... | collective-permute-start | bytes 196616 | tf_op jit(solution)/shard_map/ppermute | solution.py:175
  98.2 8.8 %collective-permute-start.26 = (f16[32,4096]{1,0:T(8,128)(2,1)S(1)}, f16[32,4096]{1,0:T(8,128)(2,1)S(1)}, u32[]{:S(2)}, u32[]{:S(2)}) collective-permute-start(f16[32,4096]{1,0:T(8,128)(2,1)S(1)} %convert_element_type.300), channel_id=1, source_target_pairs={{0,8},{8,16},{16,24},{24,0},{1,9},{9,17},{17,25},{25,1},{2,10},{10... | collective-permute-start | bytes 786440 | tf_op jit(solution)/shard_map/ppermute | solution.py:170
  104.9 9.9 %collective-permute-start.42 = (f16[32,4096]{1,0:T(8,128)(2,1)S(1)}, f16[32,4096]{1,0:T(8,128)(2,1)S(1)}, u32[]{:S(2)}, u32[]{:S(2)}) collective-permute-start(f16[32,4096]{1,0:T(8,128)(2,1)S(1)} %convert_element_type.310), channel_id=1, source_target_pairs={{0,8},{8,16},{16,24},{24,0},{1,9},{9,17},{17,25},{25,1},{2,10},{10... | collective-permute-start | bytes 786440 | tf_op jit(solution)/shard_map/ppermute | solution.py:170
  110.3 7.8 %collective-permute-start.36 = (f16[32,1024]{1,0:T(8,128)(2,1)S(1)}, f16[32,1024]{1,0:T(8,128)(2,1)S(1)}, u32[]{:S(2)}, u32[]{:S(2)}) collective-permute-start(f16[32,1024]{1,0:T(8,128)(2,1)S(1)} %fusion.7), channel_id=1, source_target_pairs={{0,6},{1,7},{2,4},{3,5},{4,2},{5,3},{6,0},{7,1},{8,14},{9,15},{10,... | collective-permute-start | bytes 196616 | tf_op jit(solution)/shard_map/ppermute | solution.py:175
  112.0 7.5 %collective-permute-start.35 = (f16[32,1024]{1,0:T(8,128)(2,1)S(1)}, f16[32,1024]{1,0:T(8,128)(2,1)S(1)}, u32[]{:S(2)}, u32[]{:S(2)}) collective-permute-start(f16[32,1024]{1,0:T(8,128)(2,1)S(1)} %fusion.7), channel_id=1, source_target_pairs={{0,4},{1,5},{2,6},{3,7},{4,0},{5,1},{6,2},{7,3},{8,12},{9,13},{10,... | collective-permute-start | bytes 196616 | tf_op jit(solution)/shard_map/ppermute | solution.py:175
  112.1 7.3 %collective-permute-start.34 = (f16[32,1024]{1,0:T(8,128)(2,1)S(1)}, f16[32,1024]{1,0:T(8,128)(2,1)S(1)}, u32[]{:S(2)}, u32[]{:S(2)}) collective-permute-start(f16[32,1024]{1,0:T(8,128)(2,1)S(1)} %fusion.7), channel_id=1, source_target_pairs={{0,2},{1,3},{2,0},{3,1},{4,6},{5,7},{6,4},{7,5},{8,10},{9,11},{10,... | collective-permute-start | bytes 196616 | tf_op jit(solution)/shard_map/ppermute | solution.py:175
  121.4 7.9 %collective-permute-start.46 = (f16[32,1024]{1,0:T(8,128)(2,1)S(1)}, f16[32,1024]{1,0:T(8,128)(2,1)S(1)}, u32[]{:S(2)}, u32[]{:S(2)}) collective-permute-start(f16[32,1024]{1,0:T(8,128)(2,1)S(1)} %fusion.8), channel_id=1, source_target_pairs={{0,6},{1,7},{2,4},{3,5},{4,2},{5,3},{6,0},{7,1},{8,14},{9,15},{10,... | collective-permute-start | bytes 196616 | tf_op jit(solution)/shard_map/ppermute | solution.py:175
  123.1 7.4 %collective-permute-start.45 = (f16[32,1024]{1,0:T(8,128)(2,1)S(1)}, f16[32,1024]{1,0:T(8,128)(2,1)S(1)}, u32[]{:S(2)}, u32[]{:S(2)}) collective-permute-start(f16[32,1024]{1,0:T(8,128)(2,1)S(1)} %fusion.8), channel_id=1, source_target_pairs={{0,4},{1,5},{2,6},{3,7},{4,0},{5,1},{6,2},{7,3},{8,12},{9,13},{10,... | collective-permute-start | bytes 196616 | tf_op jit(solution)/shard_map/ppermute | solution.py:175
  123.1 7.4 %collective-permute-start.44 = (f16[32,1024]{1,0:T(8,128)(2,1)S(1)}, f16[32,1024]{1,0:T(8,128)(2,1)S(1)}, u32[]{:S(2)}, u32[]{:S(2)}) collective-permute-start(f16[32,1024]{1,0:T(8,128)(2,1)S(1)} %fusion.8), channel_id=1, source_target_pairs={{0,2},{1,3},{2,0},{3,1},{4,6},{5,7},{6,4},{7,5},{8,10},{9,11},{10,... | collective-permute-start | bytes 196616 | tf_op jit(solution)/shard_map/ppermute | solution.py:175
  127.6 10.8 %collective-permute-start.40 = (bf16[32,4096]{1,0:T(8,128)(2,1)S(1)}, bf16[32,4096]{1,0:T(8,128)(2,1)S(1)}, u32[]{:S(2)}, u32[]{:S(2)}) collective-permute-start(bf16[32,4096]{1,0:T(8,128)(2,1)S(1)} %convert_element_type.320), channel_id=1, source_target_pairs={{0,8},{8,0},{16,24},{24,16},{1,9},{9,1},{17,25},{25,17},{2,10},{10... | collective-permute-start | bytes 786440 | tf_op jit(solution)/shard_map/ppermute | solution.py:175
  128.8 7.6 %collective-permute-start.38 = (bf16[32,4096]{1,0:T(8,128)(2,1)S(1)}, bf16[32,4096]{1,0:T(8,128)(2,1)S(1)}, u32[]{:S(2)}, u32[]{:S(2)}) collective-permute-start(bf16[32,4096]{1,0:T(8,128)(2,1)S(1)} %convert_element_type.320), channel_id=1, source_target_pairs={{0,16},{8,24},{16,0},{24,8},{1,17},{9,25},{17,1},{25,9},{2,18},{10... | collective-permute-start | bytes 786440 | tf_op jit(solution)/shard_map/ppermute | solution.py:175
  134.1 9.2 %collective-permute-start.50 = (bf16[32,4096]{1,0:T(8,128)(2,1)S(1)}, bf16[32,4096]{1,0:T(8,128)(2,1)S(1)}, u32[]{:S(2)}, u32[]{:S(2)}) collective-permute-start(bf16[32,4096]{1,0:T(8,128)(2,1)S(1)} %convert_element_type.329), channel_id=1, source_target_pairs={{0,8},{8,0},{16,24},{24,16},{1,9},{9,1},{17,25},{25,17},{2,10},{10... | collective-permute-start | bytes 786440 | tf_op jit(solution)/shard_map/ppermute | solution.py:175
  135.4 9.5 %collective-permute-start.48 = (bf16[32,4096]{1,0:T(8,128)(2,1)S(1)}, bf16[32,4096]{1,0:T(8,128)(2,1)S(1)}, u32[]{:S(2)}, u32[]{:S(2)}) collective-permute-start(bf16[32,4096]{1,0:T(8,128)(2,1)S(1)} %convert_element_type.329), channel_id=1, source_target_pairs={{0,16},{8,24},{16,0},{24,8},{1,17},{9,25},{17,1},{25,9},{2,18},{10... | collective-permute-start | bytes 786440 | tf_op jit(solution)/shard_map/ppermute | solution.py:175
  136.4 9.3 %collective-permute-start.39 = (bf16[32,2048]{1,0:T(8,128)(2,1)S(1)}, bf16[32,2048]{1,0:T(8,128)(2,1)S(1)}, u32[]{:S(2)}, u32[]{:S(2)}) collective-permute-start(bf16[32,2048]{1,0:T(8,128)(2,1)S(1)} %slice.236), channel_id=1, source_target_pairs={{0,8},{8,0},{16,24},{24,16},{1,9},{9,1},{17,25},{25,17},{2,10},{10... | collective-permute-start | bytes 393224 | tf_op jit(solution)/shard_map/ppermute | solution.py:175
  138.4 8.9 %collective-permute-start.41 = (bf16[32,2048]{1,0:T(8,128)(2,1)S(1)}, bf16[32,2048]{1,0:T(8,128)(2,1)S(1)}, u32[]{:S(2)}, u32[]{:S(2)}) collective-permute-start(bf16[32,2048]{1,0:T(8,128)(2,1)S(1)} %slice.237), channel_id=1, source_target_pairs={{0,16},{8,24},{16,0},{24,8},{1,17},{9,25},{17,1},{25,9},{2,18},{10... | collective-permute-start | bytes 393224 | tf_op jit(solution)/shard_map/ppermute | solution.py:175
  143.3 6.7 %collective-permute-start.51 = (bf16[32,2048]{1,0:T(8,128)(2,1)S(1)}, bf16[32,2048]{1,0:T(8,128)(2,1)S(1)}, u32[]{:S(2)}, u32[]{:S(2)}) collective-permute-start(bf16[32,2048]{1,0:T(8,128)(2,1)S(1)} %slice.239), channel_id=1, source_target_pairs={{0,16},{8,24},{16,0},{24,8},{1,17},{9,25},{17,1},{25,9},{2,18},{10... | collective-permute-start | bytes 393224 | tf_op jit(solution)/shard_map/ppermute | solution.py:175
  (35 other events, 144.0 us)

commit v4 on v3

--- a/solution.py
+++ b/solution.py
@@ -136,10 +136,10 @@
     residue[...] = ((target[...] - total[...]) * inverse[...]).astype(BF16)
 
 
-def spread_first(place, residue, matrix, spread):
+def spread_first(parts, place, residue, matrix, spread):
     count = residue.shape[1]
     where = pl.ds(pl.multiple_of(place[0] * count, count), count)
-    step = 2048
+    step = matrix.shape[1] // parts
 
     @pl.loop(0, matrix.shape[1] // step)
     def _(c):
@@ -150,7 +150,7 @@
 def spread_last(first, place, residue, so_far, volume, column, matrix, out, *column_out):
     count = residue.shape[1]
     slices = out.shape[0]
-    step = 2048
+    step = matrix.shape[1] // 2
     where = pl.ds(pl.multiple_of(place[0] * count, count), count)
 
     @pl.loop(0, matrix.shape[1] // step)
@@ -318,7 +318,7 @@
             height = residue.shape[0]
             their_residue = swapped(residue, "tile", 1)
             spread = products(
-                spread_first, shaped((height, voxels)), (own, residue, matrix),
+                functools.partial(spread_first, 1 if 0 < j < 3 else 2), shaped((height, voxels)), (own, residue, matrix),
                 [SM, VM, VM], "spread_first",
             )
             shapes = [shaped((batch, voxels))]

time: 152 us -> 152 us (level)
  no operation moved by 1% of the time
where the time goes in v4:
time: 152 us
  Pallas kernels  61.1 us (40%)
  starting transfers between devices  55.8 us (37%)
  waiting for transfers between devices  27 us (18%)
  other arithmetic  6.26 us (4%)
    pallas_call x35, Pallas kernels, call(): pl.pallas_call(kernel, out_shape=out_shape, in_specs=specs, out_specs=out...  61.1 us
    ppermute x46, starting transfers between devices, swapped(): return lax.ppermute(x, axis, [(i, i ^ bit) for i in range(size)])  46.7 us
    ppermute x46, waiting for transfers between devices, swapped(): return lax.ppermute(x, axis, [(i, i ^ bit) for i in range(size)])  23.9 us
    ppermute x6, starting transfers between devices, passed(): lax.ppermute(x, axis, [(i, (i + distance) % size) for i in range(size)])  9.17 us
    ppermute x6, waiting for transfers between devices, passed(): lax.ppermute(x, axis, [(i, (i + distance) % size) for i in range(size)])  3.08 us
  transfers between devices with their start and end apart: 52, of which 17 were waited for; matrix products, arithmetic and copies ran while one was open for 3% of the time, Pallas kernels for 32%

profile of v4, /device:TPU:0, one launch (start us, length us, event | category | flops | bytes accessed | tf_op | source)
XLA Modules:
  0.0 151.6 jit_solution(8567992979154561112)
XLA Ops:
  0.1 9.9 %load.1 = (bf16[2048,4096]{1,0:T(8,128)(2,1)S(1)}, bf16[4096,2048]{1,0:T(8,128)(2,1)S(1)}, bf16[2,48,4096]{2,1,0:T(8,128)(2,1)S(1)}, f32[2,32,4096]{2,1,0:T(8,12...) custom-call(s32[3]{0:T(128)S(1)} %pad_add_fusion.place, bf16[2048,4096]{1,0:T(8,128)(2,1)} %bitcast.122, ...), custom_call_target="tpu_custom_call" | custom-call | flops 17179869184 | tf_op jit(solution)/shard_map/load/pallas_call | solution.py:24
  17.6 3.1 %collective-permute-start.1 = (f16[48,1024]{1,0:T(8,128)(2,1)S(1)}, f16[48,1024]{1,0:T(8,128)(2,1)S(1)}, u32[]{:S(2)}, u32[]{:S(2)}) collective-permute-start(f16[48,1024]{1,0:T(8,128)(2,1)S(1)} %fusion.9), channel_id=1, source_target_pairs={{0,2},{1,3},{2,0},{3,1},{4,6},{5,7},{6,4},{7,5},{8,10},{9,11},{10,... | collective-permute-start | bytes 294920 | tf_op jit(solution)/shard_map/ppermute | solution.py:175
  20.8 3.3 %collective-permute-done.1 = f16[48,1024]{1,0:T(8,128)(2,1)S(1)} collective-permute-done((f16[48,1024]{1,0:T(8,128)(2,1)S(1)}, f16[48,1024]{1,0:T(8,128)(2,1)S(1)}, u32[]{:S(2)}, u32[]{:S(2)}) %collective-permute-start.1) | collective-permute-done | bytes 98336 | tf_op jit(solution)/shard_map/ppermute | solution.py:175
  24.1 3.0 %collective-permute-start.2 = (f16[48,1024]{1,0:T(8,128)(2,1)S(1)}, f16[48,1024]{1,0:T(8,128)(2,1)S(1)}, u32[]{:S(2)}, u32[]{:S(2)}) collective-permute-start(f16[48,1024]{1,0:T(8,128)(2,1)S(1)} %fusion), channel_id=1, source_target_pairs={{0,4},{1,5},{2,6},{3,7},{4,0},{5,1},{6,2},{7,3},{8,12},{9,13},{10,... | collective-permute-start | bytes 294920 | tf_op jit(solution)/shard_map/ppermute | solution.py:175
  29.8 3.1 %collective-permute-start.7 = (f16[32,1024]{1,0:T(8,128)(2,1)S(1)}, f16[32,1024]{1,0:T(8,128)(2,1)S(1)}, u32[]{:S(2)}, u32[]{:S(2)}) collective-permute-start(f16[32,1024]{1,0:T(8,128)(2,1)S(1)} %convert_element_type.267), channel_id=1, source_target_pairs={{0,4},{1,5},{2,6},{3,7},{4,0},{5,1},{6,2},{7,3},{8,12},{9,13},{10,... | collective-permute-start | bytes 196616 | tf_op jit(solution)/shard_map/ppermute | solution.py:175
  33.1 1.7 %spread_first.8.so_far = f32[48,4096]{1,0:T(8,128)S(1)} custom-call(s32[1]{0:T(128)} %bitcast.1.place, bf16[48,1024]{1,0:T(8,128)(2,1)S(1)} %concatenate.10.residue, bf16[2048,4096]{1,0:T(8,128)(2,1)S(1)} %get-tuple-element.34.matrix), custom_call_target="tpu_custom_call" | custom-call | flops 8589934592 | tf_op jit(solution)/shard_map/spread_first/pallas_call | solution.py:24
  35.2 1.7 %spread_last.8 = (f32[32,4096]{1,0:T(8,128)S(1)}, f32[1,4096]{1,0:T(1,128)S(1)}) custom-call(s32[1]{0:T(128)} %bitcast.2.place, bf16[48,1024]{1,0:T(8,128)(2,1)S(1)} %collective-permute-done.3.residue, f32[48,4096]{1,0:T(8,128)S(1)} %spread_first.8.so_far, f32[32,4096]{1,0:T(8,128)S(1)} %get-tuple-element.106.volume, ...), custom_call_target="tpu_custom_call" | custom-call | flops 8589934592 | tf_op jit(solution)/shard_map/spread_last/pallas_call | solution.py:24
  37.0 2.8 %collective-permute-start.4 = (f16[32,4096]{1,0:T(8,128)(2,1)S(1)}, f16[32,4096]{1,0:T(8,128)(2,1)S(1)}, u32[]{:S(2)}, u32[]{:S(2)}) collective-permute-start(f16[32,4096]{1,0:T(8,128)(2,1)S(1)} %convert_element_type.261), channel_id=1, source_target_pairs={{0,8},{8,16},{16,24},{24,0},{1,9},{9,17},{17,25},{25,1},{2,10},{10... | collective-permute-start | bytes 786440 | tf_op jit(solution)/shard_map/ppermute | solution.py:170
  41.7 1.7 %spread_last.9 = f32[32,4096]{1,0:T(8,128)S(1)} custom-call(s32[1]{0:T(128)} %bitcast.2.place, bf16[32,1024]{1,0:T(8,128)(2,1)S(1)} %collective-permute-done.8.residue, f32[32,4096]{1,0:T(8,128)S(1)} %spread_first.9.so_far, f32[32,4096]{1,0:T(8,128)S(1)} %get-tuple-element.105.volume, f32[1,4096]{1,0:T(1,128)S(1)} %get-tuple-element.38.column, ...), custom_call_target="tpu_custom_call" | custom-call | flops 8589934592 | tf_op jit(solution)/shard_map/spread_last/pallas_call | solution.py:24
  43.4 1.7 %collective-permute-start.15 = (f16[32,4096]{1,0:T(8,128)(2,1)S(1)}, f16[32,4096]{1,0:T(8,128)(2,1)S(1)}, u32[]{:S(2)}, u32[]{:S(2)}) collective-permute-start(f16[32,4096]{1,0:T(8,128)(2,1)S(1)} %convert_element_type.270), channel_id=1, source_target_pairs={{0,8},{8,16},{16,24},{24,0},{1,9},{9,17},{17,25},{25,1},{2,10},{10... | collective-permute-start | bytes 786440 | tf_op jit(solution)/shard_map/ppermute | solution.py:170
  49.8 4.4 %collective-permute-start.12 = (f16[32,1024]{1,0:T(8,128)(2,1)S(1)}, f16[32,1024]{1,0:T(8,128)(2,1)S(1)}, u32[]{:S(2)}, u32[]{:S(2)}) collective-permute-start(f16[32,1024]{1,0:T(8,128)(2,1)S(1)} %fusion.3), channel_id=1, source_target_pairs={{0,6},{1,7},{2,4},{3,5},{4,2},{5,3},{6,0},{7,1},{8,14},{9,15},{10,... | collective-permute-start | bytes 196616 | tf_op jit(solution)/shard_map/ppermute | solution.py:175
  58.1 2.5 %collective-permute-done.11 = f16[32,1024]{1,0:T(8,128)(2,1)S(1)} collective-permute-done((f16[32,1024]{1,0:T(8,128)(2,1)S(1)}, f16[32,1024]{1,0:T(8,128)(2,1)S(1)}, u32[]{:S(2)}, u32[]{:S(2)}) %collective-permute-start.11) | collective-permute-done | bytes 65568 | tf_op jit(solution)/shard_map/ppermute | solution.py:175
  62.5 1.7 %collective-permute-start.19 = (f16[32,1024]{1,0:T(8,128)(2,1)S(1)}, f16[32,1024]{1,0:T(8,128)(2,1)S(1)}, u32[]{:S(2)}, u32[]{:S(2)}) collective-permute-start(f16[32,1024]{1,0:T(8,128)(2,1)S(1)} %fusion.4), channel_id=1, source_target_pairs={{0,6},{1,7},{2,4},{3,5},{4,2},{5,3},{6,0},{7,1},{8,14},{9,15},{10,... | collective-permute-start | bytes 196616 | tf_op jit(solution)/shard_map/ppermute | solution.py:175
  64.3 2.6 %collective-permute-start.17 = (f16[32,1024]{1,0:T(8,128)(2,1)S(1)}, f16[32,1024]{1,0:T(8,128)(2,1)S(1)}, u32[]{:S(2)}, u32[]{:S(2)}) collective-permute-start(f16[32,1024]{1,0:T(8,128)(2,1)S(1)} %fusion.4), channel_id=1, source_target_pairs={{0,2},{1,3},{2,0},{3,1},{4,6},{5,7},{6,4},{7,5},{8,10},{9,11},{10,... | collective-permute-start | bytes 196616 | tf_op jit(solution)/shard_map/ppermute | solution.py:175
  66.9 1.7 %spread_last.10 = f32[32,4096]{1,0:T(8,128)S(1)} custom-call(s32[1]{0:T(128)} %bitcast.2.place, bf16[32,1024]{1,0:T(8,128)(2,1)S(1)} %collective-permute-done.13.residue, f32[32,4096]{1,0:T(8,128)S(1)} %spread_first.10.so_far, f32[32,4096]{1,0:T(8,128)S(1)} %get-tuple-element.121.volume, f32[1,4096]{1,0:T(1,128)S(1)} %get-tuple-element.38.column, ...), custom_call_target="tpu_custom_call" | custom-call | flops 8589934592 | tf_op jit(solution)/shard_map/spread_last/pallas_call | solution.py:24
  69.7 1.9 %collective-permute-done.18 = f16[32,1024]{1,0:T(8,128)(2,1)S(1)} collective-permute-done((f16[32,1024]{1,0:T(8,128)(2,1)S(1)}, f16[32,1024]{1,0:T(8,128)(2,1)S(1)}, u32[]{:S(2)}, u32[]{:S(2)}) %collective-permute-start.18) | collective-permute-done | bytes 65568 | tf_op jit(solution)/shard_map/ppermute | solution.py:175
  73.4 1.7 %spread_last.11 = f32[32,4096]{1,0:T(8,128)S(1)} custom-call(s32[1]{0:T(128)} %bitcast.2.place, bf16[32,1024]{1,0:T(8,128)(2,1)S(1)} %collective-permute-done.20.residue, f32[32,4096]{1,0:T(8,128)S(1)} %spread_first.11.so_far, f32[32,4096]{1,0:T(8,128)S(1)} %get-tuple-element.119.volume, f32[1,4096]{1,0:T(1,128)S(1)} %get-tuple-element.38.column, ...), custom_call_target="tpu_custom_call" | custom-call | flops 8589934592 | tf_op jit(solution)/shard_map/spread_last/pallas_call | solution.py:24
  80.8 1.7 %collective-permute-start.24 = (f16[32,1024]{1,0:T(8,128)(2,1)S(1)}, f16[32,1024]{1,0:T(8,128)(2,1)S(1)}, u32[]{:S(2)}, u32[]{:S(2)}) collective-permute-start(f16[32,1024]{1,0:T(8,128)(2,1)S(1)} %fusion.5), channel_id=1, source_target_pairs={{0,6},{1,7},{2,4},{3,5},{4,2},{5,3},{6,0},{7,1},{8,14},{9,15},{10,... | collective-permute-start | bytes 196616 | tf_op jit(solution)/shard_map/ppermute | solution.py:175
  82.6 2.6 %collective-permute-start.22 = (f16[32,1024]{1,0:T(8,128)(2,1)S(1)}, f16[32,1024]{1,0:T(8,128)(2,1)S(1)}, u32[]{:S(2)}, u32[]{:S(2)}) collective-permute-start(f16[32,1024]{1,0:T(8,128)(2,1)S(1)} %fusion.5), channel_id=1, source_target_pairs={{0,2},{1,3},{2,0},{3,1},{4,6},{5,7},{6,4},{7,5},{8,10},{9,11},{10,... | collective-permute-start | bytes 196616 | tf_op jit(solution)/shard_map/ppermute | solution.py:175
  91.7 1.7 %collective-permute-start.31 = (f16[32,1024]{1,0:T(8,128)(2,1)S(1)}, f16[32,1024]{1,0:T(8,128)(2,1)S(1)}, u32[]{:S(2)}, u32[]{:S(2)}) collective-permute-start(f16[32,1024]{1,0:T(8,128)(2,1)S(1)} %fusion.6), channel_id=1, source_target_pairs={{0,6},{1,7},{2,4},{3,5},{4,2},{5,3},{6,0},{7,1},{8,14},{9,15},{10,... | collective-permute-start | bytes 196616 | tf_op jit(solution)/shard_map/ppermute | solution.py:175
  93.4 2.7 %collective-permute-start.29 = (f16[32,1024]{1,0:T(8,128)(2,1)S(1)}, f16[32,1024]{1,0:T(8,128)(2,1)S(1)}, u32[]{:S(2)}, u32[]{:S(2)}) collective-permute-start(f16[32,1024]{1,0:T(8,128)(2,1)S(1)} %fusion.6), channel_id=1, source_target_pairs={{0,2},{1,3},{2,0},{3,1},{4,6},{5,7},{6,4},{7,5},{8,10},{9,11},{10,... | collective-permute-start | bytes 196616 | tf_op jit(solution)/shard_map/ppermute | solution.py:175
  96.2 1.7 %spread_last.12 = f32[32,4096]{1,0:T(8,128)S(1)} custom-call(s32[1]{0:T(128)} %bitcast.2.place, bf16[32,1024]{1,0:T(8,128)(2,1)S(1)} %collective-permute-done.25.residue, f32[32,4096]{1,0:T(8,128)S(1)} %spread_first.12.so_far, f32[32,4096]{1,0:T(8,128)S(1)} %get-tuple-element.117.volume, f32[1,4096]{1,0:T(1,128)S(1)} %get-tuple-element.38.column, ...), custom_call_target="tpu_custom_call" | custom-call | flops 8589934592 | tf_op jit(solution)/shard_map/spread_last/pallas_call | solution.py:24
  99.0 1.9 %collective-permute-done.30 = f16[32,1024]{1,0:T(8,128)(2,1)S(1)} collective-permute-done((f16[32,1024]{1,0:T(8,128)(2,1)S(1)}, f16[32,1024]{1,0:T(8,128)(2,1)S(1)}, u32[]{:S(2)}, u32[]{:S(2)}) %collective-permute-start.30) | collective-permute-done | bytes 65568 | tf_op jit(solution)/shard_map/ppermute | solution.py:175
  102.8 1.7 %spread_last.13 = f32[32,4096]{1,0:T(8,128)S(1)} custom-call(s32[1]{0:T(128)} %bitcast.2.place, bf16[32,1024]{1,0:T(8,128)(2,1)S(1)} %collective-permute-done.32.residue, f32[32,4096]{1,0:T(8,128)S(1)} %spread_first.13.so_far, f32[32,4096]{1,0:T(8,128)S(1)} %get-tuple-element.115.volume, f32[1,4096]{1,0:T(1,128)S(1)} %get-tuple-element.38.column, ...), custom_call_target="tpu_custom_call" | custom-call | flops 8589934592 | tf_op jit(solution)/shard_map/spread_last/pallas_call | solution.py:24
  110.1 1.7 %collective-permute-start.36 = (f16[32,1024]{1,0:T(8,128)(2,1)S(1)}, f16[32,1024]{1,0:T(8,128)(2,1)S(1)}, u32[]{:S(2)}, u32[]{:S(2)}) collective-permute-start(f16[32,1024]{1,0:T(8,128)(2,1)S(1)} %fusion.7), channel_id=1, source_target_pairs={{0,6},{1,7},{2,4},{3,5},{4,2},{5,3},{6,0},{7,1},{8,14},{9,15},{10,... | collective-permute-start | bytes 196616 | tf_op jit(solution)/shard_map/ppermute | solution.py:175
  111.9 2.6 %collective-permute-start.34 = (f16[32,1024]{1,0:T(8,128)(2,1)S(1)}, f16[32,1024]{1,0:T(8,128)(2,1)S(1)}, u32[]{:S(2)}, u32[]{:S(2)}) collective-permute-start(f16[32,1024]{1,0:T(8,128)(2,1)S(1)} %fusion.7), channel_id=1, source_target_pairs={{0,2},{1,3},{2,0},{3,1},{4,6},{5,7},{6,4},{7,5},{8,10},{9,11},{10,... | collective-permute-start | bytes 196616 | tf_op jit(solution)/shard_map/ppermute | solution.py:175
  121.2 1.7 %collective-permute-start.46 = (f16[32,1024]{1,0:T(8,128)(2,1)S(1)}, f16[32,1024]{1,0:T(8,128)(2,1)S(1)}, u32[]{:S(2)}, u32[]{:S(2)}) collective-permute-start(f16[32,1024]{1,0:T(8,128)(2,1)S(1)} %fusion.8), channel_id=1, source_target_pairs={{0,6},{1,7},{2,4},{3,5},{4,2},{5,3},{6,0},{7,1},{8,14},{9,15},{10,... | collective-permute-start | bytes 196616 | tf_op jit(solution)/shard_map/ppermute | solution.py:175
  122.9 2.7 %collective-permute-start.44 = (f16[32,1024]{1,0:T(8,128)(2,1)S(1)}, f16[32,1024]{1,0:T(8,128)(2,1)S(1)}, u32[]{:S(2)}, u32[]{:S(2)}) collective-permute-start(f16[32,1024]{1,0:T(8,128)(2,1)S(1)} %fusion.8), channel_id=1, source_target_pairs={{0,2},{1,3},{2,0},{3,1},{4,6},{5,7},{6,4},{7,5},{8,10},{9,11},{10,... | collective-permute-start | bytes 196616 | tf_op jit(solution)/shard_map/ppermute | solution.py:175
  125.6 1.7 %spread_last.14.before = f32[32,4096]{1,0:T(8,128)S(1)} custom-call(s32[1]{0:T(128)} %bitcast.2.place, bf16[32,1024]{1,0:T(8,128)(2,1)S(1)} %collective-permute-done.37.residue, f32[32,4096]{1,0:T(8,128)S(1)} %spread_first.14.so_far, f32[32,4096]{1,0:T(8,128)S(1)} %get-tuple-element.113.volume, f32[1,4096]{1,0:T(1,128)S(1)} %get-tuple-element.38.column, ...), custom_call_target="tpu_custom_call" | custom-call | flops 8589934592 | tf_op jit(solution)/shard_map/spread_last/pallas_call | solution.py:24
  132.2 1.7 %spread_last.15 = f32[32,4096]{1,0:T(8,128)S(1)} custom-call(s32[1]{0:T(128)} %bitcast.2.place, bf16[32,1024]{1,0:T(8,128)(2,1)S(1)} %collective-permute-done.47.residue, f32[32,4096]{1,0:T(8,128)S(1)} %spread_first.15.so_far, f32[32,4096]{1,0:T(8,128)S(1)} %get-tuple-element.111.volume, f32[1,4096]{1,0:T(1,128)S(1)} %get-tuple-element.38.column, ...), custom_call_target="tpu_custom_call" | custom-call | flops 8589934592 | tf_op jit(solution)/shard_map/spread_last/pallas_call | solution.py:24
  139.3 3.8 %collective-permute-done.50 = bf16[32,4096]{1,0:T(8,128)(2,1)S(1)} collective-permute-done((bf16[32,4096]{1,0:T(8,128)(2,1)S(1)}, bf16[32,4096]{1,0:T(8,128)(2,1)S(1)}, u32[]{:S(2)}, u32[]{:S(2)}) %collective-permute-start.50) | collective-permute-done | bytes 262176 | tf_op jit(solution)/shard_map/ppermute | solution.py:175
  147.4 2.4 %collective-permute-done.49 = bf16[32,2048]{1,0:T(8,128)(2,1)S(1)} collective-permute-done((bf16[32,2048]{1,0:T(8,128)(2,1)S(1)}, bf16[32,2048]{1,0:T(8,128)(2,1)S(1)}, u32[]{:S(2)}, u32[]{:S(2)}) %collective-permute-start.49) | collective-permute-done | bytes 131104 | tf_op jit(solution)/shard_map/ppermute | solution.py:175
  (206 shorter events, 69.9 us)
Async XLA Ops:
  11.6 9.1 %collective-permute-start.5 = (f16[32,1024]{1,0:T(8,128)(2,1)S(1)}, f16[32,1024]{1,0:T(8,128)(2,1)S(1)}, u32[]{:S(2)}, u32[]{:S(2)}) collective-permute-start(f16[32,1024]{1,0:T(8,128)(2,1)S(1)} %multiply_convert_fusion.13), channel_id=1, source_target_pairs={{0,1},{1,0},{2,3},{3,2},{4,5},{5,4},{6,7},{7,6},{8,9},{9,8},{10,11... | collective-permute-start | bytes 196616 | tf_op jit(solution)/shard_map/ppermute | solution.py:175
  20.7 7.6 %collective-permute-start.6 = (f16[32,1024]{1,0:T(8,128)(2,1)S(1)}, f16[32,1024]{1,0:T(8,128)(2,1)S(1)}, u32[]{:S(2)}, u32[]{:S(2)}) collective-permute-start(f16[32,1024]{1,0:T(8,128)(2,1)S(1)} %get-tuple-element.95), channel_id=1, source_target_pairs={{0,2},{1,3},{2,0},{3,1},{4,6},{5,7},{6,4},{7,5},{8,10},{9,11},{10,... | collective-permute-start | bytes 196616 | tf_op jit(solution)/shard_map/ppermute | solution.py:175
  37.0 9.3 %collective-permute-start.4 = (f16[32,4096]{1,0:T(8,128)(2,1)S(1)}, f16[32,4096]{1,0:T(8,128)(2,1)S(1)}, u32[]{:S(2)}, u32[]{:S(2)}) collective-permute-start(f16[32,4096]{1,0:T(8,128)(2,1)S(1)} %convert_element_type.261), channel_id=1, source_target_pairs={{0,8},{8,16},{16,24},{24,0},{1,9},{9,17},{17,25},{25,1},{2,10},{10... | collective-permute-start | bytes 786440 | tf_op jit(solution)/shard_map/ppermute | solution.py:170
  43.4 11.4 %collective-permute-start.15 = (f16[32,4096]{1,0:T(8,128)(2,1)S(1)}, f16[32,4096]{1,0:T(8,128)(2,1)S(1)}, u32[]{:S(2)}, u32[]{:S(2)}) collective-permute-start(f16[32,4096]{1,0:T(8,128)(2,1)S(1)} %convert_element_type.270), channel_id=1, source_target_pairs={{0,8},{8,16},{16,24},{24,0},{1,9},{9,17},{17,25},{25,1},{2,10},{10... | collective-permute-start | bytes 786440 | tf_op jit(solution)/shard_map/ppermute | solution.py:170
  49.8 8.3 %collective-permute-start.12 = (f16[32,1024]{1,0:T(8,128)(2,1)S(1)}, f16[32,1024]{1,0:T(8,128)(2,1)S(1)}, u32[]{:S(2)}, u32[]{:S(2)}) collective-permute-start(f16[32,1024]{1,0:T(8,128)(2,1)S(1)} %fusion.3), channel_id=1, source_target_pairs={{0,6},{1,7},{2,4},{3,5},{4,2},{5,3},{6,0},{7,1},{8,14},{9,15},{10,... | collective-permute-start | bytes 196616 | tf_op jit(solution)/shard_map/ppermute | solution.py:175
  54.2 6.5 %collective-permute-start.11 = (f16[32,1024]{1,0:T(8,128)(2,1)S(1)}, f16[32,1024]{1,0:T(8,128)(2,1)S(1)}, u32[]{:S(2)}, u32[]{:S(2)}) collective-permute-start(f16[32,1024]{1,0:T(8,128)(2,1)S(1)} %fusion.3), channel_id=1, source_target_pairs={{0,4},{1,5},{2,6},{3,7},{4,0},{5,1},{6,2},{7,3},{8,12},{9,13},{10,... | collective-permute-start | bytes 196616 | tf_op jit(solution)/shard_map/ppermute | solution.py:175
  62.5 7.2 %collective-permute-start.19 = (f16[32,1024]{1,0:T(8,128)(2,1)S(1)}, f16[32,1024]{1,0:T(8,128)(2,1)S(1)}, u32[]{:S(2)}, u32[]{:S(2)}) collective-permute-start(f16[32,1024]{1,0:T(8,128)(2,1)S(1)} %fusion.4), channel_id=1, source_target_pairs={{0,6},{1,7},{2,4},{3,5},{4,2},{5,3},{6,0},{7,1},{8,14},{9,15},{10,... | collective-permute-start | bytes 196616 | tf_op jit(solution)/shard_map/ppermute | solution.py:175
  64.2 7.4 %collective-permute-start.18 = (f16[32,1024]{1,0:T(8,128)(2,1)S(1)}, f16[32,1024]{1,0:T(8,128)(2,1)S(1)}, u32[]{:S(2)}, u32[]{:S(2)}) collective-permute-start(f16[32,1024]{1,0:T(8,128)(2,1)S(1)} %fusion.4), channel_id=1, source_target_pairs={{0,4},{1,5},{2,6},{3,7},{4,0},{5,1},{6,2},{7,3},{8,12},{9,13},{10,... | collective-permute-start | bytes 196616 | tf_op jit(solution)/shard_map/ppermute | solution.py:175
  64.3 7.3 %collective-permute-start.17 = (f16[32,1024]{1,0:T(8,128)(2,1)S(1)}, f16[32,1024]{1,0:T(8,128)(2,1)S(1)}, u32[]{:S(2)}, u32[]{:S(2)}) collective-permute-start(f16[32,1024]{1,0:T(8,128)(2,1)S(1)} %fusion.4), channel_id=1, source_target_pairs={{0,2},{1,3},{2,0},{3,1},{4,6},{5,7},{6,4},{7,5},{8,10},{9,11},{10,... | collective-permute-start | bytes 196616 | tf_op jit(solution)/shard_map/ppermute | solution.py:175
  68.7 8.8 %collective-permute-start.14 = (f16[32,4096]{1,0:T(8,128)(2,1)S(1)}, f16[32,4096]{1,0:T(8,128)(2,1)S(1)}, u32[]{:S(2)}, u32[]{:S(2)}) collective-permute-start(f16[32,4096]{1,0:T(8,128)(2,1)S(1)} %convert_element_type.280), channel_id=1, source_target_pairs={{0,8},{8,16},{16,24},{24,0},{1,9},{9,17},{17,25},{25,1},{2,10},{10... | collective-permute-start | bytes 786440 | tf_op jit(solution)/shard_map/ppermute | solution.py:170
  75.2 10.1 %collective-permute-start.27 = (f16[32,4096]{1,0:T(8,128)(2,1)S(1)}, f16[32,4096]{1,0:T(8,128)(2,1)S(1)}, u32[]{:S(2)}, u32[]{:S(2)}) collective-permute-start(f16[32,4096]{1,0:T(8,128)(2,1)S(1)} %convert_element_type.290), channel_id=1, source_target_pairs={{0,8},{8,16},{16,24},{24,0},{1,9},{9,17},{17,25},{25,1},{2,10},{10... | collective-permute-start | bytes 786440 | tf_op jit(solution)/shard_map/ppermute | solution.py:170
  80.8 7.8 %collective-permute-start.24 = (f16[32,1024]{1,0:T(8,128)(2,1)S(1)}, f16[32,1024]{1,0:T(8,128)(2,1)S(1)}, u32[]{:S(2)}, u32[]{:S(2)}) collective-permute-start(f16[32,1024]{1,0:T(8,128)(2,1)S(1)} %fusion.5), channel_id=1, source_target_pairs={{0,6},{1,7},{2,4},{3,5},{4,2},{5,3},{6,0},{7,1},{8,14},{9,15},{10,... | collective-permute-start | bytes 196616 | tf_op jit(solution)/shard_map/ppermute | solution.py:175
  82.5 7.5 %collective-permute-start.23 = (f16[32,1024]{1,0:T(8,128)(2,1)S(1)}, f16[32,1024]{1,0:T(8,128)(2,1)S(1)}, u32[]{:S(2)}, u32[]{:S(2)}) collective-permute-start(f16[32,1024]{1,0:T(8,128)(2,1)S(1)} %fusion.5), channel_id=1, source_target_pairs={{0,4},{1,5},{2,6},{3,7},{4,0},{5,1},{6,2},{7,3},{8,12},{9,13},{10,... | collective-permute-start | bytes 196616 | tf_op jit(solution)/shard_map/ppermute | solution.py:175
  82.6 7.3 %collective-permute-start.22 = (f16[32,1024]{1,0:T(8,128)(2,1)S(1)}, f16[32,1024]{1,0:T(8,128)(2,1)S(1)}, u32[]{:S(2)}, u32[]{:S(2)}) collective-permute-start(f16[32,1024]{1,0:T(8,128)(2,1)S(1)} %fusion.5), channel_id=1, source_target_pairs={{0,2},{1,3},{2,0},{3,1},{4,6},{5,7},{6,4},{7,5},{8,10},{9,11},{10,... | collective-permute-start | bytes 196616 | tf_op jit(solution)/shard_map/ppermute | solution.py:175
  91.7 7.2 %collective-permute-start.31 = (f16[32,1024]{1,0:T(8,128)(2,1)S(1)}, f16[32,1024]{1,0:T(8,128)(2,1)S(1)}, u32[]{:S(2)}, u32[]{:S(2)}) collective-permute-start(f16[32,1024]{1,0:T(8,128)(2,1)S(1)} %fusion.6), channel_id=1, source_target_pairs={{0,6},{1,7},{2,4},{3,5},{4,2},{5,3},{6,0},{7,1},{8,14},{9,15},{10,... | collective-permute-start | bytes 196616 | tf_op jit(solution)/shard_map/ppermute | solution.py:175
  93.4 7.4 %collective-permute-start.30 = (f16[32,1024]{1,0:T(8,128)(2,1)S(1)}, f16[32,1024]{1,0:T(8,128)(2,1)S(1)}, u32[]{:S(2)}, u32[]{:S(2)}) collective-permute-start(f16[32,1024]{1,0:T(8,128)(2,1)S(1)} %fusion.6), channel_id=1, source_target_pairs={{0,4},{1,5},{2,6},{3,7},{4,0},{5,1},{6,2},{7,3},{8,12},{9,13},{10,... | collective-permute-start | bytes 196616 | tf_op jit(solution)/shard_map/ppermute | solution.py:175
  93.4 7.4 %collective-permute-start.29 = (f16[32,1024]{1,0:T(8,128)(2,1)S(1)}, f16[32,1024]{1,0:T(8,128)(2,1)S(1)}, u32[]{:S(2)}, u32[]{:S(2)}) collective-permute-start(f16[32,1024]{1,0:T(8,128)(2,1)S(1)} %fusion.6), channel_id=1, source_target_pairs={{0,2},{1,3},{2,0},{3,1},{4,6},{5,7},{6,4},{7,5},{8,10},{9,11},{10,... | collective-permute-start | bytes 196616 | tf_op jit(solution)/shard_map/ppermute | solution.py:175
  98.0 8.8 %collective-permute-start.26 = (f16[32,4096]{1,0:T(8,128)(2,1)S(1)}, f16[32,4096]{1,0:T(8,128)(2,1)S(1)}, u32[]{:S(2)}, u32[]{:S(2)}) collective-permute-start(f16[32,4096]{1,0:T(8,128)(2,1)S(1)} %convert_element_type.300), channel_id=1, source_target_pairs={{0,8},{8,16},{16,24},{24,0},{1,9},{9,17},{17,25},{25,1},{2,10},{10... | collective-permute-start | bytes 786440 | tf_op jit(solution)/shard_map/ppermute | solution.py:170
  104.5 10.0 %collective-permute-start.42 = (f16[32,4096]{1,0:T(8,128)(2,1)S(1)}, f16[32,4096]{1,0:T(8,128)(2,1)S(1)}, u32[]{:S(2)}, u32[]{:S(2)}) collective-permute-start(f16[32,4096]{1,0:T(8,128)(2,1)S(1)} %convert_element_type.310), channel_id=1, source_target_pairs={{0,8},{8,16},{16,24},{24,0},{1,9},{9,17},{17,25},{25,1},{2,10},{10... | collective-permute-start | bytes 786440 | tf_op jit(solution)/shard_map/ppermute | solution.py:170
  110.1 7.8 %collective-permute-start.36 = (f16[32,1024]{1,0:T(8,128)(2,1)S(1)}, f16[32,1024]{1,0:T(8,128)(2,1)S(1)}, u32[]{:S(2)}, u32[]{:S(2)}) collective-permute-start(f16[32,1024]{1,0:T(8,128)(2,1)S(1)} %fusion.7), channel_id=1, source_target_pairs={{0,6},{1,7},{2,4},{3,5},{4,2},{5,3},{6,0},{7,1},{8,14},{9,15},{10,... | collective-permute-start | bytes 196616 | tf_op jit(solution)/shard_map/ppermute | solution.py:175
  111.8 7.5 %collective-permute-start.35 = (f16[32,1024]{1,0:T(8,128)(2,1)S(1)}, f16[32,1024]{1,0:T(8,128)(2,1)S(1)}, u32[]{:S(2)}, u32[]{:S(2)}) collective-permute-start(f16[32,1024]{1,0:T(8,128)(2,1)S(1)} %fusion.7), channel_id=1, source_target_pairs={{0,4},{1,5},{2,6},{3,7},{4,0},{5,1},{6,2},{7,3},{8,12},{9,13},{10,... | collective-permute-start | bytes 196616 | tf_op jit(solution)/shard_map/ppermute | solution.py:175
  111.9 7.3 %collective-permute-start.34 = (f16[32,1024]{1,0:T(8,128)(2,1)S(1)}, f16[32,1024]{1,0:T(8,128)(2,1)S(1)}, u32[]{:S(2)}, u32[]{:S(2)}) collective-permute-start(f16[32,1024]{1,0:T(8,128)(2,1)S(1)} %fusion.7), channel_id=1, source_target_pairs={{0,2},{1,3},{2,0},{3,1},{4,6},{5,7},{6,4},{7,5},{8,10},{9,11},{10,... | collective-permute-start | bytes 196616 | tf_op jit(solution)/shard_map/ppermute | solution.py:175
  121.2 7.9 %collective-permute-start.46 = (f16[32,1024]{1,0:T(8,128)(2,1)S(1)}, f16[32,1024]{1,0:T(8,128)(2,1)S(1)}, u32[]{:S(2)}, u32[]{:S(2)}) collective-permute-start(f16[32,1024]{1,0:T(8,128)(2,1)S(1)} %fusion.8), channel_id=1, source_target_pairs={{0,6},{1,7},{2,4},{3,5},{4,2},{5,3},{6,0},{7,1},{8,14},{9,15},{10,... | collective-permute-start | bytes 196616 | tf_op jit(solution)/shard_map/ppermute | solution.py:175
  122.9 7.4 %collective-permute-start.45 = (f16[32,1024]{1,0:T(8,128)(2,1)S(1)}, f16[32,1024]{1,0:T(8,128)(2,1)S(1)}, u32[]{:S(2)}, u32[]{:S(2)}) collective-permute-start(f16[32,1024]{1,0:T(8,128)(2,1)S(1)} %fusion.8), channel_id=1, source_target_pairs={{0,4},{1,5},{2,6},{3,7},{4,0},{5,1},{6,2},{7,3},{8,12},{9,13},{10,... | collective-permute-start | bytes 196616 | tf_op jit(solution)/shard_map/ppermute | solution.py:175
  122.9 7.4 %collective-permute-start.44 = (f16[32,1024]{1,0:T(8,128)(2,1)S(1)}, f16[32,1024]{1,0:T(8,128)(2,1)S(1)}, u32[]{:S(2)}, u32[]{:S(2)}) collective-permute-start(f16[32,1024]{1,0:T(8,128)(2,1)S(1)} %fusion.8), channel_id=1, source_target_pairs={{0,2},{1,3},{2,0},{3,1},{4,6},{5,7},{6,4},{7,5},{8,10},{9,11},{10,... | collective-permute-start | bytes 196616 | tf_op jit(solution)/shard_map/ppermute | solution.py:175
  127.4 10.8 %collective-permute-start.40 = (bf16[32,4096]{1,0:T(8,128)(2,1)S(1)}, bf16[32,4096]{1,0:T(8,128)(2,1)S(1)}, u32[]{:S(2)}, u32[]{:S(2)}) collective-permute-start(bf16[32,4096]{1,0:T(8,128)(2,1)S(1)} %convert_element_type.320), channel_id=1, source_target_pairs={{0,8},{8,0},{16,24},{24,16},{1,9},{9,1},{17,25},{25,17},{2,10},{10... | collective-permute-start | bytes 786440 | tf_op jit(solution)/shard_map/ppermute | solution.py:175
  128.5 7.6 %collective-permute-start.38 = (bf16[32,4096]{1,0:T(8,128)(2,1)S(1)}, bf16[32,4096]{1,0:T(8,128)(2,1)S(1)}, u32[]{:S(2)}, u32[]{:S(2)}) collective-permute-start(bf16[32,4096]{1,0:T(8,128)(2,1)S(1)} %convert_element_type.320), channel_id=1, source_target_pairs={{0,16},{8,24},{16,0},{24,8},{1,17},{9,25},{17,1},{25,9},{2,18},{10... | collective-permute-start | bytes 786440 | tf_op jit(solution)/shard_map/ppermute | solution.py:175
  133.9 9.2 %collective-permute-start.50 = (bf16[32,4096]{1,0:T(8,128)(2,1)S(1)}, bf16[32,4096]{1,0:T(8,128)(2,1)S(1)}, u32[]{:S(2)}, u32[]{:S(2)}) collective-permute-start(bf16[32,4096]{1,0:T(8,128)(2,1)S(1)} %convert_element_type.329), channel_id=1, source_target_pairs={{0,8},{8,0},{16,24},{24,16},{1,9},{9,1},{17,25},{25,17},{2,10},{10... | collective-permute-start | bytes 786440 | tf_op jit(solution)/shard_map/ppermute | solution.py:175
  135.0 9.7 %collective-permute-start.48 = (bf16[32,4096]{1,0:T(8,128)(2,1)S(1)}, bf16[32,4096]{1,0:T(8,128)(2,1)S(1)}, u32[]{:S(2)}, u32[]{:S(2)}) collective-permute-start(bf16[32,4096]{1,0:T(8,128)(2,1)S(1)} %convert_element_type.329), channel_id=1, source_target_pairs={{0,16},{8,24},{16,0},{24,8},{1,17},{9,25},{17,1},{25,9},{2,18},{10... | collective-permute-start | bytes 786440 | tf_op jit(solution)/shard_map/ppermute | solution.py:175
  136.1 9.4 %collective-permute-start.39 = (bf16[32,2048]{1,0:T(8,128)(2,1)S(1)}, bf16[32,2048]{1,0:T(8,128)(2,1)S(1)}, u32[]{:S(2)}, u32[]{:S(2)}) collective-permute-start(bf16[32,2048]{1,0:T(8,128)(2,1)S(1)} %slice.236), channel_id=1, source_target_pairs={{0,8},{8,0},{16,24},{24,16},{1,9},{9,1},{17,25},{25,17},{2,10},{10... | collective-permute-start | bytes 393224 | tf_op jit(solution)/shard_map/ppermute | solution.py:175
  138.2 8.8 %collective-permute-start.41 = (bf16[32,2048]{1,0:T(8,128)(2,1)S(1)}, bf16[32,2048]{1,0:T(8,128)(2,1)S(1)}, u32[]{:S(2)}, u32[]{:S(2)}) collective-permute-start(bf16[32,2048]{1,0:T(8,128)(2,1)S(1)} %slice.237), channel_id=1, source_target_pairs={{0,16},{8,24},{16,0},{24,8},{1,17},{9,25},{17,1},{25,9},{2,18},{10... | collective-permute-start | bytes 393224 | tf_op jit(solution)/shard_map/ppermute | solution.py:175
  143.1 6.7 %collective-permute-start.51 = (bf16[32,2048]{1,0:T(8,128)(2,1)S(1)}, bf16[32,2048]{1,0:T(8,128)(2,1)S(1)}, u32[]{:S(2)}, u32[]{:S(2)}) collective-permute-start(bf16[32,2048]{1,0:T(8,128)(2,1)S(1)} %slice.239), channel_id=1, source_target_pairs={{0,16},{8,24},{16,0},{24,8},{1,17},{9,25},{17,1},{25,9},{2,18},{10... | collective-permute-start | bytes 393224 | tf_op jit(solution)/shard_map/ppermute | solution.py:175
  (35 other events, 143.3 us)
